TPU v7x, 128 devices: a whole 4x4x4 slice. The times are simulated.
128 devices in a mesh: dp: 32 (over x_hi, y, z), tensor: 4 (over x_lo, core).
Axes of the slice: x: 4 (x_hi: 2, x_lo: 2; x = x_hi * 2 + x_lo), y: 4, z: 4, core: 2. Of those that a mesh axis runs over, the one named last changes fastest.
Arguments:
- hidden_in: bfloat16 [32768, 1536], P(('dp', 'tensor')), may hold values from -6 to 6
- cotangent: bfloat16 [32768, 1536], P(('dp', 'tensor')), may hold values from -6 to 6
- norm_gain: float32 [1536], replicated, may hold values from 0.1 to 1.9
- w_z: bfloat16 [1536, 3072], P('dp', 'tensor'), may hold values from -0.15625 to 0.15625
- w_x: bfloat16 [1536, 3072], P('dp', 'tensor'), may hold values from -0.15625 to 0.15625
- w_bc: bfloat16 [1536, 256], P('dp'), may hold values from -0.15625 to 0.15625
- w_dt: bfloat16 [1536, 48], P('dp', 'tensor'), may hold values from -0.15625 to 0.15625
- conv_x: float32 [5, 3072], P(None, 'tensor'), may hold values from -3 to 3
- conv_bc: float32 [5, 256], replicated, may hold values from -3 to 3
- head_params: float32 [3, 48], P(None, 'tensor'), may hold values from -7 to 3, as said below
- gate_gain: float32 [3072], P('tensor'), may hold values from 0.1 to 1.9
- w_out: bfloat16 [3072, 1536], P('tensor', 'dp'), may hold values from -0.109375 to 0.109375
Outputs:
- output: bfloat16 [32768, 1536], P(('dp', 'tensor'))
- input_grad: float32 [32768, 1536], P(('dp', 'tensor'))
- grad_norm_gain: float32 [1536], replicated
- grad_w_z: float32 [1536, 3072], P('dp', 'tensor')
- grad_w_x: float32 [1536, 3072], P('dp', 'tensor')
- grad_w_bc: float32 [1536, 256], P('dp')
- grad_w_dt: float32 [1536, 48], P('dp', 'tensor')
- grad_conv_x: float32 [5, 3072], P(None, 'tensor')
- grad_conv_bc: float32 [5, 256], replicated
- grad_head: float32 [3, 48], P(None, 'tensor')
- grad_gate_gain: float32 [3072], P('tensor')
- grad_w_out: float32 [3072, 1536], P('tensor', 'dp')
Inputs may be any that keep to these rules, and one draw needn't show every extreme that they name: `head_params`: row 0 holds logarithms of the heads' decay rates, row 1 the step-size biases, row 2 the skip weights.
All inputs are finite; a program needn't handle non-finite values.
Results may differ from a plain program's by a relative error of at most 0.0081.
Values may be sent and summed in bfloat16 or wider, within the bound.
No kernel may reach another device: no remote copies, remote signals or barrier semaphores. Data moves between devices by JAX's collectives and lax.ppermute only.
A program may use at most 128 MiB of HBM per device.

v0:
```python
import functools
import jax
import jax.numpy as jnp
from jax import lax
from jax.experimental import pallas as pl
from jax.experimental.pallas import tpu as pltpu
from jax.sharding import Mesh, PartitionSpec as P

EPS = 1e-05
AXES = ("xh", "y", "z", "xl", "core")
DP = ("xh", "y", "z")
TN = ("xl", "core")
GROUP = ("xh", "xl", "core")
PLANE = ("y", "z")
BF = jnp.bfloat16
F32 = jnp.float32
HI = lax.Precision.HIGHEST
SPAN = 128
SCALE = 1.15e9


def nn(left, right):
    return lax.dot_general(left, right, (((1,), (0,)), ((), ())), preferred_element_type=F32)


def nt(left, right):
    return lax.dot_general(left, right, (((1,), (1,)), ((), ())), preferred_element_type=F32)


def exact(left, right):
    return lax.dot_general(
        left, right, (((1,), (0,)), ((), ())), precision=HI, preferred_element_type=F32
    )


def exact_nt(left, right):
    return lax.dot_general(
        left, right, (((1,), (1,)), ((), ())), precision=HI, preferred_element_type=F32
    )


def halves(value):
    high = value.astype(BF)
    low = (value - high.astype(F32)).astype(BF)
    return high, low


def expand(value, spread):
    high, low = halves(value)
    return nn(jnp.concatenate([high, low], axis=1), spread)


def by_head(value, spread):
    width = spread.shape[0] // 2
    high, low = halves(value)
    return nt(high, spread[:width]) + nt(low, spread[:width])


def logistic(value):
    return 1.0 / (1.0 + jnp.exp(-value))


def sigmoid(value):
    return 0.5 * jnp.tanh(0.5 * value) + 0.5


def softplus(value):
    return jnp.maximum(value, 0.0) + jnp.log1p(jnp.exp(-jnp.abs(value)))


def conv_rows(ext_ref, taps):
    total = taps[4:5] + ext_ref[5 : 5 + SPAN] * taps[0:1]
    for k in range(1, 4):
        total = total + ext_ref[5 + k : 5 + k + SPAN] * taps[k : k + 1]
    return total


def scan_parts(conv, pre_dt, head, spread, tri):
    sig = sigmoid(conv)
    xbc = conv * sig
    raw = pre_dt + head[1:2]
    step = softplus(raw)
    decay = exact(tri, step * head[0:1])
    last = decay[SPAN - 1 : SPAN]
    grown = expand(jnp.concatenate([step, jnp.exp(decay), jnp.exp(last - decay)], axis=0), spread)
    step_x, start_x, end_x = grown[:SPAN], grown[SPAN : 2 * SPAN], grown[2 * SPAN :]
    return sig, xbc, raw, step, decay, step_x, start_x, end_x


def forward_kernel(
    pre_ref, taps_ref, head_ref, skip_ref, spread_ref, y_ref, kept_ref, conv_ref, ext_ref, state_ref
):
    inner = y_ref.shape[1]
    both = ext_ref.shape[1]

    @pl.when(pl.program_id(0) == 0)
    def _():
        ext_ref[0:8] = jnp.zeros((8, both), F32)
        state_ref[...] = jnp.zeros_like(state_ref)

    ext_ref[8 : 8 + SPAN] = pre_ref[:, :both]
    rows = lax.broadcasted_iota(jnp.int32, (SPAN, SPAN), 0)
    cols = lax.broadcasted_iota(jnp.int32, (SPAN, SPAN), 1)
    keep = rows >= cols
    tri = jnp.where(keep, 1.0, 0.0).astype(F32)
    spread = spread_ref[...]
    conv = conv_rows(ext_ref, taps_ref[...])
    conv_ref[...] = conv
    sig, xbc, raw, step, decay, step_x, start_x, end_x = scan_parts(
        conv, pre_ref[:, both:], head_ref[...], spread, tri
    )
    ext_ref[0:8] = ext_ref[SPAN : SPAN + 8]
    state_width = (both - inner) // 2
    x = xbc[:, :inner]
    b = xbc[:, inner : inner + state_width]
    c = xbc[:, inner + state_width :]
    decay_t = decay.T
    scaled = x * step_x
    low = scaled.astype(BF)
    scores = exact_nt(c, b)
    state = state_ref[...]
    state_low = state.astype(BF)
    kept_ref[...] = state_low
    carried = nn(c.astype(BF), state_low) * start_x + x * skip_ref[...]
    left = cols < 64
    for pair in range(inner // 128):
        at = slice(128 * pair, 128 * pair + 128)
        x_pair = low[:, at]
        found = []
        for h in (2 * pair, 2 * pair + 1):
            gap = decay[:, h : h + 1] - decay_t[h : h + 1]
            weight = jnp.exp(jnp.where(keep, gap, -1e30)) * scores
            found.append(nn(weight.astype(BF), x_pair))
        y_ref[:, at] = jnp.where(left, found[0], found[1]) + carried[:, at]
    state_ref[...] = state * start_x[SPAN - 1 : SPAN] + nn(
        b.T.astype(BF), (scaled * end_x).astype(BF)
    )


def backward_kernel(
    pre_ref, conv_ref, dy_ref, kept_ref, taps_ref, head_ref, skip_ref, spread_ref,
    late_ref, conv_grad_ref, head_grad_ref,
    dext_ref, dstate_ref, skip_sum_ref,
):
    inner = dy_ref.shape[1]
    both = dext_ref.shape[1]
    steps = pl.num_programs(0)
    at_step = pl.program_id(0)

    @pl.when(at_step == 0)
    def _():
        dext_ref[SPAN : SPAN + 8] = jnp.zeros((8, both), F32)
        dstate_ref[...] = jnp.zeros_like(dstate_ref)
        skip_sum_ref[...] = jnp.zeros_like(skip_sum_ref)
        conv_grad_ref[...] = jnp.zeros_like(conv_grad_ref)
        head_grad_ref[...] = jnp.zeros_like(head_grad_ref)

    rows = lax.broadcasted_iota(jnp.int32, (SPAN, SPAN), 0)
    cols = lax.broadcasted_iota(jnp.int32, (SPAN, SPAN), 1)
    tri = jnp.where(rows >= cols, 1.0, 0.0).astype(F32)
    upper = jnp.where(cols >= rows, 1.0, 0.0).astype(F32)
    keep = cols >= rows
    spread = spread_ref[...]
    taps = taps_ref[...]
    head = head_ref[...]
    conv = conv_ref[...]
    sig, xbc, raw, step, decay, step_x, start_x, end_x = scan_parts(
        conv, pre_ref[:, both:], head, spread, tri
    )
    state_width = (both - inner) // 2
    x = xbc[:, :inner]
    b = xbc[:, inner : inner + state_width]
    c = xbc[:, inner + state_width :]
    b_low, c_low = b.astype(BF), c.astype(BF)
    decay_t = decay.T
    scaled = x * step_x
    low = scaled.astype(BF)
    scores = exact_nt(b, c)
    dy = dy_ref[...].astype(F32)
    dy_low = dy.astype(BF)
    kept = kept_ref[...]
    dstate = dstate_ref[...]
    dstate_low = dstate.astype(BF)
    left = cols < 64
    wide_rows = lax.broadcasted_iota(jnp.int32, (SPAN, SPAN), 0)
    d_scores = jnp.zeros((SPAN, SPAN), F32)
    into = jnp.zeros((SPAN, SPAN), F32)
    out_of = jnp.zeros((SPAN, SPAN), F32)
    pieces = []
    none = jnp.zeros((SPAN, 128), BF)
    for pair in range(inner // 128):
        at = slice(128 * pair, 128 * pair + 128)
        x_pair = low[:, at]
        dy_pair = dy_low[:, at]
        found = []
        for side, h in enumerate((2 * pair, 2 * pair + 1)):
            gap = decay_t[h : h + 1] - decay[:, h : h + 1]
            fall = jnp.exp(jnp.where(keep, gap, -1e30))
            mine = jnp.where(left if side == 0 else ~left, dy_pair, none)
            back = nt(x_pair, mine) * fall
            d_scores = d_scores + back
            both_ways = back * scores
            into = jnp.where(wide_rows == h, jnp.sum(both_ways, axis=0, keepdims=True), into)
            out_of = jnp.where(cols == h, jnp.sum(both_ways, axis=1, keepdims=True), out_of)
            found.append(nn((fall * scores).astype(BF), dy_pair))
        pieces.append(jnp.where(left, found[0], found[1]))
    inside = jnp.concatenate(pieces, axis=1)
    dy_start = dy * start_x
    dy_start_low = dy_start.astype(BF)
    from_state = nn(c_low, kept)
    scaled_end = scaled * end_x
    d_end = nn(b_low, dstate_low)
    d_scaled = inside + d_end * end_x
    pair_start = by_head(dy_start * from_state, spread)
    pair_end = by_head(scaled_end * d_end, spread)
    d_scores_low = d_scores.astype(BF)
    d_c = nn(d_scores.T.astype(BF), b_low) + nt(dy_start_low, kept)
    d_b = nn(d_scores_low, c_low) + nt(scaled_end.astype(BF), dstate_low)
    through = jnp.sum(kept.astype(F32) * dstate, axis=0, keepdims=True)
    through = by_head(jnp.broadcast_to(through * start_x[SPAN - 1 : SPAN], (8, inner)), spread)[0:1]
    at_end = jnp.sum(pair_end, axis=0, keepdims=True) + through
    d_decay = into.T - out_of + pair_start - pair_end
    d_decay = d_decay + jnp.where(rows == SPAN - 1, at_end, 0.0)
    d_log = exact(upper, d_decay)
    d_step = by_head(d_scaled * x, spread) + d_log * head[0:1]
    d_raw = d_step * logistic(raw)
    dstate_ref[...] = dstate * start_x[SPAN - 1 : SPAN] + nn(c.T.astype(BF), dy_start_low)
    late_ref[:, both:] = d_raw.astype(BF)
    head_grad_ref[0:1] += jnp.sum(d_log * step, axis=0, keepdims=True) * head[0:1]
    head_grad_ref[1:2] += jnp.sum(d_raw, axis=0, keepdims=True)
    skip_sum_ref[0:1] += jnp.sum(dy * x, axis=0, keepdims=True)
    dx = d_scaled * step_x + dy * skip_ref[...]
    d_conv = jnp.concatenate([dx, d_b, d_c], axis=1) * (sig * (1.0 + conv * (1.0 - sig)))
    dext_ref[0:SPAN] = d_conv
    values = pre_ref[:, :both]
    d_pre = d_conv * taps[3:4]
    conv_grad_ref[3:4] += jnp.sum(d_conv * values, axis=0, keepdims=True)
    for k in range(3):
        moved = dext_ref[3 - k : 3 - k + SPAN]
        d_pre = d_pre + moved * taps[k : k + 1]
        conv_grad_ref[k : k + 1] += jnp.sum(moved * values, axis=0, keepdims=True)
    conv_grad_ref[4:5] += jnp.sum(d_conv, axis=0, keepdims=True)
    dext_ref[SPAN : SPAN + 8] = dext_ref[0:8]
    late_ref[:, :both] = d_pre.astype(BF)

    @pl.when(at_step == steps - 1)
    def _():
        head_grad_ref[2:3] += by_head(
            jnp.broadcast_to(skip_sum_ref[0:1], (8, inner)), spread
        )[0:1]


def whole(shape):
    return pl.BlockSpec(shape, lambda *_: (0,) * len(shape))


def column(rows, width, shift=0):
    return pl.BlockSpec((rows, width), lambda j, *_: (0, j + shift))


def shape_of(shape, dtype):
    return jax.ShapeDtypeStruct(shape, dtype)


def params(limit, *semantics):
    return pltpu.CompilerParams(
        dimension_semantics=semantics or None, vmem_limit_bytes=52 * 1024 * 1024
    )


def lasting(us):
    return pl.CostEstimate(flops=int(us * SCALE), bytes_accessed=1024, transcendentals=0)


def place_kernel(normalise, meta_ref, gain_ref, *refs):
    blocks, out_ref, flip_ref = refs[:4], refs[4], refs[5]
    rows, width = blocks[0].shape
    half = width // 2
    core = meta_ref[4]
    first = pl.multiple_of(core * half, 128)
    second = pl.multiple_of((1 - core) * half, 128)
    for k, block in enumerate(blocks):
        at = pl.multiple_of(meta_ref[k] * rows, rows)
        value = block[...].astype(F32)
        if normalise:
            scale = lax.rsqrt(jnp.mean(value * value, axis=1, keepdims=True) + EPS)
            value = value * scale * gain_ref[...]
        low = value.astype(BF)
        out_ref[pl.ds(at, rows), pl.ds(first, half)] = low[:, :half]
        out_ref[pl.ds(at, rows), pl.ds(second, half)] = low[:, half:]
        flip = value.T.astype(BF)
        flip_ref[pl.ds(first, half), pl.ds(at, rows)] = flip[:half]
        flip_ref[pl.ds(second, half), pl.ds(at, rows)] = flip[half:]


def place(meta, gain, blocks, normalise):
    rows, width = blocks[0].shape
    vmem = pl.BlockSpec()
    return pl.pallas_call(
        functools.partial(place_kernel, normalise),
        in_specs=[pl.BlockSpec(memory_space=pltpu.SMEM)] + [vmem] * 5,
        out_specs=[vmem, vmem],
        out_shape=[shape_of((4 * rows, width), BF), shape_of((width, 4 * rows), BF)],
        compiler_params=params(24),
        cost_estimate=lasting(6),
        name="place_normed" if normalise else "place_cotangent",
    )(meta, gain, *blocks)


def project_kernel(tokens_ref, mine_ref, other_ref, out_ref):
    half = mine_ref.shape[0]
    out_ref[...] = nn(tokens_ref[:, :half], mine_ref[...]) + nn(
        tokens_ref[:, half:], other_ref[...]
    )


def project(tokens, mine, other, inner):
    half = mine.shape[0]
    length = tokens.shape[0]
    tile = 384
    columns = mine.shape[1] - 2 * inner
    return pl.pallas_call(
        project_kernel,
        grid=(columns // tile,),
        in_specs=[whole(tokens.shape)] + [column(half, tile, 2 * inner // tile)] * 2,
        out_specs=column(length, tile),
        out_shape=shape_of((length, columns), F32),
        compiler_params=params(20, "arbitrary"),
        cost_estimate=lasting(6),
        name="project_in",
    )(tokens, mine, other)


def gate_sums_kernel(
    tokens_ref, cot_ref, zm_ref, zo_ref, om_ref, oo_ref, y_ref, gain_ref, z_ref, dy_ref, sums_ref
):
    half = zm_ref.shape[0]
    z = nn(tokens_ref[:, :half], zm_ref[...]) + nn(tokens_ref[:, half:], zo_ref[...])
    dy = nn(cot_ref[:, :half], om_ref[...]) + nn(cot_ref[:, half:], oo_ref[...])
    z_ref[...] = z
    dy_ref[...] = dy
    gated = y_ref[...] * (z * sigmoid(z))
    ones = jnp.ones((8, z.shape[1]), BF)
    found = []
    for value in (gated * gated, gated * (dy * gain_ref[...])):
        high, low = halves(value)
        found.append(nt(ones, high) + nt(ones, low))
    row = lax.broadcasted_iota(jnp.int32, found[0].shape, 0)
    total = jnp.where(row == 0, found[0], found[1])

    @pl.when(pl.program_id(0) == 0)
    def _():
        sums_ref[...] = total

    @pl.when(pl.program_id(0) > 0)
    def _():
        sums_ref[...] += total


def gate_sums(tokens, cot, mine, other, y, gain):
    length, inner = y.shape
    half = mine.shape[0]
    tile = 256
    steps = inner // tile
    return pl.pallas_call(
        gate_sums_kernel,
        grid=(steps,),
        in_specs=[
            whole(tokens.shape),
            whole(cot.shape),
            column(half, tile),
            column(half, tile),
            column(half, tile, steps),
            column(half, tile, steps),
            column(length, tile),
            column(1, tile),
        ],
        out_specs=[column(length, tile), column(length, tile), whole((8, length))],
        out_shape=[
            shape_of((length, inner), F32),
            shape_of((length, inner), F32),
            shape_of((8, length), F32),
        ],
        compiler_params=params(36, "arbitrary"),
        cost_estimate=lasting(9),
        name="gate_sums",
    )(tokens, cot, mine, other, mine, other, y, gain)


def gate_back_kernel(
    width_all, s0, s1, s2, s3, z_ref, dy_ref, y_ref, gain_ref, tokens_t_ref, cot_t_ref,
    normed_ref, gate_ref, dscan_ref, gain_grad_ref, keep_ref, send_ref,
):
    sums = (s0[...] + s1[...]) + (s2[...] + s3[...])
    flat = sums.T
    rms = lax.rsqrt(flat[:, 0:1] / width_all + EPS)
    inner = flat[:, 1:2] * (rms * rms * rms / width_all)
    z = z_ref[...]
    y = y_ref[...]
    dy = dy_ref[...]
    gain = gain_ref[...]
    sig = sigmoid(z)
    act = z * sig
    gated = y * act
    unit = gated * rms
    normed = (unit * gain).astype(BF)
    normed_ref[...] = normed
    gain_grad_ref[...] = jnp.broadcast_to(
        jnp.sum(dy * unit, axis=0, keepdims=True), gain_grad_ref.shape
    )
    d_gated = rms * (dy * gain) - gated * inner
    dscan_ref[...] = d_gated * act
    gate = (d_gated * y * (sig * (1.0 + z * (1.0 - sig)))).astype(BF)
    gate_ref[...] = gate
    half = tokens_t_ref.shape[0] // 2
    for side, (left, right) in enumerate(((tokens_t_ref, gate), (cot_t_ref, normed))):
        for out, at in ((keep_ref, slice(0, half)), (send_ref, slice(half, 2 * half))):
            found = nn(left[at], right).astype(BF)
            out[:, side] = found.reshape(out.shape[0], out.shape[2], found.shape[1])


def gate_back(block, width_all, sums, z, dy, y, gain, tokens_t, cot_t):
    length, inner = y.shape
    half = tokens_t.shape[0] // 2
    tile = 256
    pile = pl.BlockSpec((half // block, 2, block, tile), lambda j: (0, 0, 0, j))
    return pl.pallas_call(
        functools.partial(gate_back_kernel, width_all),
        grid=(inner // tile,),
        in_specs=[whole((8, length))] * 4
        + [column(length, tile)] * 3
        + [column(1, tile), whole(tokens_t.shape), whole(cot_t.shape)],
        out_specs=[column(length, tile)] * 3 + [column(8, tile), pile, pile],
        out_shape=[
            shape_of((length, inner), BF),
            shape_of((length, inner), BF),
            shape_of((length, inner), F32),
            shape_of((8, inner), F32),
            shape_of((half // block, 2, block, inner), BF),
            shape_of((half // block, 2, block, inner), BF),
        ],
        compiler_params=params(44, "arbitrary"),
        cost_estimate=lasting(12),
        name="gate_back",
    )(*sums, z, dy, y, gain, tokens_t, cot_t)


def scatter_rows(meta_ref, found, scratch, outs):
    rows = outs[0].shape[0]
    scratch[...] = found
    for k, out in enumerate(outs):
        out[...] = scratch[pl.ds(pl.multiple_of(meta_ref[k] * rows, rows), rows), :].astype(BF)


def project_out_kernel(meta_ref, normed_ref, om_ref, oo_ref, *refs):
    outs, scratch = refs[:4], refs[4]

    def step(right):
        scatter_rows(meta_ref, nt(normed_ref[...], right[...]), scratch, outs)

    first = pl.program_id(0) < pl.num_programs(0) // 2
    pl.when(first)(lambda: step(om_ref))
    pl.when(jnp.logical_not(first))(lambda: step(oo_ref))


def sides(tile, columns, shift):
    return [
        pl.BlockSpec((pl.Element(tile), pl.Element(columns)), lambda j: (jnp.minimum(j, 1) * tile, shift)),
        pl.BlockSpec((pl.Element(tile), pl.Element(columns)), lambda j: (jnp.maximum(j - 2, 0) * tile, shift)),
    ]


def project_out(meta, normed_y, mine, other):
    length, inner = normed_y.shape
    half = mine.shape[0]
    rows = length // 4
    tile = half // 2
    return pl.pallas_call(
        project_out_kernel,
        grid=(4,),
        in_specs=[pl.BlockSpec(memory_space=pltpu.SMEM), whole(normed_y.shape)]
        + sides(tile, inner, inner),
        out_specs=[column(rows, tile)] * 4,
        out_shape=[shape_of((rows, 2 * half), BF)] * 4,
        scratch_shapes=[pltpu.VMEM((length, tile), F32)],
        compiler_params=params(24, "arbitrary"),
        cost_estimate=lasting(6),
        name="project_out",
    )(meta, normed_y, mine, other)


def project_back_kernel(
    meta_ref, late_ref, gate_ref, xm_ref, xo_ref, zm_ref, zo_ref, tokens_ref, gain_ref, *refs
):
    outs, grad_ref, scratch = refs[:4], refs[4], refs[5]
    tile = scratch.shape[1]
    j = pl.program_id(0)
    side, within = j // 2, j % 2
    core = meta_ref[4]

    def step(x_ref, z_ref):
        found = nt(late_ref[...], x_ref[...]) + nt(gate_ref[...], z_ref[...])
        total = jnp.sum(found * tokens_ref[...].astype(F32), axis=0, keepdims=True)
        owner = side + core - 2 * side * core
        place = pl.ds(pl.multiple_of((2 * owner + within) * tile, 128), tile)
        grad_ref[:, place] = jnp.broadcast_to(total / gain_ref[:, place], (8, tile))
        scatter_rows(meta_ref, found, scratch, outs)

    pl.when(side == 0)(lambda: step(xm_ref, zm_ref))
    pl.when(side == 1)(lambda: step(xo_ref, zo_ref))


def project_back(meta, late, gate, mine1, other1, mine2, other2, tokens, gain):
    length, columns = late.shape
    inner = gate.shape[1]
    half = mine1.shape[0]
    rows = length // 4
    tile = half // 2
    return pl.pallas_call(
        project_back_kernel,
        grid=(4,),
        in_specs=[pl.BlockSpec(memory_space=pltpu.SMEM), whole(late.shape), whole(gate.shape)]
        + sides(tile, columns, 2 * inner)
        + sides(tile, inner, 0)
        + [column(length, tile), whole(gain.shape)],
        out_specs=[column(rows, tile)] * 4 + [whole((8, 2 * half))],
        out_shape=[shape_of((rows, 2 * half), BF)] * 4 + [shape_of((8, 2 * half), F32)],
        scratch_shapes=[pltpu.VMEM((length, tile), F32)],
        compiler_params=params(32, "arbitrary"),
        cost_estimate=lasting(0.5),
        name="project_back",
    )(meta, late, gate, mine1, other1, mine2, other2, tokens, gain)


def weight_grad_kernel(tokens_t_ref, late_ref, vector_ref, keep_ref, send_ref):
    half = keep_ref.shape[0]
    late = late_ref[...]
    keep_ref[...] = nn(tokens_t_ref[:half], late)
    send_ref[:half] = nn(tokens_t_ref[half:], late).astype(BF)
    send_ref[half:] = vector_ref[...].astype(BF)


def weight_grad(tokens_t, late, vector):
    length, columns = late.shape
    half = tokens_t.shape[0] // 2
    rows = half + vector.shape[0]
    tile = 384
    return pl.pallas_call(
        weight_grad_kernel,
        grid=(columns // tile,),
        in_specs=[whole(tokens_t.shape), column(length, tile), column(vector.shape[0], tile)],
        out_specs=[column(half, tile), column(rows, tile)],
        out_shape=[shape_of((half, columns), F32), shape_of((rows, columns), BF)],
        compiler_params=params(24, "arbitrary"),
        cost_estimate=lasting(0.5),
        name="weight_grad",
    )(tokens_t, late, vector)


def pack_kernel(z_ref, out_ref, x_ref, bc_ref, dt_ref, packed_ref):
    at = 0
    for ref in (z_ref, out_ref, x_ref, bc_ref):
        packed_ref[:, at : at + ref.shape[1]] = ref[...]
        at += ref.shape[1]
    heads, rows = dt_ref.shape
    tall = jnp.concatenate([dt_ref[...].astype(F32), jnp.zeros((128 - heads, rows), F32)], axis=0)
    packed_ref[:, at:] = tall.T.astype(BF)


def pack(*parts):
    vmem = pl.BlockSpec()
    return pl.pallas_call(
        pack_kernel,
        in_specs=[vmem] * 5,
        out_specs=vmem,
        out_shape=shape_of(
            (parts[0].shape[0], sum(part.shape[1] for part in parts[:4]) + 128), BF
        ),
        compiler_params=params(8),
        cost_estimate=lasting(1),
        name="pack_weights",
    )(*parts)


def total_kernel(states, got_ref, own_ref, shared_ref):
    total = jnp.sum(got_ref[...].astype(F32), axis=0)
    rows = total.shape[0]
    inner = own_ref.shape[1] - 128
    both = inner + states
    own_ref[:, :inner] = total[:, :inner]
    own_ref[:, inner:] = total[:, both:]
    shared_ref[:rows] = total[:, inner:both]
    per = inner // states
    for k in range(2 * per):
        line = rows - 3 + k // per
        at = states * (k % per)
        shared_ref[rows + k : rows + k + 1] = total[line : line + 1, at : at + states]


def total_of(got, states):
    count, rows, columns = got.shape
    vmem = pl.BlockSpec()
    extra = rows + 2 * ((columns - states - 128) // states)
    return pl.pallas_call(
        functools.partial(total_kernel, states),
        in_specs=[vmem],
        out_specs=[vmem, vmem],
        out_shape=[shape_of((rows, columns - states), F32), shape_of((extra, states), F32)],
        compiler_params=params(16),
        cost_estimate=lasting(3),
        name="late_total",
    )(got)


def deliver_kernel(
    own_ref, s0, s1, s2, s3,
    norm_ref, x_ref, bc_ref, dt_ref, conv_x_ref, conv_bc_ref, head_ref, gate_ref,
):
    shared = (s0[...] + s1[...]) + (s2[...] + s3[...])
    own = own_ref[...]
    block, inner = x_ref.shape
    heads = dt_ref.shape[0]
    x_ref[...] = own[:block, :inner]
    dt_ref[...] = own[:block, inner:].T[:heads]
    conv_x_ref[...] = own[block : block + 5, :inner]
    head_ref[...] = own[block : block + 3, inner : inner + heads]
    gate_ref[...] = own[block + 7, :inner]
    bc_ref[...] = shared[:block]
    conv_bc_ref[...] = shared[block : block + 5]
    states = bc_ref.shape[1]
    for k in range(norm_ref.shape[0] // states):
        norm_ref[states * k : states * k + states] = shared[block + 8 + k]


def deliver(own, shared, block, heads):
    vmem = pl.BlockSpec()
    inner = own.shape[1] - 128
    states = shared[0].shape[1]
    shapes = [
        (2 * inner,), (block, inner), (block, states), (heads, block),
        (5, inner), (5, states), (3, heads), (inner,),
    ]
    return pl.pallas_call(
        deliver_kernel,
        in_specs=[vmem] * 5,
        out_specs=[vmem] * 8,
        out_shape=[shape_of(shape, F32) for shape in shapes],
        compiler_params=params(16),
        cost_estimate=lasting(2),
        name="deliver_late",
    )(own, *shared)


def owner_total(xh_ref, blocks):
    total = sum(block[...].astype(F32) for block in blocks)
    half = total.shape[1] // 2
    turned = jnp.concatenate([total[:, half:], total[:, :half]], axis=1)
    return jnp.where(xh_ref[5] == 0, total, turned)


def output_kernel(meta_ref, b0, b1, b2, b3, hidden_ref, out_ref):
    mixed = owner_total(meta_ref, (b0, b1, b2, b3))
    out_ref[...] = (hidden_ref[...].astype(F32) + mixed).astype(BF)


def finish_output(meta, blocks, hidden):
    vmem = pl.BlockSpec()
    return pl.pallas_call(
        output_kernel,
        in_specs=[pl.BlockSpec(memory_space=pltpu.SMEM)] + [vmem] * 5,
        out_specs=vmem,
        out_shape=shape_of(hidden.shape, BF),
        compiler_params=params(16),
        cost_estimate=lasting(3),
        name="finish_output",
    )(meta, *blocks, hidden)


def input_kernel(meta_ref, b0, b1, b2, b3, hidden_ref, cot_ref, gain_ref, out_ref):
    scaled = owner_total(meta_ref, (b0, b1, b2, b3)) * gain_ref[...]
    resid = hidden_ref[...].astype(F32)
    inv = lax.rsqrt(jnp.mean(resid * resid, axis=1, keepdims=True) + EPS)
    along = jnp.mean(resid * scaled, axis=1, keepdims=True) * (inv * inv * inv)
    out_ref[...] = inv * scaled - resid * along + cot_ref[...].astype(F32)


def finish_input(meta, blocks, hidden, cot, gain):
    vmem = pl.BlockSpec()
    return pl.pallas_call(
        input_kernel,
        in_specs=[pl.BlockSpec(memory_space=pltpu.SMEM)] + [vmem] * 7,
        out_specs=vmem,
        out_shape=shape_of(hidden.shape, F32),
        compiler_params=params(16),
        cost_estimate=lasting(3),
        name="finish_input",
    )(meta, *blocks, hidden, cot, gain)


def mixer_tables(conv_x, conv_bc, head_params):
    heads = head_params.shape[1]
    inner = conv_x.shape[1]
    taps = jnp.pad(jnp.concatenate([conv_x, conv_bc], axis=1), ((0, 3), (0, 0)))
    head = jnp.stack([-jnp.exp(head_params[0]), head_params[1]])
    head = jnp.pad(head, ((0, 6), (0, 128 - heads)))
    skip = jnp.repeat(head_params[2], inner // heads)[None]
    owner = lax.broadcasted_iota(jnp.int32, (256, inner), 1) // (inner // heads)
    one = owner == lax.broadcasted_iota(jnp.int32, (256, inner), 0) % 128
    return taps, head, skip, one.astype(BF)


def mixer_forward(pre, taps, head, skip, spread):
    length, columns = pre.shape
    both = taps.shape[1]
    inner = skip.shape[1]
    steps = length // SPAN
    return pl.pallas_call(
        forward_kernel,
        grid=(steps,),
        in_specs=[
            pl.BlockSpec((SPAN, columns), lambda i: (i, 0)),
            whole(taps.shape), whole(head.shape), whole(skip.shape), whole(spread.shape),
        ],
        out_specs=[
            pl.BlockSpec((SPAN, inner), lambda i: (i, 0)),
            pl.BlockSpec((128, inner), lambda i: (i, 0)),
            pl.BlockSpec((SPAN, both), lambda i: (i, 0)),
        ],
        out_shape=[
            shape_of((length, inner), F32),
            shape_of((steps * 128, inner), BF),
            shape_of((length, both), F32),
        ],
        scratch_shapes=[pltpu.VMEM((SPAN + 8, both), F32), pltpu.VMEM((128, inner), F32)],
        compiler_params=params(20, "arbitrary"),
        cost_estimate=lasting(13),
        name="mixer_forward",
    )(pre, taps, head, skip, spread)


def mixer_backward(pre, conv, dy, kept, taps, head, skip, spread):
    length, columns = pre.shape
    both = taps.shape[1]
    inner = skip.shape[1]
    steps = length // SPAN
    last = steps - 1
    return pl.pallas_call(
        backward_kernel,
        grid=(steps,),
        in_specs=[
            pl.BlockSpec((SPAN, columns), lambda i: (last - i, 0)),
            pl.BlockSpec((SPAN, both), lambda i: (last - i, 0)),
            pl.BlockSpec((SPAN, inner), lambda i: (last - i, 0)),
            pl.BlockSpec((128, inner), lambda i: (last - i, 0)),
            whole(taps.shape), whole(head.shape), whole(skip.shape), whole(spread.shape),
        ],
        out_specs=[
            pl.BlockSpec((SPAN, columns), lambda i: (last - i, 0)),
            whole((8, both)),
            whole((8, 128)),
        ],
        out_shape=[
            shape_of((length, columns), BF),
            shape_of((8, both), F32),
            shape_of((8, 128), F32),
        ],
        scratch_shapes=[
            pltpu.VMEM((SPAN + 8, both), F32),
            pltpu.VMEM((128, inner), F32),
            pltpu.VMEM((8, inner), F32),
        ],
        compiler_params=params(24, "arbitrary"),
        cost_estimate=lasting(30),
        name="mixer_backward",
    )(pre, conv, dy, kept, taps, head, skip, spread)


CELLS = [(xh, xl, core) for xh in range(2) for xl in range(2) for core in range(2)]
TURNS = [(a, b) for a in range(2) for b in range(2)]


def moves(rule):
    return [(4 * c[0] + 2 * c[1] + c[2], 4 * d[0] + 2 * d[1] + d[2]) for c in CELLS for d in [rule(*c)]]


def permute(value, rule):
    return lax.ppermute(value, GROUP, moves(rule))


def trade(value):
    return permute(
        value, lambda xh, xl, core: (xh, xl, core) if xh == core else (1 - xh, xl, 1 - core)
    )


def swap_core(value):
    return lax.ppermute(value, "core", [(0, 1), (1, 0)])


def to_workers(value):
    return [
        permute(value, lambda xh, xl, core, a=a, b=b: (core ^ a, xl ^ b, xh)) for a, b in TURNS
    ]


def to_owners(blocks):
    return [
        permute(block, lambda xh, xl, core, a=a, b=b: (core, xl ^ b, xh ^ a))
        for block, (a, b) in zip(blocks, TURNS)
    ]


def around(value):
    return [value] + [
        permute(value, lambda xh, xl, core, a=a, b=b: (xh ^ a, xl ^ b, core)) for a, b in TURNS[1:]
    ]


def gather_plane(shard):
    count = lax.axis_size(PLANE)
    spread = jnp.broadcast_to(shard[None], (count,) + shard.shape)
    got = lax.all_to_all(spread, PLANE, 0, 0, tiled=True)
    return got.reshape((count * shard.shape[0],) + shard.shape[1:])


def exchange(blocks):
    return lax.all_to_all(blocks, PLANE, 0, 0, tiled=True)


def after(*values):
    return lax.optimization_barrier(values)


def on_device(
    hidden_in,
    cotangent,
    norm_gain,
    w_z,
    w_x,
    w_bc,
    w_dt,
    conv_x,
    conv_bc,
    head_params,
    gate_gain,
    w_out,
):
    block, wide = w_x.shape
    states = w_bc.shape[1]
    heads = w_dt.shape[1]
    both = wide + states
    xh, xl, core = (lax.axis_index(axis) for axis in GROUP)
    meta = jnp.stack([(xl ^ b) * 2 + (xh ^ a) for a, b in TURNS] + [core, xh]).astype(jnp.int32)
    gain = norm_gain[None]

    weights = trade(pack(w_z, w_out.T, w_x, w_bc, w_dt.T))
    small = jnp.concatenate(
        [conv_x, gate_gain[None], jnp.pad(head_params, ((0, 0), (0, wide - heads)))[:2]]
    )
    small = jnp.concatenate([small, jnp.pad(head_params[2:], ((0, 7), (0, wide - heads)))])
    small, weights = after(small, weights)
    small = jnp.where(core == xh, small, swap_core(small))

    mine = gather_plane(weights)
    hidden, weights = after(hidden_in, weights)
    hidden_blocks = to_workers(hidden)
    first_half, cot, small = after(hidden_blocks[:2], cotangent, small)
    hidden_blocks = first_half + hidden_blocks[2:]
    cot_blocks = to_workers(cot)
    tokens, tokens_t = place(meta, gain, hidden_blocks, True)
    tokens, mine, cot_first = after(tokens, mine, cot_blocks[0])
    cot_blocks = [cot_first] + cot_blocks[1:]
    other = swap_core(mine)

    conv_x, gate_row, head_params = small[:5], small[5:6], small[6:9, :heads]
    taps, head, skip, spread = mixer_tables(conv_x, conv_bc, head_params)
    pre = project(tokens, mine, other, wide)
    y, kept, conv = mixer_forward(pre, taps, head, skip, spread)
    y, cot_blocks = after(y, cot_blocks)
    cot, cot_t = place(meta, gain, cot_blocks, False)
    z, dy, sums = gate_sums(tokens, cot, mine, other, y, gate_row)
    normed_y, gate, dscan, gain_grad, keep, send = gate_back(
        block, 4.0 * wide, around(sums), z, dy, y, gate_row, tokens_t, cot_t
    )

    early = (keep.astype(F32) + swap_core(send).astype(F32)).astype(BF)
    out_blocks = project_out(meta, normed_y, mine, other)
    dscan, early, out_blocks = after(dscan, early, out_blocks)
    early = exchange(early)
    out_blocks = to_owners(out_blocks)
    late, conv_grad, head_grad = mixer_backward(pre, conv, dscan, kept, taps, head, skip, spread)
    *back_blocks, norm_part = project_back(
        meta, late, gate, mine, other, mine, other, tokens, gain
    )
    late, back_blocks, out_blocks = after(late, back_blocks, out_blocks)
    back_blocks = to_owners(back_blocks)

    rest = jnp.pad(
        jnp.concatenate([norm_part[:1, :wide], norm_part[:1, wide:], gain_grad[:1]]),
        ((0, 0), (0, states)),
    )
    vector = jnp.concatenate([jnp.concatenate([conv_grad[:5], rest]), head_grad], axis=1)
    vector = jnp.pad(vector, ((0, 8), (0, 0)))
    keep, send = weight_grad(tokens_t, late, vector)
    send, early, back_first = after(send, early, back_blocks[0])
    output = finish_output(meta, out_blocks, hidden_in)
    got = swap_core(send).astype(F32)
    half = keep.shape[0]
    late_sum = (keep + got[:half]).astype(BF).reshape(-1, block, both + 128)
    vector = (vector[:8] + got[half : half + 8]).astype(BF)
    vector = jnp.broadcast_to(vector[None], (late_sum.shape[0],) + vector.shape)
    late_sum = jnp.concatenate([late_sum, vector], axis=1)
    back_blocks = [back_first] + back_blocks[1:]
    input_grad = finish_input(meta, back_blocks, hidden_in, cotangent, gain)
    early = trade(early.astype(F32).sum(axis=0))
    got, input_grad, early, output = after(exchange(late_sum), input_grad, early, output)
    own, shared = total_of(got, states)

    shared = [
        permute(shared, lambda xh, xl, core, a=a, b=b: (core, xl ^ b, xh ^ a)) for a, b in TURNS
    ]
    norm_grad, x_grad, bc_grad, dt_grad, conv_x_grad, conv_bc_grad, head_part, gate_part = deliver(
        trade(own), shared, block, heads
    )
    return (
        output,
        input_grad,
        norm_grad,
        early[0],
        x_grad,
        bc_grad,
        dt_grad.T,
        conv_x_grad,
        conv_bc_grad,
        head_part,
        gate_part,
        early[1].T,
    )


def solution(mesh):
    fine = Mesh(mesh.devices.reshape(2, 4, 4, 2, 2), AXES)
    rows, both, lanes = P(AXES, None), P(DP, TN), P(None, TN)
    return jax.shard_map(
        on_device,
        mesh=fine,
        in_specs=(rows, rows, P(), both, both, P(DP, None), both, lanes, P(), lanes, P(TN), P(TN, DP)),
        out_specs=(
            rows, rows, P(), both, both, P(DP, None), both, lanes, P(), lanes, P(TN), P(TN, DP)
        ),
        check_vma=False,
    )
```

profile of v0, /device:TPU:1, one launch (start us, length us, event | category | flops | bytes accessed | tf_op | source)
XLA Modules:
  0.0 298.9 jit_solution(10329168487568323274)
XLA Ops:
  0.7 0.9 copy-done.6
  1.6 0.9 copy-done.7
  2.4 0.9 copy-done.8
  3.3 0.7 copy-done.9
  4.8 6.0 %collective-permute-start = (bf16[48,2688]{1,0:T(8,128)(2,1)S(1)}, bf16[48,2688]{1,0:T(8,128)(2,1)S(1)}, u32[]{:S(2)}, u32[]{:S(2)}) collective-permute-start(bf16[48,2688]{1,0:T(8,128)(2,1)S(1)} %pack_weights.1), channel_id=1, source_target_pairs={{0,0},{1,64},{2,2},{3,66},{64,1},{65,65},{66,3},{67,67},{4,4},{5,6... | collective-permute-start | bytes 774152 | tf_op jit(solution)/shard_map/ppermute | solution.py:787
  11.0 3.9 %collective-permute-done = bf16[48,2688]{1,0:T(8,128)(2,1)S(1)} collective-permute-done((bf16[48,2688]{1,0:T(8,128)(2,1)S(1)}, bf16[48,2688]{1,0:T(8,128)(2,1)S(1)}, u32[]{:S(2)}, u32[]{:S(2)}) %collective-permute-start) | collective-permute-done | bytes 258080 | tf_op jit(solution)/shard_map/ppermute | solution.py:787
  14.9 2.2 broadcast_in_dim.23
  17.1 7.9 %all-to-all-start = ((bf16[16,48,2688]{2,1,0:T(8,128)(2,1)}), bf16[16,48,2688]{2,1,0:T(8,128)(2,1)}, u32[]{:S(2)}, u32[]{:S(2)}) async-start(bf16[16,48,2688]{2,1,0:T(8,128)(2,1)} %broadcast_in_dim.23), calls=%async_computation | async-start | bytes 8257536 | tf_op jit(solution)/shard_map/all_to_all | solution.py:822
  25.1 3.3 %collective-permute-start.2 = (bf16[256,1536]{1,0:T(8,128)(2,1)S(1)}, bf16[256,1536]{1,0:T(8,128)(2,1)S(1)}, u32[]{:S(2)}, u32[]{:S(2)}) collective-permute-start(bf16[256,1536]{1,0:T(8,128)(2,1)S(1)} %copy-done.20), channel_id=1, source_target_pairs={{0,2},{1,66},{2,0},{3,64},{64,3},{65,67},{66,1},{67,65},{4,6},{5,7... | collective-permute-start | bytes 2359304 | tf_op jit(solution)/shard_map/ppermute | solution.py:787
  28.4 2.2 collective-permute-start.1
  30.7 2.7 collective-permute-start.4
  33.4 0.7 collective-permute-start.3
  34.1 1.3 collective-permute-done.3
  35.4 24.9 %collective-permute-done.2.refs_1_ = bf16[256,1536]{1,0:T(8,128)(2,1)S(1)} collective-permute-done((bf16[256,1536]{1,0:T(8,128)(2,1)S(1)}, bf16[256,1536]{1,0:T(8,128)(2,1)S(1)}, u32[]{:S(2)}, u32[]{:S(2)}) %collective-permute-start.2) | collective-permute-done | bytes 786464 | tf_op jit(solution)/shard_map/ppermute | solution.py:787
  60.2 3.4 %collective-permute-start.6 = (bf16[256,1536]{1,0:T(8,128)(2,1)}, bf16[256,1536]{1,0:T(8,128)(2,1)S(1)}, u32[]{:S(2)}, u32[]{:S(2)}) collective-permute-start(bf16[256,1536]{1,0:T(8,128)(2,1)} %cot_ref.1), channel_id=1, source_target_pairs={{0,0},{1,64},{2,2},{3,66},{64,1},{65,65},{66,3},{67,67},{4,4},{5,6... | collective-permute-start | bytes 2359304 | tf_op jit(solution)/shard_map/ppermute | solution.py:787
  63.8 6.0 %place_normed.1 = (bf16[1024,1536]{1,0:T(8,128)(2,1)}, bf16[1536,1024]{1,0:T(8,128)(2,1)}) custom-call(s32[6]{0:T(128)S(1)} %stack.31.meta_ref, f32[1,1536]{1,0:T(1,128)S(1)} %broadcast_in_dim.10.gain_ref, bf16[256,1536]{1,0:T(8,128)(2,1)S(1)} %collective-permute-done.1.refs_0_, bf16[256,1536]{1,0:T(8,128)(2,1)S(1)} %collective-permute-done.2.refs_1_, ...), custom_call_target="tpu_custom_call" | custom-call | flops 6899999744 | bytes 1024 | tf_op jit(solution)/shard_map/place_normed/pallas_call | solution.py:299
  69.8 5.5 %collective-permute-done.6.refs_0_ = bf16[256,1536]{1,0:T(8,128)(2,1)S(1)} collective-permute-done((bf16[256,1536]{1,0:T(8,128)(2,1)}, bf16[256,1536]{1,0:T(8,128)(2,1)S(1)}, u32[]{:S(2)}, u32[]{:S(2)}) %collective-permute-start.6) | collective-permute-done | bytes 786464 | tf_op jit(solution)/shard_map/ppermute | solution.py:787
  75.5 1.5 collective-permute-start.10
  77.0 2.7 collective-permute-start.9
  80.1 2.6 collective-permute-done.7.other_ref.zo_ref.oo_ref.xo_ref
  82.7 8.9 %project_in.1.pre_ref = f32[1024,1152]{1,0:T(8,128)} custom-call(bf16[1024,1536]{1,0:T(8,128)(2,1)} %get-tuple-element.97.tokens_ref, bf16[768,2688]{1,0:T(8,128)(2,1)} %bitcast.8.mine_ref.zm_ref.om_ref.xm_ref, bf16[768,2688]{1,0:T(8,128)(2,1)} %collective-permute-done.7.other_ref.zo_ref.oo_ref.xo_ref), custom_call_target="tpu_custom_call" | custom-call | flops 6899999744 | bytes 1024 | tf_op jit(solution)/shard_map/project_in/pallas_call | solution.py:322
  91.5 13.0 %mixer_forward.1 = (f32[1024,768]{1,0:T(8,128)}, bf16[1024,768]{1,0:T(8,128)(2,1)S(1)}, f32[1024,1024]{1,0:T(8,128)}) custom-call(f32[1024,1152]{1,0:T(8,128)} %project_in.1.pre_ref, f32[8,1024]{1,0:T(8,128)S(1)} %select_maximum_fusion.1.taps_ref, f32[8,128]{1,0:T(8,128)S(1)} %select_maximum_fusion.4.head_ref, ...), custom_call_target="tpu_custom_call" | custom-call | flops 14949999616 | bytes 1024 | tf_op jit(solution)/shard_map/mixer_forward/pallas_call | solution.py:717
  104.6 1.1 collective-permute-done.8.refs_1_
  105.7 5.0 %place_cotangent.1 = (bf16[1024,1536]{1,0:T(8,128)(2,1)}, bf16[1536,1024]{1,0:T(8,128)(2,1)}) custom-call(s32[6]{0:T(128)S(1)} %stack.31.meta_ref, f32[1,1536]{1,0:T(1,128)S(1)} %broadcast_in_dim.10.gain_ref, bf16[256,1536]{1,0:T(8,128)(2,1)S(1)} %collective-permute-done.6.refs_0_, bf16[256,1536]{1,0:T(8,128)(2,1)S(1)} %collective-permute-done.8.refs_1_, ...), custom_call_target="tpu_custom_call" | custom-call | flops 6899999744 | bytes 1024 | tf_op jit(solution)/shard_map/place_cotangent/pallas_call | solution.py:299
  110.7 12.6 %gate_sums.1 = (f32[1024,768]{1,0:T(8,128)}, f32[1024,768]{1,0:T(8,128)}, f32[8,1024]{1,0:T(8,128)S(1)}) custom-call(bf16[1024,1536]{1,0:T(8,128)(2,1)} %get-tuple-element.97.tokens_ref, bf16[1024,1536]{1,0:T(8,128)(2,1)} %get-tuple-element.107.cot_ref, bf16[768,2688]{1,0:T(8,128)(2,1)} %bitcast.8.mine_ref.zm_ref.om_ref.xm_ref, ...), custom_call_target="tpu_custom_call" | custom-call | flops 10350000128 | bytes 1024 | tf_op jit(solution)/shard_map/gate_sums/pallas_call | solution.py:365
  123.3 2.9 collective-permute-start.13
  126.3 0.8 collective-permute-start.11
  127.6 3.0 collective-permute-done.12.s2
  130.5 14.2 %gate_back.1 = (bf16[1024,768]{1,0:T(8,128)(2,1)S(1)}, bf16[1024,768]{1,0:T(8,128)(2,1)}, f32[1024,768]{1,0:T(8,128)}, f32[8,768]{1,0:T(8,128)S(1)}, bf16[16,2,4...) custom-call(f32[8,1024]{1,0:T(8,128)S(1)} %get-tuple-element.109.s0, f32[8,1024]{1,0:T(8,128)S(1)} %collective-permute-done.11.s1, ...), custom_call_target="tpu_custom_call" | custom-call | flops 13799999488 | bytes 1024 | tf_op jit(solution)/shard_map/gate_back/pallas_call | solution.py:427
  144.8 1.2 copy-done.11
  145.9 2.4 collective-permute-start.14
  148.4 7.4 %project_out.1 = (bf16[256,1536]{1,0:T(8,128)(2,1)}, bf16[256,1536]{1,0:T(8,128)(2,1)S(1)}, bf16[256,1536]{1,0:T(8,128)(2,1)}, bf16[256,1536]{1,0:T(8,128)(2,1)}) custom-call(s32[6]{0:T(128)S(1)} %stack.31.meta_ref, bf16[1024,768]{1,0:T(8,128)(2,1)} %copy-done.11, bf16[768,2688]{1,0:T(8,128)(2,1)} %bitcast.8.mine_ref.zm_ref.om_ref.xm_ref, ...), custom_call_target="tpu_custom_call" | custom-call | flops 6899999744 | bytes 1024 | tf_op jit(solution)/shard_map/project_out/pallas_call | solution.py:478
  155.8 2.2 add_convert_fusion
  158.0 7.1 %all-to-all-start.1 = ((bf16[16,2,48,768]{3,2,1,0:T(8,128)(2,1)}), bf16[16,2,48,768]{3,2,1,0:T(8,128)(2,1)}, u32[]{:S(2)}, u32[]{:S(2)}) async-start(bf16[16,2,48,768]{3,2,1,0:T(8,128)(2,1)} %add_convert_fusion), calls=%async_computation.1 | async-start | bytes 4718592 | tf_op jit(solution)/shard_map/all_to_all | solution.py:827
  165.0 3.8 %collective-permute-start.15 = (bf16[256,1536]{1,0:T(8,128)(2,1)}, bf16[256,1536]{1,0:T(8,128)(2,1)S(1)}, u32[]{:S(2)}, u32[]{:S(2)}) collective-permute-start(bf16[256,1536]{1,0:T(8,128)(2,1)} %get-tuple-element.129), channel_id=1, source_target_pairs={{0,0},{1,64},{2,2},{3,66},{64,1},{65,65},{66,3},{67,67},{4,4},{5,6... | collective-permute-start | bytes 2359304 | tf_op jit(solution)/shard_map/ppermute | solution.py:787
  169.1 3.0 collective-permute-start.18
  172.0 27.3 %mixer_backward.1 = (bf16[1024,1152]{1,0:T(8,128)(2,1)}, f32[8,1024]{1,0:T(8,128)S(1)}, f32[8,128]{1,0:T(8,128)S(1)}) custom-call(f32[1024,1152]{1,0:T(8,128)} %project_in.1.pre_ref, f32[1024,1024]{1,0:T(8,128)} %get-tuple-element.100.conv_ref, f32[1024,768]{1,0:T(8,128)} %get-tuple-element.121.dy_ref, bf16[1024,768]{1,0:T(8,128)(2,1)} %copy-done.12, ...), custom_call_target="tpu_custom_call" | custom-call | flops 34500001792 | bytes 1024 | tf_op jit(solution)/shard_map/mixer_backward/pallas_call | solution.py:747
  199.4 14.0 %project_back.1 = (bf16[256,1536]{1,0:T(8,128)(2,1)S(1)}, bf16[256,1536]{1,0:T(8,128)(2,1)S(1)}, bf16[256,1536]{1,0:T(8,128)(2,1)}, bf16[256,1536]{1,0:T(8,128)(2,1)}, f32[8,1536]{1,0:T(8,128)S(1)}) custom-call(s32[6]{0:T(128)S(1)} %stack.31.meta_ref, bf16[1024,1152]{1,0:T(8,128)(2,1)} %get-tuple-element.133.late_ref, ...), custom_call_target="tpu_custom_call" | custom-call | flops 575000000 | bytes 1024 | tf_op jit(solution)/shard_map/project_back/pallas_call | solution.py:519
  213.4 0.9 copy-done.2
  214.3 0.9 copy-done
  215.2 2.3 collective-permute-start.19
  217.6 7.9 %weight_grad.1 = (f32[768,1152]{1,0:T(8,128)}, bf16[784,1152]{1,0:T(8,128)(2,1)S(1)}) custom-call(bf16[1536,1024]{1,0:T(8,128)(2,1)} %get-tuple-element.94.tokens_t_ref, bf16[1024,1152]{1,0:T(8,128)(2,1)} %get-tuple-element.133.late_ref, f32[16,1152]{1,0:T(8,128)S(1)} %pad.29.vector_ref), custom_call_target="tpu_custom_call" | custom-call | flops 575000000 | bytes 1024 | tf_op jit(solution)/shard_map/weight_grad/pallas_call | solution.py:548
  225.5 4.5 %collective-permute-done.19.b0 = bf16[256,1536]{1,0:T(8,128)(2,1)S(1)} collective-permute-done((bf16[256,1536]{1,0:T(8,128)(2,1)S(1)}, bf16[256,1536]{1,0:T(8,128)(2,1)S(1)}, u32[]{:S(2)}, u32[]{:S(2)}) %collective-permute-start.19) | collective-permute-done | bytes 786464 | tf_op jit(solution)/shard_map/ppermute | solution.py:787
  230.0 0.9 copy-done.4
  230.9 3.7 %collective-permute-done.20 = bf16[784,1152]{1,0:T(8,128)(2,1)S(1)} collective-permute-done((bf16[784,1152]{1,0:T(8,128)(2,1)S(1)}, bf16[784,1152]{1,0:T(8,128)(2,1)S(1)}, u32[]{:S(2)}, u32[]{:S(2)}) %collective-permute-start.20) | collective-permute-done | bytes 1806368 | tf_op jit(solution)/shard_map/ppermute | solution.py:797
  235.5 1.5 pad_maximum_fusion
  237.0 7.0 %all-to-all-start.2 = ((bf16[16,56,1152]{2,1,0:T(8,128)(2,1)}), bf16[16,56,1152]{2,1,0:T(8,128)(2,1)}, u32[]{:S(2)}, u32[]{:S(2)}) async-start(bf16[16,56,1152]{2,1,0:T(8,128)(2,1)} %pad_maximum_fusion), calls=%async_computation.2 | async-start | bytes 4128768 | tf_op jit(solution)/shard_map/all_to_all | solution.py:827
  245.3 1.8 collective-permute-start.23
  247.2 3.0 %finish_output.1 = bf16[256,1536]{1,0:T(8,128)(2,1)} custom-call(s32[6]{0:T(128)S(1)} %stack.31.meta_ref, bf16[256,1536]{1,0:T(8,128)(2,1)S(1)} %collective-permute-done.15.b0, bf16[256,1536]{1,0:T(8,128)(2,1)S(1)} %copy-done.1, bf16[256,1536]{1,0:T(8,128)(2,1)} %copy-done.22, bf16[256,1536]{1,0:T(8,128)(2,1)} %copy-done.23, bf16[256,1536]{1,0:T(8,128)(2,1)} %hidden_ref.3), custom_call_target="tpu_custom_call" | custom-call | flops 3449999872 | bytes 1024 | tf_op jit(solution)/shard_map/finish_output/pallas_call | solution.py:668
  250.2 2.0 convert_reduce_fusion
  252.2 3.2 %collective-permute-start.24 = (f32[2,48,768]{2,1,0:T(8,128)S(1)}, f32[2,48,768]{2,1,0:T(8,128)S(1)}, u32[]{:S(2)}, u32[]{:S(2)}) collective-permute-start(f32[2,48,768]{2,1,0:T(8,128)S(1)} %convert_reduce_fusion), channel_id=1, source_target_pairs={{0,0},{1,64},{2,2},{3,66},{64,1},{65,65},{66,3},{67,67},{4,4},{5,6... | collective-permute-start | bytes 884744 | tf_op jit(solution)/shard_map/ppermute | solution.py:787
  255.5 9.1 %collective-permute-done.21.b1 = bf16[256,1536]{1,0:T(8,128)(2,1)S(1)} collective-permute-done((bf16[256,1536]{1,0:T(8,128)(2,1)S(1)}, bf16[256,1536]{1,0:T(8,128)(2,1)S(1)}, u32[]{:S(2)}, u32[]{:S(2)}) %collective-permute-start.21) | collective-permute-done | bytes 786464 | tf_op jit(solution)/shard_map/ppermute | solution.py:787
  264.6 10.2 %collective-permute-done.23.b3 = bf16[256,1536]{1,0:T(8,128)(2,1)S(1)} collective-permute-done((bf16[256,1536]{1,0:T(8,128)(2,1)S(1)}, bf16[256,1536]{1,0:T(8,128)(2,1)S(1)}, u32[]{:S(2)}, u32[]{:S(2)}) %collective-permute-start.23) | collective-permute-done | bytes 786464 | tf_op jit(solution)/shard_map/ppermute | solution.py:787
  274.8 0.9 copy-done.27
  275.7 4.2 %finish_input.1 = f32[256,1536]{1,0:T(8,128)} custom-call(s32[6]{0:T(128)S(1)} %stack.31.meta_ref, bf16[256,1536]{1,0:T(8,128)(2,1)S(1)} %copy-done.5, bf16[256,1536]{1,0:T(8,128)(2,1)S(1)} %collective-permute-done.21.b1, bf16[256,1536]{1,0:T(8,128)(2,1)} %copy-done.26, bf16[256,1536]{1,0:T(8,128)(2,1)} %copy-done.27, bf16[256,1536]{1,0:T(8,128)(2,1)} %hidden_ref.3, ...), custom_call_target="tpu_custom_call" | custom-call | flops 3449999872 | bytes 1024 | tf_op jit(solution)/shard_map/finish_input/pallas_call | solution.py:689
  279.9 1.8 late_total.1
  281.7 2.1 collective-permute-start.29
  283.8 1.0 collective-permute-start.28
  284.8 2.5 collective-permute-start.27
  287.3 2.3 collective-permute-start.26
  289.6 4.8 %collective-permute-start.25 = (f32[56,896]{1,0:T(8,128)S(1)}, f32[56,896]{1,0:T(8,128)S(1)}, u32[]{:S(2)}, u32[]{:S(2)}) collective-permute-start(f32[56,896]{1,0:T(8,128)S(1)} %get-tuple-element.155), channel_id=1, source_target_pairs={{0,0},{1,64},{2,2},{3,66},{64,1},{65,65},{66,3},{67,67},{4,4},{5,6... | collective-permute-start | bytes 602120 | tf_op jit(solution)/shard_map/ppermute | solution.py:787
  294.4 0.7 slice_bitcast_fusion
  295.1 3.0 %collective-permute-done.25.own_ref = f32[56,896]{1,0:T(8,128)S(1)} collective-permute-done((f32[56,896]{1,0:T(8,128)S(1)}, f32[56,896]{1,0:T(8,128)S(1)}, u32[]{:S(2)}, u32[]{:S(2)}) %collective-permute-start.25) | collective-permute-done | bytes 200736 | tf_op jit(solution)/shard_map/ppermute | solution.py:787
  298.1 0.7 deliver_late.1
  (106 shorter events, 4.5 us)
Async XLA Ops:
  0.6 10.2 %copy-start.19 = (f32[3,12]{1,0:T(4,128)S(1)}, f32[3,12]{1,0:T(4,128)}, u32[]{:S(2)}) copy-start(f32[3,12]{1,0:T(4,128)} %param.21) | copy-start | bytes 436
  0.7 0.9 copy-start.6
  1.5 0.9 copy-start.7
  2.4 0.9 copy-start.8
  3.3 0.7 copy-start.9
  4.1 0.7 copy-start.10
  4.7 6.2 %copy-start.18 = (f32[768]{0:T(1024)S(1)}, f32[768]{0:T(1024)}, u32[]{:S(2)}) copy-start(f32[768]{0:T(1024)} %param.22) | copy-start | bytes 9220
  4.7 6.2 %copy-start.15 = (f32[5,768]{1,0:T(8,128)S(1)}, f32[5,768]{1,0:T(8,128)}, u32[]{:S(2)}) copy-start(f32[5,768]{1,0:T(8,128)} %param.19) | copy-start | bytes 46084
  4.8 10.0 %collective-permute-start = (bf16[48,2688]{1,0:T(8,128)(2,1)S(1)}, bf16[48,2688]{1,0:T(8,128)(2,1)S(1)}, u32[]{:S(2)}, u32[]{:S(2)}) collective-permute-start(bf16[48,2688]{1,0:T(8,128)(2,1)S(1)} %pack_weights.1), channel_id=1, source_target_pairs={{0,0},{1,64},{2,2},{3,66},{64,1},{65,65},{66,3},{67,67},{4,4},{5,6... | collective-permute-start | bytes 774152 | tf_op jit(solution)/shard_map/ppermute | solution.py:787
  17.1 8.0 %copy-start.20 = (bf16[256,1536]{1,0:T(8,128)(2,1)S(1)}, bf16[256,1536]{1,0:T(8,128)(2,1)}, u32[]{:S(2)}) copy-start(bf16[256,1536]{1,0:T(8,128)(2,1)} %hidden_ref.3) | copy-start | bytes 2359300
  17.1 46.6 %copy-start.16 = (f32[1536]{0:T(1024)S(1)}, f32[1536]{0:T(1024)}, u32[]{:S(2)}) copy-start(f32[1536]{0:T(1024)} %param.14) | copy-start | bytes 18436
  17.1 58.2 %all-to-all-start = ((bf16[16,48,2688]{2,1,0:T(8,128)(2,1)}), bf16[16,48,2688]{2,1,0:T(8,128)(2,1)}, u32[]{:S(2)}, u32[]{:S(2)}) async-start(bf16[16,48,2688]{2,1,0:T(8,128)(2,1)} %broadcast_in_dim.23), calls=%async_computation | async-start | bytes 8257536 | tf_op jit(solution)/shard_map/all_to_all | solution.py:822
  25.1 35.2 %collective-permute-start.2 = (bf16[256,1536]{1,0:T(8,128)(2,1)S(1)}, bf16[256,1536]{1,0:T(8,128)(2,1)S(1)}, u32[]{:S(2)}, u32[]{:S(2)}) collective-permute-start(bf16[256,1536]{1,0:T(8,128)(2,1)S(1)} %copy-done.20), channel_id=1, source_target_pairs={{0,2},{1,66},{2,0},{3,64},{64,3},{65,67},{66,1},{67,65},{4,6},{5,7... | collective-permute-start | bytes 2359304 | tf_op jit(solution)/shard_map/ppermute | solution.py:787
  28.4 31.8 %collective-permute-start.1 = (bf16[256,1536]{1,0:T(8,128)(2,1)S(1)}, bf16[256,1536]{1,0:T(8,128)(2,1)S(1)}, u32[]{:S(2)}, u32[]{:S(2)}) collective-permute-start(bf16[256,1536]{1,0:T(8,128)(2,1)S(1)} %copy-done.20), channel_id=1, source_target_pairs={{0,0},{1,64},{2,2},{3,66},{64,1},{65,65},{66,3},{67,67},{4,4},{5,6... | collective-permute-start | bytes 2359304 | tf_op jit(solution)/shard_map/ppermute | solution.py:787
  30.6 33.2 %collective-permute-start.5 = (bf16[256,1536]{1,0:T(8,128)(2,1)S(1)}, bf16[256,1536]{1,0:T(8,128)(2,1)}, u32[]{:S(2)}, u32[]{:S(2)}) collective-permute-start(bf16[256,1536]{1,0:T(8,128)(2,1)S(1)} %copy-done.20), channel_id=1, source_target_pairs={{0,66},{1,2},{2,64},{3,0},{64,67},{65,3},{66,65},{67,1},{4,70},{5,... | collective-permute-start | bytes 2359304 | tf_op jit(solution)/shard_map/ppermute | solution.py:787
  30.7 33.1 %collective-permute-start.4 = (bf16[256,1536]{1,0:T(8,128)(2,1)S(1)}, bf16[256,1536]{1,0:T(8,128)(2,1)}, u32[]{:S(2)}, u32[]{:S(2)}) collective-permute-start(bf16[256,1536]{1,0:T(8,128)(2,1)S(1)} %copy-done.20), channel_id=1, source_target_pairs={{0,64},{1,0},{2,66},{3,2},{64,65},{65,1},{66,67},{67,3},{4,68},{5,... | collective-permute-start | bytes 2359304 | tf_op jit(solution)/shard_map/ppermute | solution.py:787
  33.4 2.0 collective-permute-start.3
  60.2 15.0 %collective-permute-start.6 = (bf16[256,1536]{1,0:T(8,128)(2,1)}, bf16[256,1536]{1,0:T(8,128)(2,1)S(1)}, u32[]{:S(2)}, u32[]{:S(2)}) collective-permute-start(bf16[256,1536]{1,0:T(8,128)(2,1)} %cot_ref.1), channel_id=1, source_target_pairs={{0,0},{1,64},{2,2},{3,66},{64,1},{65,65},{66,3},{67,67},{4,4},{5,6... | collective-permute-start | bytes 2359304 | tf_op jit(solution)/shard_map/ppermute | solution.py:787
  63.8 16.2 %copy-start.17 = (f32[5,256]{1,0:T(8,128)S(1)}, f32[5,256]{1,0:T(8,128)}, u32[]{:S(2)}) copy-start(f32[5,256]{1,0:T(8,128)} %param.20) | copy-start | bytes 15364
  63.8 11.7 %copy-start.21 = (bf16[256,1536]{1,0:T(8,128)(2,1)S(1)}, bf16[256,1536]{1,0:T(8,128)(2,1)}, u32[]{:S(2)}) copy-start(bf16[256,1536]{1,0:T(8,128)(2,1)} %cot_ref.1) | copy-start | bytes 2359300
  75.3 7.4 %collective-permute-start.7 = (bf16[768,2688]{1,0:T(8,128)(2,1)}, bf16[768,2688]{1,0:T(8,128)(2,1)}, u32[]{:S(2)}, u32[]{:S(2)}) collective-permute-start(bf16[768,2688]{1,0:T(8,128)(2,1)} %bitcast.8.mine_ref.zm_ref.om_ref.xm_ref), channel_id=1, source_target_pairs={{0,1},{1,0},{2,3},{3,2},{4,5},{5,4},{6,7},{7,6},{8,9},{9,8},{10,11... | collective-permute-start | bytes 12386312 | tf_op jit(solution)/shard_map/ppermute | solution.py:797
  75.5 29.1 %collective-permute-start.10 = (bf16[256,1536]{1,0:T(8,128)(2,1)S(1)}, bf16[256,1536]{1,0:T(8,128)(2,1)}, u32[]{:S(2)}, u32[]{:S(2)}) collective-permute-start(bf16[256,1536]{1,0:T(8,128)(2,1)S(1)} %copy-done.21), channel_id=1, source_target_pairs={{0,66},{1,2},{2,64},{3,0},{64,67},{65,3},{66,65},{67,1},{4,70},{5,... | collective-permute-start | bytes 2359304 | tf_op jit(solution)/shard_map/ppermute | solution.py:787
  77.0 27.6 %collective-permute-start.9 = (bf16[256,1536]{1,0:T(8,128)(2,1)S(1)}, bf16[256,1536]{1,0:T(8,128)(2,1)}, u32[]{:S(2)}, u32[]{:S(2)}) collective-permute-start(bf16[256,1536]{1,0:T(8,128)(2,1)S(1)} %copy-done.21), channel_id=1, source_target_pairs={{0,64},{1,0},{2,66},{3,2},{64,65},{65,1},{66,67},{67,3},{4,68},{5,... | collective-permute-start | bytes 2359304 | tf_op jit(solution)/shard_map/ppermute | solution.py:787
  79.7 26.0 %collective-permute-start.8 = (bf16[256,1536]{1,0:T(8,128)(2,1)S(1)}, bf16[256,1536]{1,0:T(8,128)(2,1)S(1)}, u32[]{:S(2)}, u32[]{:S(2)}) collective-permute-start(bf16[256,1536]{1,0:T(8,128)(2,1)S(1)} %copy-done.21), channel_id=1, source_target_pairs={{0,2},{1,66},{2,0},{3,64},{64,3},{65,67},{66,1},{67,65},{4,6},{5,7... | collective-permute-start | bytes 2359304 | tf_op jit(solution)/shard_map/ppermute | solution.py:787
  104.6 6.1 %copy-start.12 = (bf16[1024,768]{1,0:T(8,128)(2,1)}, bf16[1024,768]{1,0:T(8,128)(2,1)S(1)}, u32[]{:S(2)}) copy-start(bf16[1024,768]{1,0:T(8,128)(2,1)S(1)} %get-tuple-element.122.kept_ref) | copy-start | bytes 4718596
  123.3 4.2 %collective-permute-start.13 = (f32[8,1024]{1,0:T(8,128)S(1)}, f32[8,1024]{1,0:T(8,128)S(1)}, u32[]{:S(2)}, u32[]{:S(2)}) collective-permute-start(f32[8,1024]{1,0:T(8,128)S(1)} %get-tuple-element.109.s0), channel_id=1, source_target_pairs={{0,66},{1,67},{2,64},{3,65},{64,2},{65,3},{66,0},{67,1},{4,70},{5,... | collective-permute-start | bytes 98312 | tf_op jit(solution)/shard_map/ppermute | solution.py:787
  126.3 4.3 %collective-permute-start.12 = (f32[8,1024]{1,0:T(8,128)S(1)}, f32[8,1024]{1,0:T(8,128)S(1)}, u32[]{:S(2)}, u32[]{:S(2)}) collective-permute-start(f32[8,1024]{1,0:T(8,128)S(1)} %get-tuple-element.109.s0), channel_id=1, source_target_pairs={{0,64},{1,65},{2,66},{3,67},{64,0},{65,1},{66,2},{67,3},{4,68},{5,... | collective-permute-start | bytes 98312 | tf_op jit(solution)/shard_map/ppermute | solution.py:787
  126.3 4.3 %collective-permute-start.11 = (f32[8,1024]{1,0:T(8,128)S(1)}, f32[8,1024]{1,0:T(8,128)S(1)}, u32[]{:S(2)}, u32[]{:S(2)}) collective-permute-start(f32[8,1024]{1,0:T(8,128)S(1)} %get-tuple-element.109.s0), channel_id=1, source_target_pairs={{0,2},{1,3},{2,0},{3,1},{64,66},{65,67},{66,64},{67,65},{4,6},{5,7... | collective-permute-start | bytes 98312 | tf_op jit(solution)/shard_map/ppermute | solution.py:787
  144.8 1.2 copy-start.11
  145.9 9.8 %collective-permute-start.14 = (bf16[16,2,48,768]{3,2,1,0:T(8,128)(2,1)}, bf16[16,2,48,768]{3,2,1,0:T(8,128)(2,1)S(1)}, u32[]{:S(2)}, u32[]{:S(2)}) collective-permute-start(bf16[16,2,48,768]{3,2,1,0:T(8,128)(2,1)} %get-tuple-element.115), channel_id=1, source_target_pairs={{0,1},{1,0},{2,3},{3,2},{4,5},{5,4},{6,7},{7,6},{8,9},{9,8},{10,11... | collective-permute-start | bytes 7077896 | tf_op jit(solution)/shard_map/ppermute | solution.py:797
  148.4 7.4 %copy-start.14 = (bf16[16,2,48,768]{3,2,1,0:T(8,128)(2,1)S(1)}, bf16[16,2,48,768]{3,2,1,0:T(8,128)(2,1)}, u32[]{:S(2)}) copy-start(bf16[16,2,48,768]{3,2,1,0:T(8,128)(2,1)} %get-tuple-element.114) | copy-start | bytes 7077892
  158.0 11.1 %copy-start.25 = (bf16[256,1536]{1,0:T(8,128)(2,1)S(1)}, bf16[256,1536]{1,0:T(8,128)(2,1)}, u32[]{:S(2)}) copy-start(bf16[256,1536]{1,0:T(8,128)(2,1)} %get-tuple-element.132) | copy-start | bytes 2359300
  158.0 72.9 %all-to-all-start.1 = ((bf16[16,2,48,768]{3,2,1,0:T(8,128)(2,1)}), bf16[16,2,48,768]{3,2,1,0:T(8,128)(2,1)}, u32[]{:S(2)}, u32[]{:S(2)}) async-start(bf16[16,2,48,768]{3,2,1,0:T(8,128)(2,1)} %add_convert_fusion), calls=%async_computation.1 | async-start | bytes 4718592 | tf_op jit(solution)/shard_map/all_to_all | solution.py:827
  165.0 49.3 %collective-permute-start.15 = (bf16[256,1536]{1,0:T(8,128)(2,1)}, bf16[256,1536]{1,0:T(8,128)(2,1)S(1)}, u32[]{:S(2)}, u32[]{:S(2)}) collective-permute-start(bf16[256,1536]{1,0:T(8,128)(2,1)} %get-tuple-element.129), channel_id=1, source_target_pairs={{0,0},{1,64},{2,2},{3,66},{64,1},{65,65},{66,3},{67,67},{4,4},{5,6... | collective-permute-start | bytes 2359304 | tf_op jit(solution)/shard_map/ppermute | solution.py:787
  168.9 45.4 %collective-permute-start.16 = (bf16[256,1536]{1,0:T(8,128)(2,1)S(1)}, bf16[256,1536]{1,0:T(8,128)(2,1)S(1)}, u32[]{:S(2)}, u32[]{:S(2)}) collective-permute-start(bf16[256,1536]{1,0:T(8,128)(2,1)S(1)} %get-tuple-element.130), channel_id=1, source_target_pairs={{0,2},{1,66},{2,0},{3,64},{64,3},{65,67},{66,1},{67,65},{4,6},{5,7... | collective-permute-start | bytes 2359304 | tf_op jit(solution)/shard_map/ppermute | solution.py:787
  169.0 46.2 %collective-permute-start.17 = (bf16[256,1536]{1,0:T(8,128)(2,1)}, bf16[256,1536]{1,0:T(8,128)(2,1)S(1)}, u32[]{:S(2)}, u32[]{:S(2)}) collective-permute-start(bf16[256,1536]{1,0:T(8,128)(2,1)} %get-tuple-element.131), channel_id=1, source_target_pairs={{0,1},{1,65},{2,3},{3,67},{64,0},{65,64},{66,2},{67,66},{4,5},{5,6... | collective-permute-start | bytes 2359304 | tf_op jit(solution)/shard_map/ppermute | solution.py:787
  169.1 46.1 %collective-permute-start.18 = (bf16[256,1536]{1,0:T(8,128)(2,1)S(1)}, bf16[256,1536]{1,0:T(8,128)(2,1)S(1)}, u32[]{:S(2)}, u32[]{:S(2)}) collective-permute-start(bf16[256,1536]{1,0:T(8,128)(2,1)S(1)} %copy-done.25), channel_id=1, source_target_pairs={{0,3},{1,67},{2,1},{3,65},{64,2},{65,66},{66,0},{67,64},{4,7},{5,7... | collective-permute-start | bytes 2359304 | tf_op jit(solution)/shard_map/ppermute | solution.py:787
  213.4 0.9 copy-start.2
  214.3 0.9 copy-start
  215.2 10.3 %copy-start.22 = (bf16[256,1536]{1,0:T(8,128)(2,1)}, bf16[256,1536]{1,0:T(8,128)(2,1)S(1)}, u32[]{:S(2)}) copy-start(bf16[256,1536]{1,0:T(8,128)(2,1)S(1)} %collective-permute-done.17.b2) | copy-start | bytes 2359300
  215.2 10.3 %copy-start.23 = (bf16[256,1536]{1,0:T(8,128)(2,1)}, bf16[256,1536]{1,0:T(8,128)(2,1)S(1)}, u32[]{:S(2)}) copy-start(bf16[256,1536]{1,0:T(8,128)(2,1)S(1)} %collective-permute-done.18.b3) | copy-start | bytes 2359300
  215.2 14.8 %collective-permute-start.19 = (bf16[256,1536]{1,0:T(8,128)(2,1)S(1)}, bf16[256,1536]{1,0:T(8,128)(2,1)S(1)}, u32[]{:S(2)}, u32[]{:S(2)}) collective-permute-start(bf16[256,1536]{1,0:T(8,128)(2,1)S(1)} %get-tuple-element.141), channel_id=1, source_target_pairs={{0,0},{1,64},{2,2},{3,66},{64,1},{65,65},{66,3},{67,67},{4,4},{5,6... | collective-permute-start | bytes 2359304 | tf_op jit(solution)/shard_map/ppermute | solution.py:787
  230.0 0.9 copy-start.4
  230.9 4.0 %copy-start.13 = (f32[768,1152]{1,0:T(8,128)S(1)}, f32[768,1152]{1,0:T(8,128)}, u32[]{:S(2)}) copy-start(f32[768,1152]{1,0:T(8,128)} %get-tuple-element.138) | copy-start | bytes 10616836
  230.9 3.7 %collective-permute-start.20 = (bf16[784,1152]{1,0:T(8,128)(2,1)S(1)}, bf16[784,1152]{1,0:T(8,128)(2,1)S(1)}, u32[]{:S(2)}, u32[]{:S(2)}) collective-permute-start(bf16[784,1152]{1,0:T(8,128)(2,1)S(1)} %get-tuple-element.142), channel_id=1, source_target_pairs={{0,1},{1,0},{2,3},{3,2},{4,5},{5,4},{6,7},{7,6},{8,9},{9,8},{10,11... | collective-permute-start | bytes 5419016 | tf_op jit(solution)/shard_map/ppermute | solution.py:797
  235.5 8.5 %copy-start.3 = (bf16[256,1536]{1,0:T(8,128)(2,1)S(1)}, bf16[256,1536]{1,0:T(8,128)(2,1)}, u32[]{:S(2)}) copy-start(bf16[256,1536]{1,0:T(8,128)(2,1)} %copy-done.2) | copy-start | bytes 2359300
  235.5 9.8 %copy-start.24 = (bf16[256,1536]{1,0:T(8,128)(2,1)S(1)}, bf16[256,1536]{1,0:T(8,128)(2,1)}, u32[]{:S(2)}) copy-start(bf16[256,1536]{1,0:T(8,128)(2,1)} %get-tuple-element.146) | copy-start | bytes 2359300
  235.5 11.7 %copy-start.1 = (bf16[256,1536]{1,0:T(8,128)(2,1)S(1)}, bf16[256,1536]{1,0:T(8,128)(2,1)}, u32[]{:S(2)}) copy-start(bf16[256,1536]{1,0:T(8,128)(2,1)} %copy-done) | copy-start | bytes 2359300
  237.0 42.9 %all-to-all-start.2 = ((bf16[16,56,1152]{2,1,0:T(8,128)(2,1)}), bf16[16,56,1152]{2,1,0:T(8,128)(2,1)}, u32[]{:S(2)}, u32[]{:S(2)}) async-start(bf16[16,56,1152]{2,1,0:T(8,128)(2,1)} %pad_maximum_fusion), calls=%async_computation.2 | async-start | bytes 4128768 | tf_op jit(solution)/shard_map/all_to_all | solution.py:827
  244.0 31.7 %copy-start.5 = (bf16[256,1536]{1,0:T(8,128)(2,1)S(1)}, bf16[256,1536]{1,0:T(8,128)(2,1)}, u32[]{:S(2)}) copy-start(bf16[256,1536]{1,0:T(8,128)(2,1)} %copy-done.4) | copy-start | bytes 2359300
  244.0 20.5 %collective-permute-start.21 = (bf16[256,1536]{1,0:T(8,128)(2,1)S(1)}, bf16[256,1536]{1,0:T(8,128)(2,1)S(1)}, u32[]{:S(2)}, u32[]{:S(2)}) collective-permute-start(bf16[256,1536]{1,0:T(8,128)(2,1)S(1)} %copy-done.3), channel_id=1, source_target_pairs={{0,2},{1,66},{2,0},{3,64},{64,3},{65,67},{66,1},{67,65},{4,6},{5,7... | collective-permute-start | bytes 2359304 | tf_op jit(solution)/shard_map/ppermute | solution.py:787
  244.7 19.9 %collective-permute-start.22 = (bf16[256,1536]{1,0:T(8,128)(2,1)}, bf16[256,1536]{1,0:T(8,128)(2,1)S(1)}, u32[]{:S(2)}, u32[]{:S(2)}) collective-permute-start(bf16[256,1536]{1,0:T(8,128)(2,1)} %get-tuple-element.145), channel_id=1, source_target_pairs={{0,1},{1,65},{2,3},{3,67},{64,0},{65,64},{66,2},{67,66},{4,5},{5,6... | collective-permute-start | bytes 2359304 | tf_op jit(solution)/shard_map/ppermute | solution.py:787
  245.3 29.4 %collective-permute-start.23 = (bf16[256,1536]{1,0:T(8,128)(2,1)S(1)}, bf16[256,1536]{1,0:T(8,128)(2,1)S(1)}, u32[]{:S(2)}, u32[]{:S(2)}) collective-permute-start(bf16[256,1536]{1,0:T(8,128)(2,1)S(1)} %copy-done.24), channel_id=1, source_target_pairs={{0,3},{1,67},{2,1},{3,65},{64,2},{65,66},{66,0},{67,64},{4,7},{5,7... | collective-permute-start | bytes 2359304 | tf_op jit(solution)/shard_map/ppermute | solution.py:787
  252.2 27.6 %collective-permute-start.24 = (f32[2,48,768]{2,1,0:T(8,128)S(1)}, f32[2,48,768]{2,1,0:T(8,128)S(1)}, u32[]{:S(2)}, u32[]{:S(2)}) collective-permute-start(f32[2,48,768]{2,1,0:T(8,128)S(1)} %convert_reduce_fusion), channel_id=1, source_target_pairs={{0,0},{1,64},{2,2},{3,66},{64,1},{65,65},{66,3},{67,67},{4,4},{5,6... | collective-permute-start | bytes 884744 | tf_op jit(solution)/shard_map/ppermute | solution.py:787
  264.6 10.2 %copy-start.26 = (bf16[256,1536]{1,0:T(8,128)(2,1)}, bf16[256,1536]{1,0:T(8,128)(2,1)S(1)}, u32[]{:S(2)}) copy-start(bf16[256,1536]{1,0:T(8,128)(2,1)S(1)} %collective-permute-done.22.b2) | copy-start | bytes 2359300
  274.8 0.9 copy-start.27
  281.7 13.4 %collective-permute-start.29 = (f32[62,256]{1,0:T(8,128)S(1)}, f32[62,256]{1,0:T(8,128)S(1)}, u32[]{:S(2)}, u32[]{:S(2)}) collective-permute-start(f32[62,256]{1,0:T(8,128)S(1)} %get-tuple-element.156), channel_id=1, source_target_pairs={{0,3},{1,67},{2,1},{3,65},{64,2},{65,66},{66,0},{67,64},{4,7},{5,7... | collective-permute-start | bytes 190472 | tf_op jit(solution)/shard_map/ppermute | solution.py:787
  283.8 11.3 %collective-permute-start.28 = (f32[62,256]{1,0:T(8,128)S(1)}, f32[62,256]{1,0:T(8,128)S(1)}, u32[]{:S(2)}, u32[]{:S(2)}) collective-permute-start(f32[62,256]{1,0:T(8,128)S(1)} %get-tuple-element.156), channel_id=1, source_target_pairs={{0,1},{1,65},{2,3},{3,67},{64,0},{65,64},{66,2},{67,66},{4,5},{5,6... | collective-permute-start | bytes 190472 | tf_op jit(solution)/shard_map/ppermute | solution.py:787
  284.8 10.3 %collective-permute-start.27 = (f32[62,256]{1,0:T(8,128)S(1)}, f32[62,256]{1,0:T(8,128)S(1)}, u32[]{:S(2)}, u32[]{:S(2)}) collective-permute-start(f32[62,256]{1,0:T(8,128)S(1)} %get-tuple-element.156), channel_id=1, source_target_pairs={{0,2},{1,66},{2,0},{3,64},{64,3},{65,67},{66,1},{67,65},{4,6},{5,7... | collective-permute-start | bytes 190472 | tf_op jit(solution)/shard_map/ppermute | solution.py:787
  287.3 7.8 %collective-permute-start.26 = (f32[62,256]{1,0:T(8,128)S(1)}, f32[62,256]{1,0:T(8,128)S(1)}, u32[]{:S(2)}, u32[]{:S(2)}) collective-permute-start(f32[62,256]{1,0:T(8,128)S(1)} %get-tuple-element.156), channel_id=1, source_target_pairs={{0,0},{1,64},{2,2},{3,66},{64,1},{65,65},{66,3},{67,67},{4,4},{5,6... | collective-permute-start | bytes 190472 | tf_op jit(solution)/shard_map/ppermute | solution.py:787
  289.6 8.5 %collective-permute-start.25 = (f32[56,896]{1,0:T(8,128)S(1)}, f32[56,896]{1,0:T(8,128)S(1)}, u32[]{:S(2)}, u32[]{:S(2)}) collective-permute-start(f32[56,896]{1,0:T(8,128)S(1)} %get-tuple-element.155), channel_id=1, source_target_pairs={{0,0},{1,64},{2,2},{3,66},{64,1},{65,65},{66,3},{67,67},{4,4},{5,6... | collective-permute-start | bytes 602120 | tf_op jit(solution)/shard_map/ppermute | solution.py:787
where the time goes:
time: 300 us; the launch traced here: 299 us
  Pallas kernels  126 us (42%)
  starting transfers between devices  79.3 us (26%)
  waiting for transfers between devices  73.2 us (24%)
  local copies, waits for them, and re-layouts  12.1 us (4%)
  other arithmetic  6.73 us (2%)
    ppermute x26, waiting for transfers between devices, permute(): return lax.ppermute(value, GROUP, moves(rule))  65.6 us
    ppermute x26, starting transfers between devices, permute(): return lax.ppermute(value, GROUP, moves(rule))  54.2 us
    pallas_call x1, Pallas kernels, mixer_backward(): pl.pallas_call(backward_kernel, grid=(steps,), in_specs=[pl.BlockSpec((SP...  27.3 us
    pallas_call x1, Pallas kernels, gate_back(): pl.pallas_call(functools.partial(gate_back_kernel, width_all), grid=(inne...  14.2 us
    all_to_all x2, starting transfers between devices, exchange(): return lax.all_to_all(blocks, PLANE, 0, 0, tiled=True)  14 us
    pallas_call x1, Pallas kernels, project_back(): pl.pallas_call(project_back_kernel, grid=(4,), in_specs=[pl.BlockSpec(mem...  14 us
    pallas_call x1, Pallas kernels, mixer_forward(): pl.pallas_call(forward_kernel, grid=(steps,), in_specs=[pl.BlockSpec((SPA...  13 us
    pallas_call x1, Pallas kernels, gate_sums(): pl.pallas_call(gate_sums_kernel, grid=(steps,), in_specs=[whole(tokens.sh...  12.6 us
  transfers between devices with their start and end apart: 33, of which 13 were waited for; matrix products, arithmetic and copies ran while one was open for 1% of the time, Pallas kernels for 31%

commit v1 on v0

--- a/solution.py
+++ b/solution.py
@@ -16,6 +16,18 @@
 F32 = jnp.float32
 HI = lax.Precision.HIGHEST
 SPAN = 128
+LIMIT = 36
+
+
+def near(value):
+    return pltpu.with_memory_space_constraint(value, pltpu.VMEM)
+
+
+def far(value):
+    return pltpu.with_memory_space_constraint(value, pltpu.HBM)
+
+
+ROWS = 512
 SCALE = 1.15e9
 
 
@@ -262,9 +274,17 @@
     return jax.ShapeDtypeStruct(shape, dtype)
 
 
+def stored(shape, dtype):
+    return pltpu.HBM(shape, dtype)
+
+
+def held_near(shape, dtype):
+    return pltpu.VMEM(shape, dtype)
+
+
 def params(limit, *semantics):
     return pltpu.CompilerParams(
-        dimension_semantics=semantics or None, vmem_limit_bytes=52 * 1024 * 1024
+        dimension_semantics=semantics or None, vmem_limit_bytes=LIMIT * 1024 * 1024
     )
 
 
@@ -300,11 +320,14 @@
         functools.partial(place_kernel, normalise),
         in_specs=[pl.BlockSpec(memory_space=pltpu.SMEM)] + [vmem] * 5,
         out_specs=[vmem, vmem],
-        out_shape=[shape_of((4 * rows, width), BF), shape_of((width, 4 * rows), BF)],
+        out_shape=[
+            (stored if normalise else shape_of)((4 * rows, width), BF),
+            shape_of((width, 4 * rows), BF),
+        ],
         compiler_params=params(24),
         cost_estimate=lasting(6),
         name="place_normed" if normalise else "place_cotangent",
-    )(meta, gain, *blocks)
+    )(meta, gain, *[far(block) for block in blocks])
 
 
 def project_kernel(tokens_ref, mine_ref, other_ref, out_ref):
@@ -317,18 +340,19 @@
 def project(tokens, mine, other, inner):
     half = mine.shape[0]
     length = tokens.shape[0]
-    tile = 384
     columns = mine.shape[1] - 2 * inner
+    rows = ROWS
+    part = pl.BlockSpec((pl.Element(half), pl.Element(columns)), lambda i: (0, 2 * inner))
     return pl.pallas_call(
         project_kernel,
-        grid=(columns // tile,),
-        in_specs=[whole(tokens.shape)] + [column(half, tile, 2 * inner // tile)] * 2,
-        out_specs=column(length, tile),
+        grid=(length // rows,),
+        in_specs=[pl.BlockSpec((rows, 2 * half), lambda i: (i, 0)), part, part],
+        out_specs=pl.BlockSpec((rows, columns), lambda i: (i, 0)),
         out_shape=shape_of((length, columns), F32),
         compiler_params=params(20, "arbitrary"),
         cost_estimate=lasting(6),
         name="project_in",
-    )(tokens, mine, other)
+    )(far(tokens), far(mine), far(other))
 
 
 def gate_sums_kernel(
@@ -384,7 +408,7 @@
         compiler_params=params(36, "arbitrary"),
         cost_estimate=lasting(9),
         name="gate_sums",
-    )(tokens, cot, mine, other, mine, other, y, gain)
+    )(near(tokens), near(cot), far(mine), far(other), far(mine), far(other), near(y), gain)
 
 
 def gate_back_kernel(
@@ -432,9 +456,9 @@
         + [column(1, tile), whole(tokens_t.shape), whole(cot_t.shape)],
         out_specs=[column(length, tile)] * 3 + [column(8, tile), pile, pile],
         out_shape=[
-            shape_of((length, inner), BF),
-            shape_of((length, inner), BF),
-            shape_of((length, inner), F32),
+            stored((length, inner), BF),
+            stored((length, inner), BF),
+            stored((length, inner), F32),
             shape_of((8, inner), F32),
             shape_of((half // block, 2, block, inner), BF),
             shape_of((half // block, 2, block, inner), BF),
@@ -442,7 +466,7 @@
         compiler_params=params(44, "arbitrary"),
         cost_estimate=lasting(12),
         name="gate_back",
-    )(*sums, z, dy, y, gain, tokens_t, cot_t)
+    )(*sums, near(z), near(dy), near(y), gain, near(tokens_t), near(cot_t))
 
 
 def scatter_rows(meta_ref, found, scratch, outs):
@@ -463,10 +487,16 @@
     pl.when(jnp.logical_not(first))(lambda: step(oo_ref))
 
 
-def sides(tile, columns, shift):
+def sides(tile, columns, shift, per):
     return [
-        pl.BlockSpec((pl.Element(tile), pl.Element(columns)), lambda j: (jnp.minimum(j, 1) * tile, shift)),
-        pl.BlockSpec((pl.Element(tile), pl.Element(columns)), lambda j: (jnp.maximum(j - 2, 0) * tile, shift)),
+        pl.BlockSpec(
+            (pl.Element(tile), pl.Element(columns)),
+            lambda j: (jnp.minimum(j, per - 1) * tile, shift),
+        ),
+        pl.BlockSpec(
+            (pl.Element(tile), pl.Element(columns)),
+            lambda j: (jnp.maximum(j - per, 0) * tile, shift),
+        ),
     ]
 
 
@@ -474,19 +504,20 @@
     length, inner = normed_y.shape
     half = mine.shape[0]
     rows = length // 4
-    tile = half // 2
+    per = 3
+    tile = half // per
     return pl.pallas_call(
         project_out_kernel,
-        grid=(4,),
+        grid=(2 * per,),
         in_specs=[pl.BlockSpec(memory_space=pltpu.SMEM), whole(normed_y.shape)]
-        + sides(tile, inner, inner),
+        + sides(tile, inner, inner, per),
         out_specs=[column(rows, tile)] * 4,
-        out_shape=[shape_of((rows, 2 * half), BF)] * 4,
+        out_shape=[stored((rows, 2 * half), BF)] * 4,
         scratch_shapes=[pltpu.VMEM((length, tile), F32)],
         compiler_params=params(24, "arbitrary"),
         cost_estimate=lasting(6),
         name="project_out",
-    )(meta, normed_y, mine, other)
+    )(meta, far(normed_y), far(mine), far(other))
 
 
 def project_back_kernel(
@@ -495,14 +526,15 @@
     outs, grad_ref, scratch = refs[:4], refs[4], refs[5]
     tile = scratch.shape[1]
     j = pl.program_id(0)
-    side, within = j // 2, j % 2
+    per = pl.num_programs(0) // 2
+    side, within = j // per, j % per
     core = meta_ref[4]
 
     def step(x_ref, z_ref):
         found = nt(late_ref[...], x_ref[...]) + nt(gate_ref[...], z_ref[...])
         total = jnp.sum(found * tokens_ref[...].astype(F32), axis=0, keepdims=True)
         owner = side + core - 2 * side * core
-        place = pl.ds(pl.multiple_of((2 * owner + within) * tile, 128), tile)
+        place = pl.ds(pl.multiple_of((per * owner + within) * tile, 128), tile)
         grad_ref[:, place] = jnp.broadcast_to(total / gain_ref[:, place], (8, tile))
         scatter_rows(meta_ref, found, scratch, outs)
 
@@ -515,21 +547,24 @@
     inner = gate.shape[1]
     half = mine1.shape[0]
     rows = length // 4
-    tile = half // 2
+    per = 3
+    tile = half // per
     return pl.pallas_call(
         project_back_kernel,
-        grid=(4,),
+        grid=(2 * per,),
         in_specs=[pl.BlockSpec(memory_space=pltpu.SMEM), whole(late.shape), whole(gate.shape)]
-        + sides(tile, columns, 2 * inner)
-        + sides(tile, inner, 0)
+        + sides(tile, columns, 2 * inner, per)
+        + sides(tile, inner, 0, per)
         + [column(length, tile), whole(gain.shape)],
         out_specs=[column(rows, tile)] * 4 + [whole((8, 2 * half))],
-        out_shape=[shape_of((rows, 2 * half), BF)] * 4 + [shape_of((8, 2 * half), F32)],
+        out_shape=[stored((rows, 2 * half), BF)] * 4 + [shape_of((8, 2 * half), F32)],
         scratch_shapes=[pltpu.VMEM((length, tile), F32)],
         compiler_params=params(32, "arbitrary"),
         cost_estimate=lasting(0.5),
         name="project_back",
-    )(meta, late, gate, mine1, other1, mine2, other2, tokens, gain)
+    )(
+        meta, near(late), far(gate), far(mine1), far(other1), far(mine2), far(other2), far(tokens), gain
+    )
 
 
 def weight_grad_kernel(tokens_t_ref, late_ref, vector_ref, keep_ref, send_ref):
@@ -550,11 +585,11 @@
         grid=(columns // tile,),
         in_specs=[whole(tokens_t.shape), column(length, tile), column(vector.shape[0], tile)],
         out_specs=[column(half, tile), column(rows, tile)],
-        out_shape=[shape_of((half, columns), F32), shape_of((rows, columns), BF)],
+        out_shape=[stored((half, columns), F32), stored((rows, columns), BF)],
         compiler_params=params(24, "arbitrary"),
         cost_estimate=lasting(0.5),
         name="weight_grad",
-    )(tokens_t, late, vector)
+    )(far(tokens_t), near(late), vector)
 
 
 def pack_kernel(z_ref, out_ref, x_ref, bc_ref, dt_ref, packed_ref):
@@ -579,7 +614,7 @@
         compiler_params=params(8),
         cost_estimate=lasting(1),
         name="pack_weights",
-    )(*parts)
+    )(*[far(part) for part in parts])
 
 
 def total_kernel(states, got_ref, own_ref, shared_ref):
@@ -673,7 +708,7 @@
         compiler_params=params(16),
         cost_estimate=lasting(3),
         name="finish_output",
-    )(meta, *blocks, hidden)
+    )(meta, *[far(block) for block in blocks], far(hidden))
 
 
 def input_kernel(meta_ref, b0, b1, b2, b3, hidden_ref, cot_ref, gain_ref, out_ref):
@@ -694,7 +729,7 @@
         compiler_params=params(16),
         cost_estimate=lasting(3),
         name="finish_input",
-    )(meta, *blocks, hidden, cot, gain)
+    )(meta, *blocks, far(hidden), far(cot), gain)
 
 
 def mixer_tables(conv_x, conv_bc, head_params):
@@ -728,14 +763,14 @@
         ],
         out_shape=[
             shape_of((length, inner), F32),
-            shape_of((steps * 128, inner), BF),
-            shape_of((length, both), F32),
+            stored((steps * 128, inner), BF),
+            stored((length, both), F32),
         ],
         scratch_shapes=[pltpu.VMEM((SPAN + 8, both), F32), pltpu.VMEM((128, inner), F32)],
         compiler_params=params(20, "arbitrary"),
         cost_estimate=lasting(13),
         name="mixer_forward",
-    )(pre, taps, head, skip, spread)
+    )(near(pre), taps, head, skip, spread)
 
 
 def mixer_backward(pre, conv, dy, kept, taps, head, skip, spread):
@@ -760,7 +795,7 @@
             whole((8, 128)),
         ],
         out_shape=[
-            shape_of((length, columns), BF),
+            held_near((length, columns), BF),
             shape_of((8, both), F32),
             shape_of((8, 128), F32),
         ],
@@ -772,7 +807,7 @@
         compiler_params=params(24, "arbitrary"),
         cost_estimate=lasting(30),
         name="mixer_backward",
-    )(pre, conv, dy, kept, taps, head, skip, spread)
+    )(far(pre), far(conv), far(dy), far(kept), taps, head, skip, spread)
 
 
 CELLS = [(xh, xl, core) for xh in range(2) for xl in range(2) for core in range(2)]

time: 300 us -> 282 us (0.940)
  Pallas kernels: 126 us -> 111 us
  waiting for transfers between devices: 73.2 us -> 69.1 us
  other arithmetic: 6.73 us -> 9.92 us
  local copies, waits for them, and re-layouts: 12.1 us -> 8.94 us
    unnamed x56 -> x48, local copies, waits for them, and re-layouts: 8.85 us -> 0.98 us
    pallas_call x1, Pallas kernels: 14.2 us -> 10 us  [gate_back(): pl.pallas_call(functools.partial(gate_back_kernel, width_all), grid=(inne...]
    pallas_call x3, Pallas kernels: 30.3 us -> 26.4 us  [the longest x1 11.8 us: project_back(): pl.pallas_call(project_back_kernel, grid=(2 * per,), in_specs=[pl.BlockSp...]
    pallas_call x1, Pallas kernels: 12.6 us -> 9.62 us  [gate_sums(): pl.pallas_call(gate_sums_kernel, grid=(steps,), in_specs=[whole(tokens.sh...]
  transfers between devices with their start and end apart: 33 -> 33, of which waited for: 13 -> 13; matrix products, arithmetic and copies ran while one was open for 1% -> 4% of each run, Pallas kernels for 31% -> 31%
where the time goes in v1:
time: 282 us; the launch traced here: 280 us
  Pallas kernels  111 us (39%)
  starting transfers between devices  80.1 us (28%)
  waiting for transfers between devices  69.1 us (25%)
  other arithmetic  9.92 us (4%)
  local copies, waits for them, and re-layouts  8.94 us (3%)
    ppermute x26, waiting for transfers between devices, permute(): return lax.ppermute(value, GROUP, moves(rule))  63.9 us
    ppermute x26, starting transfers between devices, permute(): return lax.ppermute(value, GROUP, moves(rule))  53.6 us
    pallas_call x1, Pallas kernels, mixer_backward(): pl.pallas_call(backward_kernel, grid=(steps,), in_specs=[pl.BlockSpec((SP...  26.8 us
    all_to_all x2, starting transfers between devices, exchange(): return lax.all_to_all(blocks, PLANE, 0, 0, tiled=True)  13.9 us
    pallas_call x1, Pallas kernels, mixer_forward(): pl.pallas_call(forward_kernel, grid=(steps,), in_specs=[pl.BlockSpec((SPA...  11.8 us
    pallas_call x1, Pallas kernels, project_back(): pl.pallas_call(project_back_kernel, grid=(2 * per,), in_specs=[pl.BlockSp...  11.8 us
    pallas_call x1, Pallas kernels, gate_back(): pl.pallas_call(functools.partial(gate_back_kernel, width_all), grid=(inne...  10 us
    pallas_call x1, Pallas kernels, gate_sums(): pl.pallas_call(gate_sums_kernel, grid=(steps,), in_specs=[whole(tokens.sh...  9.62 us
  transfers between devices with their start and end apart: 33, of which 13 were waited for; matrix products, arithmetic and copies ran while one was open for 4% of the time, Pallas kernels for 31%

profile of v1, /device:TPU:1, one launch (start us, length us, event | category | flops | bytes accessed | tf_op | source)
XLA Modules:
  0.0 280.1 jit_solution(639722736659874966)
XLA Ops:
  0.7 1.1 pack_weights.1
  1.8 6.0 %collective-permute-start = (bf16[48,2688]{1,0:T(8,128)(2,1)S(1)}, bf16[48,2688]{1,0:T(8,128)(2,1)S(1)}, u32[]{:S(2)}, u32[]{:S(2)}) collective-permute-start(bf16[48,2688]{1,0:T(8,128)(2,1)S(1)} %pack_weights.1), channel_id=1, source_target_pairs={{0,0},{1,64},{2,2},{3,66},{64,1},{65,65},{66,3},{67,67},{4,4},{5,6... | collective-permute-start | bytes 774152 | tf_op jit(solution)/shard_map/ppermute | solution.py:822
  7.9 3.9 %collective-permute-done = bf16[48,2688]{1,0:T(8,128)(2,1)S(1)} collective-permute-done((bf16[48,2688]{1,0:T(8,128)(2,1)S(1)}, bf16[48,2688]{1,0:T(8,128)(2,1)S(1)}, u32[]{:S(2)}, u32[]{:S(2)}) %collective-permute-start) | collective-permute-done | bytes 258080 | tf_op jit(solution)/shard_map/ppermute | solution.py:822
  11.8 2.2 broadcast_in_dim.23
  14.1 7.9 %all-to-all-start = ((bf16[16,48,2688]{2,1,0:T(8,128)(2,1)}), bf16[16,48,2688]{2,1,0:T(8,128)(2,1)}, u32[]{:S(2)}, u32[]{:S(2)}) async-start(bf16[16,48,2688]{2,1,0:T(8,128)(2,1)} %broadcast_in_dim.23), calls=%async_computation | async-start | bytes 8257536 | tf_op jit(solution)/shard_map/all_to_all | solution.py:857
  22.0 3.3 %collective-permute-start.2 = (bf16[256,1536]{1,0:T(8,128)(2,1)S(1)}, bf16[256,1536]{1,0:T(8,128)(2,1)S(1)}, u32[]{:S(2)}, u32[]{:S(2)}) collective-permute-start(bf16[256,1536]{1,0:T(8,128)(2,1)S(1)} %copy-done.16), channel_id=1, source_target_pairs={{0,2},{1,66},{2,0},{3,64},{64,3},{65,67},{66,1},{67,65},{4,6},{5,7... | collective-permute-start | bytes 2359304 | tf_op jit(solution)/shard_map/ppermute | solution.py:822
  25.4 2.2 collective-permute-start.1
  27.6 2.7 collective-permute-start.4
  30.3 0.7 collective-permute-start.3
  31.1 1.3 collective-permute-done.3
  33.0 24.2 %collective-permute-done.2.refs_1_ = bf16[256,1536]{1,0:T(8,128)(2,1)S(1)} collective-permute-done((bf16[256,1536]{1,0:T(8,128)(2,1)S(1)}, bf16[256,1536]{1,0:T(8,128)(2,1)S(1)}, u32[]{:S(2)}, u32[]{:S(2)}) %collective-permute-start.2) | collective-permute-done | bytes 786464 | tf_op jit(solution)/shard_map/ppermute | solution.py:822
  57.2 3.4 %collective-permute-start.6 = (bf16[256,1536]{1,0:T(8,128)(2,1)}, bf16[256,1536]{1,0:T(8,128)(2,1)}, u32[]{:S(2)}, u32[]{:S(2)}) collective-permute-start(bf16[256,1536]{1,0:T(8,128)(2,1)} %cot_ref.1), channel_id=1, source_target_pairs={{0,0},{1,64},{2,2},{3,66},{64,1},{65,65},{66,3},{67,67},{4,4},{5,6... | collective-permute-start | bytes 2359304 | tf_op jit(solution)/shard_map/ppermute | solution.py:822
  60.8 0.9 copy-done.23
  61.7 5.5 %place_normed.1 = (bf16[1024,1536]{1,0:T(8,128)(2,1)}, bf16[1536,1024]{1,0:T(8,128)(2,1)S(1)}) custom-call(s32[6]{0:T(128)S(1)} %stack.31.meta_ref, f32[1,1536]{1,0:T(1,128)S(1)} %broadcast_in_dim.10.gain_ref, bf16[256,1536]{1,0:T(8,128)(2,1)} %copy-done.22, bf16[256,1536]{1,0:T(8,128)(2,1)} %copy-done.21, bf16[256,1536]{1,0:T(8,128)(2,1)} %collective-permute-done.4.refs_2_, ...), custom_call_target="tpu_custom_call" | custom-call | flops 6899999744 | bytes 1024 | tf_op jit(solution)/shard_map/place_normed/pallas_call | solution.py:319
  67.2 5.2 %collective-permute-done.6.refs_0_ = bf16[256,1536]{1,0:T(8,128)(2,1)} collective-permute-done((bf16[256,1536]{1,0:T(8,128)(2,1)}, bf16[256,1536]{1,0:T(8,128)(2,1)}, u32[]{:S(2)}, u32[]{:S(2)}) %collective-permute-start.6) | collective-permute-done | bytes 786464 | tf_op jit(solution)/shard_map/ppermute | solution.py:822
  72.6 0.7 slice.56.gain_ref
  73.3 1.3 slice.52
  74.6 1.4 collective-permute-start.10
  76.1 2.7 collective-permute-start.9
  78.8 1.3 slice_bitcast_fusion.2
  80.8 1.4 broadcast_in_dim_reshape.3.skip_ref
  82.8 0.8 select_maximum_fusion.1.taps_ref
  83.6 6.9 %project_in.1.pre_ref = f32[1024,1152]{1,0:T(8,128)S(1)} custom-call(bf16[1024,1536]{1,0:T(8,128)(2,1)} %get-tuple-element.97.tokens_ref, bf16[768,2688]{1,0:T(8,128)(2,1)} %bitcast.8.mine_ref.zm_ref.om_ref.xm_ref, bf16[768,2688]{1,0:T(8,128)(2,1)} %collective-permute-done.7.other_ref.zo_ref.oo_ref.xo_ref), custom_call_target="tpu_custom_call" | custom-call | flops 6899999744 | bytes 1024 | tf_op jit(solution)/shard_map/project_in/pallas_call | solution.py:346
  90.6 11.8 %mixer_forward.1 = (f32[1024,768]{1,0:T(8,128)S(1)}, bf16[1024,768]{1,0:T(8,128)(2,1)}, f32[1024,1024]{1,0:T(8,128)}) custom-call(f32[1024,1152]{1,0:T(8,128)S(1)} %project_in.1.pre_ref, f32[8,1024]{1,0:T(8,128)S(1)} %select_maximum_fusion.1.taps_ref, f32[8,128]{1,0:T(8,128)S(1)} %select_maximum_fusion.4.head_ref, f32[1,768]{1,0:T(1,128)S(1)} %copy-done.4, ...), custom_call_target="tpu_custom_call" | custom-call | flops 14949999616 | bytes 1024 | tf_op jit(solution)/shard_map/mixer_forward/pallas_call | solution.py:752
  102.4 1.0 collective-permute-done.10.refs_3_
  103.4 1.6 collective-permute-done.8.refs_1_
  105.0 3.1 %place_cotangent.1 = (bf16[1024,1536]{1,0:T(8,128)(2,1)S(1)}, bf16[1536,1024]{1,0:T(8,128)(2,1)S(1)}) custom-call(s32[6]{0:T(128)S(1)} %copy-done.7, f32[1,1536]{1,0:T(1,128)S(1)} %broadcast_in_dim.10.gain_ref, bf16[256,1536]{1,0:T(8,128)(2,1)} %collective-permute-done.6.refs_0_, bf16[256,1536]{1,0:T(8,128)(2,1)} %collective-permute-done.8.refs_1_, ...), custom_call_target="tpu_custom_call" | custom-call | flops 6899999744 | bytes 1024 | tf_op jit(solution)/shard_map/place_cotangent/pallas_call | solution.py:319
  108.1 9.6 %gate_sums.1 = (f32[1024,768]{1,0:T(8,128)S(1)}, f32[1024,768]{1,0:T(8,128)S(1)}, f32[8,1024]{1,0:T(8,128)S(1)}) custom-call(bf16[1024,1536]{1,0:T(8,128)(2,1)S(1)} %copy-done.1, bf16[1024,1536]{1,0:T(8,128)(2,1)S(1)} %get-tuple-element.107.cot_ref, bf16[768,2688]{1,0:T(8,128)(2,1)} %bitcast.8.mine_ref.zm_ref.om_ref.xm_ref, ...), custom_call_target="tpu_custom_call" | custom-call | flops 10350000128 | bytes 1024 | tf_op jit(solution)/shard_map/gate_sums/pallas_call | solution.py:389
  117.7 1.3 collective-permute-start.13
  119.3 1.8 collective-permute-start.11
  121.1 0.7 collective-permute-done.13.s3
  121.8 1.6 collective-permute-done.12.s2
  123.4 10.0 %gate_back.1 = (bf16[1024,768]{1,0:T(8,128)(2,1)}, bf16[1024,768]{1,0:T(8,128)(2,1)}, f32[1024,768]{1,0:T(8,128)}, f32[8,768]{1,0:T(8,128)S(1)}, bf16[16,2,48,76...) custom-call(f32[8,1024]{1,0:T(8,128)S(1)} %get-tuple-element.109.s0, f32[8,1024]{1,0:T(8,128)S(1)} %collective-permute-done.11.s1, ...), custom_call_target="tpu_custom_call" | custom-call | flops 13799999488 | bytes 1024 | tf_op jit(solution)/shard_map/gate_back/pallas_call | solution.py:451
  133.4 3.9 %collective-permute-start.14 = (bf16[16,2,48,768]{3,2,1,0:T(8,128)(2,1)}, bf16[16,2,48,768]{3,2,1,0:T(8,128)(2,1)S(1)}, u32[]{:S(2)}, u32[]{:S(2)}) collective-permute-start(bf16[16,2,48,768]{3,2,1,0:T(8,128)(2,1)} %get-tuple-element.115), channel_id=1, source_target_pairs={{0,1},{1,0},{2,3},{3,2},{4,5},{5,4},{6,7},{7,6},{8,9},{9,8},{10,11... | collective-permute-start | bytes 7077896 | tf_op jit(solution)/shard_map/ppermute | solution.py:832
  137.3 7.7 %project_out.1 = (bf16[256,1536]{1,0:T(8,128)(2,1)}, bf16[256,1536]{1,0:T(8,128)(2,1)}, bf16[256,1536]{1,0:T(8,128)(2,1)}, bf16[256,1536]{1,0:T(8,128)(2,1)}) custom-call(s32[6]{0:T(128)S(1)} %copy-done.7, bf16[1024,768]{1,0:T(8,128)(2,1)} %get-tuple-element.116.normed_ref, bf16[768,2688]{1,0:T(8,128)(2,1)} %bitcast.8.mine_ref.zm_ref.om_ref.xm_ref, ...), custom_call_target="tpu_custom_call" | custom-call | flops 6899999744 | bytes 1024 | tf_op jit(solution)/shard_map/project_out/pallas_call | solution.py:509
  145.0 2.1 add_convert_fusion
  147.1 7.1 %all-to-all-start.1 = ((bf16[16,2,48,768]{3,2,1,0:T(8,128)(2,1)}), bf16[16,2,48,768]{3,2,1,0:T(8,128)(2,1)}, u32[]{:S(2)}, u32[]{:S(2)}) async-start(bf16[16,2,48,768]{3,2,1,0:T(8,128)(2,1)} %add_convert_fusion), calls=%async_computation.1 | async-start | bytes 4718592 | tf_op jit(solution)/shard_map/all_to_all | solution.py:862
  154.2 3.8 %collective-permute-start.15 = (bf16[256,1536]{1,0:T(8,128)(2,1)}, bf16[256,1536]{1,0:T(8,128)(2,1)S(1)}, u32[]{:S(2)}, u32[]{:S(2)}) collective-permute-start(bf16[256,1536]{1,0:T(8,128)(2,1)} %get-tuple-element.129), channel_id=1, source_target_pairs={{0,0},{1,64},{2,2},{3,66},{64,1},{65,65},{66,3},{67,67},{4,4},{5,6... | collective-permute-start | bytes 2359304 | tf_op jit(solution)/shard_map/ppermute | solution.py:822
  158.5 2.7 collective-permute-start.18
  161.2 26.8 %mixer_backward.1 = (bf16[1024,1152]{1,0:T(8,128)(2,1)S(1)}, f32[8,1024]{1,0:T(8,128)S(1)}, f32[8,128]{1,0:T(8,128)S(1)}) custom-call(f32[1024,1152]{1,0:T(8,128)} %copy-done.10, f32[1024,1024]{1,0:T(8,128)} %get-tuple-element.100.conv_ref, f32[1024,768]{1,0:T(8,128)} %get-tuple-element.121.dy_ref, bf16[1024,768]{1,0:T(8,128)(2,1)} %get-tuple-element.122.kept_ref, ...), custom_call_target="tpu_custom_call" | custom-call | flops 34500001792 | bytes 1024 | tf_op jit(solution)/shard_map/mixer_backward/pallas_call | solution.py:782
  188.1 11.8 %project_back.1 = (bf16[256,1536]{1,0:T(8,128)(2,1)}, bf16[256,1536]{1,0:T(8,128)(2,1)}, bf16[256,1536]{1,0:T(8,128)(2,1)}, bf16[256,1536]{1,0:T(8,128)(2,1)}, f32[8,1536]{1,0:T(8,128)S(1)}) custom-call(s32[6]{0:T(128)S(1)} %copy-done.8, bf16[1024,1152]{1,0:T(8,128)(2,1)S(1)} %get-tuple-element.133.late_ref, bf16[1024,768]{1,0:T(8,128)(2,1)} %get-tuple-element.124.gate_ref, ...), custom_call_target="tpu_custom_call" | custom-call | flops 575000000 | bytes 1024 | tf_op jit(solution)/shard_map/project_back/pallas_call | solution.py:552
  199.9 2.3 collective-permute-start.19
  202.2 0.7 slice.60
  203.0 8.3 %weight_grad.1 = (f32[768,1152]{1,0:T(8,128)}, bf16[784,1152]{1,0:T(8,128)(2,1)}) custom-call(bf16[1536,1024]{1,0:T(8,128)(2,1)} %copy-done, bf16[1024,1152]{1,0:T(8,128)(2,1)S(1)} %get-tuple-element.133.late_ref, f32[16,1152]{1,0:T(8,128)S(1)} %pad.29.vector_ref), custom_call_target="tpu_custom_call" | custom-call | flops 575000000 | bytes 1024 | tf_op jit(solution)/shard_map/weight_grad/pallas_call | solution.py:583
  211.3 3.6 %collective-permute-done.19.b0 = bf16[256,1536]{1,0:T(8,128)(2,1)S(1)} collective-permute-done((bf16[256,1536]{1,0:T(8,128)(2,1)}, bf16[256,1536]{1,0:T(8,128)(2,1)S(1)}, u32[]{:S(2)}, u32[]{:S(2)}) %collective-permute-start.19) | collective-permute-done | bytes 786464 | tf_op jit(solution)/shard_map/ppermute | solution.py:822
  214.9 4.0 %collective-permute-done.20 = bf16[784,1152]{1,0:T(8,128)(2,1)S(1)} collective-permute-done((bf16[784,1152]{1,0:T(8,128)(2,1)}, bf16[784,1152]{1,0:T(8,128)(2,1)S(1)}, u32[]{:S(2)}, u32[]{:S(2)}) %collective-permute-start.20) | collective-permute-done | bytes 1806368 | tf_op jit(solution)/shard_map/ppermute | solution.py:832
  219.7 1.5 pad_maximum_fusion
  221.1 6.9 %all-to-all-start.2 = ((bf16[16,56,1152]{2,1,0:T(8,128)(2,1)}), bf16[16,56,1152]{2,1,0:T(8,128)(2,1)S(1)}, u32[]{:S(2)}, u32[]{:S(2)}) async-start(bf16[16,56,1152]{2,1,0:T(8,128)(2,1)} %pad_maximum_fusion), calls=%async_computation.2 | async-start | bytes 4128768 | tf_op jit(solution)/shard_map/all_to_all | solution.py:862
  228.0 0.9 collective-permute-start.21
  229.6 1.6 collective-permute-start.23
  231.2 3.5 %finish_output.1 = bf16[256,1536]{1,0:T(8,128)(2,1)} custom-call(s32[6]{0:T(128)S(1)} %copy-done.8, bf16[256,1536]{1,0:T(8,128)(2,1)} %copy-done.17, bf16[256,1536]{1,0:T(8,128)(2,1)} %copy-done.18, bf16[256,1536]{1,0:T(8,128)(2,1)} %copy-done.19, bf16[256,1536]{1,0:T(8,128)(2,1)} %copy-done.20, bf16[256,1536]{1,0:T(8,128)(2,1)} %hidden_ref.3), custom_call_target="tpu_custom_call" | custom-call | flops 3449999872 | bytes 1024 | tf_op jit(solution)/shard_map/finish_output/pallas_call | solution.py:703
  234.7 2.0 convert_reduce_fusion
  236.7 3.2 %collective-permute-start.24 = (f32[2,48,768]{2,1,0:T(8,128)S(1)}, f32[2,48,768]{2,1,0:T(8,128)S(1)}, u32[]{:S(2)}, u32[]{:S(2)}) collective-permute-start(f32[2,48,768]{2,1,0:T(8,128)S(1)} %convert_reduce_fusion), channel_id=1, source_target_pairs={{0,0},{1,64},{2,2},{3,66},{64,1},{65,65},{66,3},{67,67},{4,4},{5,6... | collective-permute-start | bytes 884744 | tf_op jit(solution)/shard_map/ppermute | solution.py:822
  239.9 9.0 %collective-permute-done.21.b1 = bf16[256,1536]{1,0:T(8,128)(2,1)S(1)} collective-permute-done((bf16[256,1536]{1,0:T(8,128)(2,1)}, bf16[256,1536]{1,0:T(8,128)(2,1)S(1)}, u32[]{:S(2)}, u32[]{:S(2)}) %collective-permute-start.21) | collective-permute-done | bytes 786464 | tf_op jit(solution)/shard_map/ppermute | solution.py:822
  248.9 10.1 %collective-permute-done.23.b3 = bf16[256,1536]{1,0:T(8,128)(2,1)S(1)} collective-permute-done((bf16[256,1536]{1,0:T(8,128)(2,1)}, bf16[256,1536]{1,0:T(8,128)(2,1)S(1)}, u32[]{:S(2)}, u32[]{:S(2)}) %collective-permute-start.23) | collective-permute-done | bytes 786464 | tf_op jit(solution)/shard_map/ppermute | solution.py:822
  259.0 3.7 %finish_input.1 = f32[256,1536]{1,0:T(8,128)} custom-call(s32[6]{0:T(128)S(1)} %copy-done.8, bf16[256,1536]{1,0:T(8,128)(2,1)S(1)} %collective-permute-done.19.b0, bf16[256,1536]{1,0:T(8,128)(2,1)S(1)} %collective-permute-done.21.b1, bf16[256,1536]{1,0:T(8,128)(2,1)S(1)} %collective-permute-done.22.b2, bf16[256,1536]{1,0:T(8,128)(2,1)S(1)} %collective-permute-done.23.b3, ...), custom_call_target="tpu_custom_call" | custom-call | flops 3449999872 | bytes 1024 | tf_op jit(solution)/shard_map/finish_input/pallas_call | solution.py:724
  263.0 2.2 collective-permute-start.29
  265.2 1.0 collective-permute-start.28
  266.1 2.4 collective-permute-start.27
  268.6 2.3 collective-permute-start.26
  270.8 4.8 %collective-permute-start.25 = (f32[56,896]{1,0:T(8,128)S(1)}, f32[56,896]{1,0:T(8,128)S(1)}, u32[]{:S(2)}, u32[]{:S(2)}) collective-permute-start(f32[56,896]{1,0:T(8,128)S(1)} %get-tuple-element.155), channel_id=1, source_target_pairs={{0,0},{1,64},{2,2},{3,66},{64,1},{65,65},{66,3},{67,67},{4,4},{5,6... | collective-permute-start | bytes 602120 | tf_op jit(solution)/shard_map/ppermute | solution.py:822
  275.6 0.7 slice_bitcast_fusion
  276.4 3.0 %collective-permute-done.25.own_ref = f32[56,896]{1,0:T(8,128)S(1)} collective-permute-done((f32[56,896]{1,0:T(8,128)S(1)}, f32[56,896]{1,0:T(8,128)S(1)}, u32[]{:S(2)}, u32[]{:S(2)}) %collective-permute-start.25) | collective-permute-done | bytes 200736 | tf_op jit(solution)/shard_map/ppermute | solution.py:822
  279.4 0.7 deliver_late.1
  (98 shorter events, 5.0 us)
Async XLA Ops:
  0.6 7.2 %copy-start.15 = (f32[3,12]{1,0:T(4,128)S(1)}, f32[3,12]{1,0:T(4,128)}, u32[]{:S(2)}) copy-start(f32[3,12]{1,0:T(4,128)} %param.21) | copy-start | bytes 436
  0.7 7.2 %copy-start.14 = (f32[768]{0:T(1024)S(1)}, f32[768]{0:T(1024)}, u32[]{:S(2)}) copy-start(f32[768]{0:T(1024)} %param.22) | copy-start | bytes 9220
  0.7 7.2 %copy-start.12 = (f32[5,768]{1,0:T(8,128)S(1)}, f32[5,768]{1,0:T(8,128)}, u32[]{:S(2)}) copy-start(f32[5,768]{1,0:T(8,128)} %param.19) | copy-start | bytes 46084
  1.8 10.0 %collective-permute-start = (bf16[48,2688]{1,0:T(8,128)(2,1)S(1)}, bf16[48,2688]{1,0:T(8,128)(2,1)S(1)}, u32[]{:S(2)}, u32[]{:S(2)}) collective-permute-start(bf16[48,2688]{1,0:T(8,128)(2,1)S(1)} %pack_weights.1), channel_id=1, source_target_pairs={{0,0},{1,64},{2,2},{3,66},{64,1},{65,65},{66,3},{67,67},{4,4},{5,6... | collective-permute-start | bytes 774152 | tf_op jit(solution)/shard_map/ppermute | solution.py:822
  14.1 8.0 %copy-start.16 = (bf16[256,1536]{1,0:T(8,128)(2,1)S(1)}, bf16[256,1536]{1,0:T(8,128)(2,1)}, u32[]{:S(2)}) copy-start(bf16[256,1536]{1,0:T(8,128)(2,1)} %hidden_ref.3) | copy-start | bytes 2359300
  14.1 46.6 %copy-start.13 = (f32[1536]{0:T(1024)S(1)}, f32[1536]{0:T(1024)}, u32[]{:S(2)}) copy-start(f32[1536]{0:T(1024)} %param.14) | copy-start | bytes 18436
  14.1 58.3 %all-to-all-start = ((bf16[16,48,2688]{2,1,0:T(8,128)(2,1)}), bf16[16,48,2688]{2,1,0:T(8,128)(2,1)}, u32[]{:S(2)}, u32[]{:S(2)}) async-start(bf16[16,48,2688]{2,1,0:T(8,128)(2,1)} %broadcast_in_dim.23), calls=%async_computation | async-start | bytes 8257536 | tf_op jit(solution)/shard_map/all_to_all | solution.py:857
  22.0 35.2 %collective-permute-start.2 = (bf16[256,1536]{1,0:T(8,128)(2,1)S(1)}, bf16[256,1536]{1,0:T(8,128)(2,1)S(1)}, u32[]{:S(2)}, u32[]{:S(2)}) collective-permute-start(bf16[256,1536]{1,0:T(8,128)(2,1)S(1)} %copy-done.16), channel_id=1, source_target_pairs={{0,2},{1,66},{2,0},{3,64},{64,3},{65,67},{66,1},{67,65},{4,6},{5,7... | collective-permute-start | bytes 2359304 | tf_op jit(solution)/shard_map/ppermute | solution.py:822
  25.4 31.8 %collective-permute-start.1 = (bf16[256,1536]{1,0:T(8,128)(2,1)S(1)}, bf16[256,1536]{1,0:T(8,128)(2,1)S(1)}, u32[]{:S(2)}, u32[]{:S(2)}) collective-permute-start(bf16[256,1536]{1,0:T(8,128)(2,1)S(1)} %copy-done.16), channel_id=1, source_target_pairs={{0,0},{1,64},{2,2},{3,66},{64,1},{65,65},{66,3},{67,67},{4,4},{5,6... | collective-permute-start | bytes 2359304 | tf_op jit(solution)/shard_map/ppermute | solution.py:822
  27.5 33.2 %collective-permute-start.5 = (bf16[256,1536]{1,0:T(8,128)(2,1)S(1)}, bf16[256,1536]{1,0:T(8,128)(2,1)S(1)}, u32[]{:S(2)}, u32[]{:S(2)}) collective-permute-start(bf16[256,1536]{1,0:T(8,128)(2,1)S(1)} %copy-done.16), channel_id=1, source_target_pairs={{0,66},{1,2},{2,64},{3,0},{64,67},{65,3},{66,65},{67,1},{4,70},{5,... | collective-permute-start | bytes 2359304 | tf_op jit(solution)/shard_map/ppermute | solution.py:822
  27.6 34.1 %collective-permute-start.4 = (bf16[256,1536]{1,0:T(8,128)(2,1)S(1)}, bf16[256,1536]{1,0:T(8,128)(2,1)}, u32[]{:S(2)}, u32[]{:S(2)}) collective-permute-start(bf16[256,1536]{1,0:T(8,128)(2,1)S(1)} %copy-done.16), channel_id=1, source_target_pairs={{0,64},{1,0},{2,66},{3,2},{64,65},{65,1},{66,67},{67,3},{4,68},{5,... | collective-permute-start | bytes 2359304 | tf_op jit(solution)/shard_map/ppermute | solution.py:822
  30.3 2.0 collective-permute-start.3
  57.2 3.6 %copy-start.21 = (bf16[256,1536]{1,0:T(8,128)(2,1)}, bf16[256,1536]{1,0:T(8,128)(2,1)S(1)}, u32[]{:S(2)}) copy-start(bf16[256,1536]{1,0:T(8,128)(2,1)S(1)} %collective-permute-done.2.refs_1_) | copy-start | bytes 2359300
  57.2 3.6 %copy-start.22 = (bf16[256,1536]{1,0:T(8,128)(2,1)}, bf16[256,1536]{1,0:T(8,128)(2,1)S(1)}, u32[]{:S(2)}) copy-start(bf16[256,1536]{1,0:T(8,128)(2,1)S(1)} %collective-permute-done.1.refs_0_) | copy-start | bytes 2359300
  57.2 15.1 %collective-permute-start.6 = (bf16[256,1536]{1,0:T(8,128)(2,1)}, bf16[256,1536]{1,0:T(8,128)(2,1)}, u32[]{:S(2)}, u32[]{:S(2)}) collective-permute-start(bf16[256,1536]{1,0:T(8,128)(2,1)} %cot_ref.1), channel_id=1, source_target_pairs={{0,0},{1,64},{2,2},{3,66},{64,1},{65,65},{66,3},{67,67},{4,4},{5,6... | collective-permute-start | bytes 2359304 | tf_op jit(solution)/shard_map/ppermute | solution.py:822
  60.8 6.4 %copy-start.6 = (s32[6]{0:T(128)}, s32[6]{0:T(128)S(1)}, u32[]{:S(2)}) copy-start(s32[6]{0:T(128)S(1)} %stack.31.meta_ref) | copy-start | bytes 76
  60.8 0.9 copy-start.23
  67.2 56.3 %copy-start = (bf16[1536,1024]{1,0:T(8,128)(2,1)}, bf16[1536,1024]{1,0:T(8,128)(2,1)S(1)}, u32[]{:S(2)}) copy-start(bf16[1536,1024]{1,0:T(8,128)(2,1)S(1)} %get-tuple-element.94.tokens_t_ref) | copy-start | bytes 9437188
  72.3 11.3 %collective-permute-start.7 = (bf16[768,2688]{1,0:T(8,128)(2,1)}, bf16[768,2688]{1,0:T(8,128)(2,1)}, u32[]{:S(2)}, u32[]{:S(2)}) collective-permute-start(bf16[768,2688]{1,0:T(8,128)(2,1)} %bitcast.8.mine_ref.zm_ref.om_ref.xm_ref), channel_id=1, source_target_pairs={{0,1},{1,0},{2,3},{3,2},{4,5},{5,4},{6,7},{7,6},{8,9},{9,8},{10,11... | collective-permute-start | bytes 12386312 | tf_op jit(solution)/shard_map/ppermute | solution.py:832
  74.6 28.8 %collective-permute-start.10 = (bf16[256,1536]{1,0:T(8,128)(2,1)}, bf16[256,1536]{1,0:T(8,128)(2,1)}, u32[]{:S(2)}, u32[]{:S(2)}) collective-permute-start(bf16[256,1536]{1,0:T(8,128)(2,1)} %cot_ref.1), channel_id=1, source_target_pairs={{0,66},{1,2},{2,64},{3,0},{64,67},{65,3},{66,65},{67,1},{4,70},{5,... | collective-permute-start | bytes 2359304 | tf_op jit(solution)/shard_map/ppermute | solution.py:822
  76.1 27.3 %collective-permute-start.9 = (bf16[256,1536]{1,0:T(8,128)(2,1)}, bf16[256,1536]{1,0:T(8,128)(2,1)}, u32[]{:S(2)}, u32[]{:S(2)}) collective-permute-start(bf16[256,1536]{1,0:T(8,128)(2,1)} %cot_ref.1), channel_id=1, source_target_pairs={{0,64},{1,0},{2,66},{3,2},{64,65},{65,1},{66,67},{67,3},{4,68},{5,... | collective-permute-start | bytes 2359304 | tf_op jit(solution)/shard_map/ppermute | solution.py:822
  78.7 26.3 %collective-permute-start.8 = (bf16[256,1536]{1,0:T(8,128)(2,1)}, bf16[256,1536]{1,0:T(8,128)(2,1)}, u32[]{:S(2)}, u32[]{:S(2)}) collective-permute-start(bf16[256,1536]{1,0:T(8,128)(2,1)} %cot_ref.1), channel_id=1, source_target_pairs={{0,2},{1,66},{2,0},{3,64},{64,3},{65,67},{66,1},{67,65},{4,6},{5,7... | collective-permute-start | bytes 2359304 | tf_op jit(solution)/shard_map/ppermute | solution.py:822
  83.6 7.0 %copy-start.2 = (f32[8,1024]{1,0:T(8,128)}, f32[8,1024]{1,0:T(8,128)S(1)}, u32[]{:S(2)}) copy-start(f32[8,1024]{1,0:T(8,128)S(1)} %select_maximum_fusion.1.taps_ref) | copy-start | bytes 98308
  83.6 7.0 %copy-start.4 = (f32[1,768]{1,0:T(1,128)S(1)}, f32[1,768]{1,0:T(1,128)}, u32[]{:S(2)}) copy-start(f32[1,768]{1,0:T(1,128)} %broadcast_in_dim_reshape.3.skip_ref) | copy-start | bytes 9220
  90.6 11.8 %copy-start.10 = (f32[1024,1152]{1,0:T(8,128)}, f32[1024,1152]{1,0:T(8,128)S(1)}, u32[]{:S(2)}) copy-start(f32[1024,1152]{1,0:T(8,128)S(1)} %project_in.1.pre_ref) | copy-start | bytes 14155780
  90.6 14.4 %copy-start.7 = (s32[6]{0:T(128)S(1)}, s32[6]{0:T(128)}, u32[]{:S(2)}) copy-start(s32[6]{0:T(128)} %copy-done.6) | copy-start | bytes 76
  105.0 3.1 %copy-start.1 = (bf16[1024,1536]{1,0:T(8,128)(2,1)S(1)}, bf16[1024,1536]{1,0:T(8,128)(2,1)}, u32[]{:S(2)}) copy-start(bf16[1024,1536]{1,0:T(8,128)(2,1)} %get-tuple-element.97.tokens_ref) | copy-start | bytes 9437188
  117.7 4.1 %collective-permute-start.13 = (f32[8,1024]{1,0:T(8,128)S(1)}, f32[8,1024]{1,0:T(8,128)S(1)}, u32[]{:S(2)}, u32[]{:S(2)}) collective-permute-start(f32[8,1024]{1,0:T(8,128)S(1)} %get-tuple-element.109.s0), channel_id=1, source_target_pairs={{0,66},{1,67},{2,64},{3,65},{64,2},{65,3},{66,0},{67,1},{4,70},{5,... | collective-permute-start | bytes 98312 | tf_op jit(solution)/shard_map/ppermute | solution.py:822
  119.0 4.4 %collective-permute-start.12 = (f32[8,1024]{1,0:T(8,128)S(1)}, f32[8,1024]{1,0:T(8,128)S(1)}, u32[]{:S(2)}, u32[]{:S(2)}) collective-permute-start(f32[8,1024]{1,0:T(8,128)S(1)} %get-tuple-element.109.s0), channel_id=1, source_target_pairs={{0,64},{1,65},{2,66},{3,67},{64,0},{65,1},{66,2},{67,3},{4,68},{5,... | collective-permute-start | bytes 98312 | tf_op jit(solution)/shard_map/ppermute | solution.py:822
  119.3 4.1 %collective-permute-start.11 = (f32[8,1024]{1,0:T(8,128)S(1)}, f32[8,1024]{1,0:T(8,128)S(1)}, u32[]{:S(2)}, u32[]{:S(2)}) collective-permute-start(f32[8,1024]{1,0:T(8,128)S(1)} %get-tuple-element.109.s0), channel_id=1, source_target_pairs={{0,2},{1,3},{2,0},{3,1},{64,66},{65,67},{66,64},{67,65},{4,6},{5,7... | collective-permute-start | bytes 98312 | tf_op jit(solution)/shard_map/ppermute | solution.py:822
  133.4 11.5 %copy-start.9 = (f32[8,768]{1,0:T(8,128)}, f32[8,768]{1,0:T(8,128)S(1)}, u32[]{:S(2)}) copy-start(f32[8,768]{1,0:T(8,128)S(1)} %get-tuple-element.136) | copy-start | bytes 73732
  133.4 11.6 %collective-permute-start.14 = (bf16[16,2,48,768]{3,2,1,0:T(8,128)(2,1)}, bf16[16,2,48,768]{3,2,1,0:T(8,128)(2,1)S(1)}, u32[]{:S(2)}, u32[]{:S(2)}) collective-permute-start(bf16[16,2,48,768]{3,2,1,0:T(8,128)(2,1)} %get-tuple-element.115), channel_id=1, source_target_pairs={{0,1},{1,0},{2,3},{3,2},{4,5},{5,4},{6,7},{7,6},{8,9},{9,8},{10,11... | collective-permute-start | bytes 7077896 | tf_op jit(solution)/shard_map/ppermute | solution.py:832
  147.1 14.1 %copy-start.3 = (f32[8,1024]{1,0:T(8,128)S(1)}, f32[8,1024]{1,0:T(8,128)}, u32[]{:S(2)}) copy-start(f32[8,1024]{1,0:T(8,128)} %copy-done.2) | copy-start | bytes 98308
  147.1 14.1 %copy-start.5 = (f32[1,768]{1,0:T(1,128)S(1)}, f32[1,768]{1,0:T(1,128)}, u32[]{:S(2)}) copy-start(f32[1,768]{1,0:T(1,128)} %broadcast_in_dim_reshape.3.skip_ref) | copy-start | bytes 9220
  147.1 67.8 %all-to-all-start.1 = ((bf16[16,2,48,768]{3,2,1,0:T(8,128)(2,1)}), bf16[16,2,48,768]{3,2,1,0:T(8,128)(2,1)}, u32[]{:S(2)}, u32[]{:S(2)}) async-start(bf16[16,2,48,768]{3,2,1,0:T(8,128)(2,1)} %add_convert_fusion), calls=%async_computation.1 | async-start | bytes 4718592 | tf_op jit(solution)/shard_map/all_to_all | solution.py:862
  154.2 45.6 %collective-permute-start.15 = (bf16[256,1536]{1,0:T(8,128)(2,1)}, bf16[256,1536]{1,0:T(8,128)(2,1)S(1)}, u32[]{:S(2)}, u32[]{:S(2)}) collective-permute-start(bf16[256,1536]{1,0:T(8,128)(2,1)} %get-tuple-element.129), channel_id=1, source_target_pairs={{0,0},{1,64},{2,2},{3,66},{64,1},{65,65},{66,3},{67,67},{4,4},{5,6... | collective-permute-start | bytes 2359304 | tf_op jit(solution)/shard_map/ppermute | solution.py:822
  158.1 41.8 %collective-permute-start.16 = (bf16[256,1536]{1,0:T(8,128)(2,1)}, bf16[256,1536]{1,0:T(8,128)(2,1)S(1)}, u32[]{:S(2)}, u32[]{:S(2)}) collective-permute-start(bf16[256,1536]{1,0:T(8,128)(2,1)} %get-tuple-element.130), channel_id=1, source_target_pairs={{0,2},{1,66},{2,0},{3,64},{64,3},{65,67},{66,1},{67,65},{4,6},{5,7... | collective-permute-start | bytes 2359304 | tf_op jit(solution)/shard_map/ppermute | solution.py:822
  158.2 41.7 %collective-permute-start.17 = (bf16[256,1536]{1,0:T(8,128)(2,1)}, bf16[256,1536]{1,0:T(8,128)(2,1)S(1)}, u32[]{:S(2)}, u32[]{:S(2)}) collective-permute-start(bf16[256,1536]{1,0:T(8,128)(2,1)} %get-tuple-element.131), channel_id=1, source_target_pairs={{0,1},{1,65},{2,3},{3,67},{64,0},{65,64},{66,2},{67,66},{4,5},{5,6... | collective-permute-start | bytes 2359304 | tf_op jit(solution)/shard_map/ppermute | solution.py:822
  158.5 41.4 %collective-permute-start.18 = (bf16[256,1536]{1,0:T(8,128)(2,1)}, bf16[256,1536]{1,0:T(8,128)(2,1)S(1)}, u32[]{:S(2)}, u32[]{:S(2)}) collective-permute-start(bf16[256,1536]{1,0:T(8,128)(2,1)} %get-tuple-element.132), channel_id=1, source_target_pairs={{0,3},{1,67},{2,1},{3,65},{64,2},{65,66},{66,0},{67,64},{4,7},{5,7... | collective-permute-start | bytes 2359304 | tf_op jit(solution)/shard_map/ppermute | solution.py:822
  161.2 26.8 %copy-start.8 = (s32[6]{0:T(128)S(1)}, s32[6]{0:T(128)}, u32[]{:S(2)}) copy-start(s32[6]{0:T(128)} %copy-done.6) | copy-start | bytes 76
  199.8 19.3 %copy-start.17 = (bf16[256,1536]{1,0:T(8,128)(2,1)}, bf16[256,1536]{1,0:T(8,128)(2,1)S(1)}, u32[]{:S(2)}) copy-start(bf16[256,1536]{1,0:T(8,128)(2,1)S(1)} %collective-permute-done.15.b0) | copy-start | bytes 2359300
  199.9 19.3 %copy-start.18 = (bf16[256,1536]{1,0:T(8,128)(2,1)}, bf16[256,1536]{1,0:T(8,128)(2,1)S(1)}, u32[]{:S(2)}) copy-start(bf16[256,1536]{1,0:T(8,128)(2,1)S(1)} %collective-permute-done.16.b1) | copy-start | bytes 2359300
  199.9 11.5 %copy-start.19 = (bf16[256,1536]{1,0:T(8,128)(2,1)}, bf16[256,1536]{1,0:T(8,128)(2,1)S(1)}, u32[]{:S(2)}) copy-start(bf16[256,1536]{1,0:T(8,128)(2,1)S(1)} %collective-permute-done.17.b2) | copy-start | bytes 2359300
  199.9 11.4 %copy-start.20 = (bf16[256,1536]{1,0:T(8,128)(2,1)}, bf16[256,1536]{1,0:T(8,128)(2,1)S(1)}, u32[]{:S(2)}) copy-start(bf16[256,1536]{1,0:T(8,128)(2,1)S(1)} %collective-permute-done.18.b3) | copy-start | bytes 2359300
  199.9 15.0 %collective-permute-start.19 = (bf16[256,1536]{1,0:T(8,128)(2,1)}, bf16[256,1536]{1,0:T(8,128)(2,1)S(1)}, u32[]{:S(2)}, u32[]{:S(2)}) collective-permute-start(bf16[256,1536]{1,0:T(8,128)(2,1)} %get-tuple-element.141), channel_id=1, source_target_pairs={{0,0},{1,64},{2,2},{3,66},{64,1},{65,65},{66,3},{67,67},{4,4},{5,6... | collective-permute-start | bytes 2359304 | tf_op jit(solution)/shard_map/ppermute | solution.py:822
  214.9 4.2 %copy-start.11 = (f32[768,1152]{1,0:T(8,128)S(1)}, f32[768,1152]{1,0:T(8,128)}, u32[]{:S(2)}) copy-start(f32[768,1152]{1,0:T(8,128)} %get-tuple-element.138) | copy-start | bytes 10616836
  214.9 4.0 %collective-permute-start.20 = (bf16[784,1152]{1,0:T(8,128)(2,1)}, bf16[784,1152]{1,0:T(8,128)(2,1)S(1)}, u32[]{:S(2)}, u32[]{:S(2)}) collective-permute-start(bf16[784,1152]{1,0:T(8,128)(2,1)} %get-tuple-element.142), channel_id=1, source_target_pairs={{0,1},{1,0},{2,3},{3,2},{4,5},{5,4},{6,7},{7,6},{8,9},{9,8},{10,11... | collective-permute-start | bytes 5419016 | tf_op jit(solution)/shard_map/ppermute | solution.py:832
  221.1 41.6 %all-to-all-start.2 = ((bf16[16,56,1152]{2,1,0:T(8,128)(2,1)}), bf16[16,56,1152]{2,1,0:T(8,128)(2,1)S(1)}, u32[]{:S(2)}, u32[]{:S(2)}) async-start(bf16[16,56,1152]{2,1,0:T(8,128)(2,1)} %pad_maximum_fusion), calls=%async_computation.2 | async-start | bytes 4128768 | tf_op jit(solution)/shard_map/all_to_all | solution.py:862
  228.0 20.9 %collective-permute-start.21 = (bf16[256,1536]{1,0:T(8,128)(2,1)}, bf16[256,1536]{1,0:T(8,128)(2,1)S(1)}, u32[]{:S(2)}, u32[]{:S(2)}) collective-permute-start(bf16[256,1536]{1,0:T(8,128)(2,1)} %get-tuple-element.144), channel_id=1, source_target_pairs={{0,2},{1,66},{2,0},{3,64},{64,3},{65,67},{66,1},{67,65},{4,6},{5,7... | collective-permute-start | bytes 2359304 | tf_op jit(solution)/shard_map/ppermute | solution.py:822
  229.0 19.9 %collective-permute-start.22 = (bf16[256,1536]{1,0:T(8,128)(2,1)}, bf16[256,1536]{1,0:T(8,128)(2,1)S(1)}, u32[]{:S(2)}, u32[]{:S(2)}) collective-permute-start(bf16[256,1536]{1,0:T(8,128)(2,1)} %get-tuple-element.145), channel_id=1, source_target_pairs={{0,1},{1,65},{2,3},{3,67},{64,0},{65,64},{66,2},{67,66},{4,5},{5,6... | collective-permute-start | bytes 2359304 | tf_op jit(solution)/shard_map/ppermute | solution.py:822
  229.6 29.4 %collective-permute-start.23 = (bf16[256,1536]{1,0:T(8,128)(2,1)}, bf16[256,1536]{1,0:T(8,128)(2,1)S(1)}, u32[]{:S(2)}, u32[]{:S(2)}) collective-permute-start(bf16[256,1536]{1,0:T(8,128)(2,1)} %get-tuple-element.146), channel_id=1, source_target_pairs={{0,3},{1,67},{2,1},{3,65},{64,2},{65,66},{66,0},{67,64},{4,7},{5,7... | collective-permute-start | bytes 2359304 | tf_op jit(solution)/shard_map/ppermute | solution.py:822
  236.7 26.0 %collective-permute-start.24 = (f32[2,48,768]{2,1,0:T(8,128)S(1)}, f32[2,48,768]{2,1,0:T(8,128)S(1)}, u32[]{:S(2)}, u32[]{:S(2)}) collective-permute-start(f32[2,48,768]{2,1,0:T(8,128)S(1)} %convert_reduce_fusion), channel_id=1, source_target_pairs={{0,0},{1,64},{2,2},{3,66},{64,1},{65,65},{66,3},{67,67},{4,4},{5,6... | collective-permute-start | bytes 884744 | tf_op jit(solution)/shard_map/ppermute | solution.py:822
  263.0 13.4 %collective-permute-start.29 = (f32[62,256]{1,0:T(8,128)S(1)}, f32[62,256]{1,0:T(8,128)S(1)}, u32[]{:S(2)}, u32[]{:S(2)}) collective-permute-start(f32[62,256]{1,0:T(8,128)S(1)} %get-tuple-element.156), channel_id=1, source_target_pairs={{0,3},{1,67},{2,1},{3,65},{64,2},{65,66},{66,0},{67,64},{4,7},{5,7... | collective-permute-start | bytes 190472 | tf_op jit(solution)/shard_map/ppermute | solution.py:822
  265.2 11.2 %collective-permute-start.28 = (f32[62,256]{1,0:T(8,128)S(1)}, f32[62,256]{1,0:T(8,128)S(1)}, u32[]{:S(2)}, u32[]{:S(2)}) collective-permute-start(f32[62,256]{1,0:T(8,128)S(1)} %get-tuple-element.156), channel_id=1, source_target_pairs={{0,1},{1,65},{2,3},{3,67},{64,0},{65,64},{66,2},{67,66},{4,5},{5,6... | collective-permute-start | bytes 190472 | tf_op jit(solution)/shard_map/ppermute | solution.py:822
  266.1 10.2 %collective-permute-start.27 = (f32[62,256]{1,0:T(8,128)S(1)}, f32[62,256]{1,0:T(8,128)S(1)}, u32[]{:S(2)}, u32[]{:S(2)}) collective-permute-start(f32[62,256]{1,0:T(8,128)S(1)} %get-tuple-element.156), channel_id=1, source_target_pairs={{0,2},{1,66},{2,0},{3,64},{64,3},{65,67},{66,1},{67,65},{4,6},{5,7... | collective-permute-start | bytes 190472 | tf_op jit(solution)/shard_map/ppermute | solution.py:822
  268.6 7.8 %collective-permute-start.26 = (f32[62,256]{1,0:T(8,128)S(1)}, f32[62,256]{1,0:T(8,128)S(1)}, u32[]{:S(2)}, u32[]{:S(2)}) collective-permute-start(f32[62,256]{1,0:T(8,128)S(1)} %get-tuple-element.156), channel_id=1, source_target_pairs={{0,0},{1,64},{2,2},{3,66},{64,1},{65,65},{66,3},{67,67},{4,4},{5,6... | collective-permute-start | bytes 190472 | tf_op jit(solution)/shard_map/ppermute | solution.py:822
  270.8 8.5 %collective-permute-start.25 = (f32[56,896]{1,0:T(8,128)S(1)}, f32[56,896]{1,0:T(8,128)S(1)}, u32[]{:S(2)}, u32[]{:S(2)}) collective-permute-start(f32[56,896]{1,0:T(8,128)S(1)} %get-tuple-element.155), channel_id=1, source_target_pairs={{0,0},{1,64},{2,2},{3,66},{64,1},{65,65},{66,3},{67,67},{4,4},{5,6... | collective-permute-start | bytes 602120 | tf_op jit(solution)/shard_map/ppermute | solution.py:822

commit v2 on v1

--- a/solution.py
+++ b/solution.py
@@ -330,11 +330,10 @@
     )(meta, gain, *[far(block) for block in blocks])
 
 
-def project_kernel(tokens_ref, mine_ref, other_ref, out_ref):
-    half = mine_ref.shape[0]
-    out_ref[...] = nn(tokens_ref[:, :half], mine_ref[...]) + nn(
-        tokens_ref[:, half:], other_ref[...]
-    )
+def project_kernel(tokens_ref, xm_ref, xo_ref, zm_ref, zo_ref, pre_ref, z_ref):
+    half = xm_ref.shape[0]
+    for first, second, out in ((xm_ref, xo_ref, pre_ref), (zm_ref, zo_ref, z_ref)):
+        out[...] = nn(tokens_ref[:, :half], first[...]) + nn(tokens_ref[:, half:], second[...])
 
 
 def project(tokens, mine, other, inner):
@@ -342,26 +341,37 @@
     length = tokens.shape[0]
     columns = mine.shape[1] - 2 * inner
     rows = ROWS
-    part = pl.BlockSpec((pl.Element(half), pl.Element(columns)), lambda i: (0, 2 * inner))
+
+    def part(width, shift):
+        return pl.BlockSpec(
+            (pl.Element(half), pl.Element(width)),
+            lambda i: (0, shift),
+            pipeline_mode=pl.Buffered(1),
+        )
+
     return pl.pallas_call(
         project_kernel,
         grid=(length // rows,),
-        in_specs=[pl.BlockSpec((rows, 2 * half), lambda i: (i, 0)), part, part],
-        out_specs=pl.BlockSpec((rows, columns), lambda i: (i, 0)),
-        out_shape=shape_of((length, columns), F32),
+        in_specs=[pl.BlockSpec((rows, 2 * half), lambda i: (i, 0))]
+        + [part(columns, 2 * inner)] * 2
+        + [part(inner, 0)] * 2,
+        out_specs=[
+            pl.BlockSpec((rows, columns), lambda i: (i, 0)),
+            pl.BlockSpec((rows, inner), lambda i: (i, 0)),
+        ],
+        out_shape=[shape_of((length, columns), F32), shape_of((length, inner), F32)],
         compiler_params=params(20, "arbitrary"),
         cost_estimate=lasting(6),
         name="project_in",
-    )(far(tokens), far(mine), far(other))
+    )(far(tokens), far(mine), other, far(mine), other)
 
 
 def gate_sums_kernel(
-    tokens_ref, cot_ref, zm_ref, zo_ref, om_ref, oo_ref, y_ref, gain_ref, z_ref, dy_ref, sums_ref
+    cot_ref, om_ref, oo_ref, y_ref, z_ref, gain_ref, dy_ref, sums_ref
 ):
-    half = zm_ref.shape[0]
-    z = nn(tokens_ref[:, :half], zm_ref[...]) + nn(tokens_ref[:, half:], zo_ref[...])
+    half = om_ref.shape[0]
+    z = z_ref[...]
     dy = nn(cot_ref[:, :half], om_ref[...]) + nn(cot_ref[:, half:], oo_ref[...])
-    z_ref[...] = z
     dy_ref[...] = dy
     gated = y_ref[...] * (z * sigmoid(z))
     ones = jnp.ones((8, z.shape[1]), BF)
@@ -381,7 +391,7 @@
         sums_ref[...] += total
 
 
-def gate_sums(tokens, cot, mine, other, y, gain):
+def gate_sums(cot, mine, other, y, z, gain):
     length, inner = y.shape
     half = mine.shape[0]
     tile = 256
@@ -390,25 +400,19 @@
         gate_sums_kernel,
         grid=(steps,),
         in_specs=[
-            whole(tokens.shape),
             whole(cot.shape),
-            column(half, tile),
-            column(half, tile),
             column(half, tile, steps),
             column(half, tile, steps),
             column(length, tile),
+            column(length, tile),
             column(1, tile),
         ],
-        out_specs=[column(length, tile), column(length, tile), whole((8, length))],
-        out_shape=[
-            shape_of((length, inner), F32),
-            shape_of((length, inner), F32),
-            shape_of((8, length), F32),
-        ],
+        out_specs=[column(length, tile), whole((8, length))],
+        out_shape=[shape_of((length, inner), F32), shape_of((8, length), F32)],
         compiler_params=params(36, "arbitrary"),
-        cost_estimate=lasting(9),
+        cost_estimate=lasting(6),
         name="gate_sums",
-    )(near(tokens), near(cot), far(mine), far(other), far(mine), far(other), near(y), gain)
+    )(near(cot), far(mine), far(other), near(y), near(z), gain)
 
 
 def gate_back_kernel(
@@ -899,7 +903,11 @@
     mine = gather_plane(weights)
     hidden, weights = after(hidden_in, weights)
     hidden_blocks = to_workers(hidden)
-    first_half, cot, small = after(hidden_blocks[:2], cotangent, small)
+    conv_x, gate_row, head_params = small[:5], small[5:6], small[6:9, :heads]
+    taps, head, skip, spread = mixer_tables(conv_x, conv_bc, head_params)
+    first_half, cot, taps, head, skip, spread, gate_row, meta, gain = after(
+        hidden_blocks[:2], cotangent, taps, head, skip, spread, gate_row, meta, gain
+    )
     hidden_blocks = first_half + hidden_blocks[2:]
     cot_blocks = to_workers(cot)
     tokens, tokens_t = place(meta, gain, hidden_blocks, True)
@@ -907,13 +915,11 @@
     cot_blocks = [cot_first] + cot_blocks[1:]
     other = swap_core(mine)
 
-    conv_x, gate_row, head_params = small[:5], small[5:6], small[6:9, :heads]
-    taps, head, skip, spread = mixer_tables(conv_x, conv_bc, head_params)
-    pre = project(tokens, mine, other, wide)
+    pre, z = project(tokens, mine, other, wide)
     y, kept, conv = mixer_forward(pre, taps, head, skip, spread)
     y, cot_blocks = after(y, cot_blocks)
     cot, cot_t = place(meta, gain, cot_blocks, False)
-    z, dy, sums = gate_sums(tokens, cot, mine, other, y, gate_row)
+    dy, sums = gate_sums(cot, mine, other, y, z, gate_row)
     normed_y, gate, dscan, gain_grad, keep, send = gate_back(
         block, 4.0 * wide, around(sums), z, dy, y, gate_row, tokens_t, cot_t
     )
@@ -946,16 +952,18 @@
     vector = jnp.broadcast_to(vector[None], (late_sum.shape[0],) + vector.shape)
     late_sum = jnp.concatenate([late_sum, vector], axis=1)
     back_blocks = [back_first] + back_blocks[1:]
-    input_grad = finish_input(meta, back_blocks, hidden_in, cotangent, gain)
     early = trade(early.astype(F32).sum(axis=0))
-    got, input_grad, early, output = after(exchange(late_sum), input_grad, early, output)
+    got, early, output = after(exchange(late_sum), early, output)
     own, shared = total_of(got, states)
+    own, back_blocks = after(own, back_blocks)
+    own = trade(own)
 
     shared = [
         permute(shared, lambda xh, xl, core, a=a, b=b: (core, xl ^ b, xh ^ a)) for a, b in TURNS
     ]
+    input_grad = finish_input(meta, back_blocks, hidden_in, cotangent, gain)
     norm_grad, x_grad, bc_grad, dt_grad, conv_x_grad, conv_bc_grad, head_part, gate_part = deliver(
-        trade(own), shared, block, heads
+        own, shared, block, heads
     )
     return (
         output,

time: 282 us -> 273 us (0.968)
  waiting for transfers between devices: 69.1 us -> 65.9 us
    ppermute x26, waiting for transfers between devices: 63.9 us -> 58.8 us  [permute(): return lax.ppermute(value, GROUP, moves(rule))]
    pallas_call x1, Pallas kernels: 6.94 us -> 10.7 us  [project(): pl.pallas_call(project_kernel, grid=(length // rows,), in_specs=[pl.Block...]
  transfers between devices with their start and end apart: 33 -> 33, of which waited for: 13 -> 11; matrix products, arithmetic and copies ran while one was open for 4% -> 2% of each run, Pallas kernels for 31% -> 33%
where the time goes in v2:
time: 273 us; the launch traced here: 272 us
  Pallas kernels  113 us (41%)
  starting transfers between devices  78 us (29%)
  waiting for transfers between devices  65.9 us (24%)
  other arithmetic  7.35 us (3%)
  local copies, waits for them, and re-layouts  6.74 us (2%)
    ppermute x26, waiting for transfers between devices, permute(): return lax.ppermute(value, GROUP, moves(rule))  58.8 us
    ppermute x26, starting transfers between devices, permute(): return lax.ppermute(value, GROUP, moves(rule))  53.6 us
    pallas_call x1, Pallas kernels, mixer_backward(): pl.pallas_call(backward_kernel, grid=(steps,), in_specs=[pl.BlockSpec((SP...  26.8 us
    all_to_all x2, starting transfers between devices, exchange(): return lax.all_to_all(blocks, PLANE, 0, 0, tiled=True)  13.9 us
    pallas_call x1, Pallas kernels, project_back(): pl.pallas_call(project_back_kernel, grid=(2 * per,), in_specs=[pl.BlockSp...  11.8 us
    pallas_call x1, Pallas kernels, mixer_forward(): pl.pallas_call(forward_kernel, grid=(steps,), in_specs=[pl.BlockSpec((SPA...  11.7 us
    pallas_call x1, Pallas kernels, project(): pl.pallas_call(project_kernel, grid=(length // rows,), in_specs=[pl.Block...  10.7 us
    pallas_call x1, Pallas kernels, gate_back(): pl.pallas_call(functools.partial(gate_back_kernel, width_all), grid=(inne...  9.94 us
  transfers between devices with their start and end apart: 33, of which 11 were waited for; matrix products, arithmetic and copies ran while one was open for 2% of the time, Pallas kernels for 33%

profile of v2, /device:TPU:1, one launch (start us, length us, event | category | flops | bytes accessed | tf_op | source)
XLA Modules:
  0.0 272.0 jit_solution(12332655294542925955)
XLA Ops:
  0.7 1.1 pack_weights.1
  1.8 6.0 %collective-permute-start = (bf16[48,2688]{1,0:T(8,128)(2,1)S(1)}, bf16[48,2688]{1,0:T(8,128)(2,1)S(1)}, u32[]{:S(2)}, u32[]{:S(2)}) collective-permute-start(bf16[48,2688]{1,0:T(8,128)(2,1)S(1)} %pack_weights.1), channel_id=1, source_target_pairs={{0,0},{1,64},{2,2},{3,66},{64,1},{65,65},{66,3},{67,67},{4,4},{5,6... | collective-permute-start | bytes 774152 | tf_op jit(solution)/shard_map/ppermute | solution.py:826
  7.9 3.9 %collective-permute-done = bf16[48,2688]{1,0:T(8,128)(2,1)S(1)} collective-permute-done((bf16[48,2688]{1,0:T(8,128)(2,1)S(1)}, bf16[48,2688]{1,0:T(8,128)(2,1)S(1)}, u32[]{:S(2)}, u32[]{:S(2)}) %collective-permute-start) | collective-permute-done | bytes 258080 | tf_op jit(solution)/shard_map/ppermute | solution.py:826
  11.8 2.2 broadcast_in_dim.24
  14.1 7.9 %all-to-all-start = ((bf16[16,48,2688]{2,1,0:T(8,128)(2,1)}), bf16[16,48,2688]{2,1,0:T(8,128)(2,1)}, u32[]{:S(2)}, u32[]{:S(2)}) async-start(bf16[16,48,2688]{2,1,0:T(8,128)(2,1)} %broadcast_in_dim.24), calls=%async_computation | async-start | bytes 8257536 | tf_op jit(solution)/shard_map/all_to_all | solution.py:861
  22.1 3.3 %collective-permute-start.2 = (bf16[256,1536]{1,0:T(8,128)(2,1)S(1)}, bf16[256,1536]{1,0:T(8,128)(2,1)S(1)}, u32[]{:S(2)}, u32[]{:S(2)}) collective-permute-start(bf16[256,1536]{1,0:T(8,128)(2,1)S(1)} %copy-done.17), channel_id=1, source_target_pairs={{0,2},{1,66},{2,0},{3,64},{64,3},{65,67},{66,1},{67,65},{4,6},{5,7... | collective-permute-start | bytes 2359304 | tf_op jit(solution)/shard_map/ppermute | solution.py:826
  25.4 2.2 collective-permute-start.1
  27.9 0.6 stack.32.meta_ref
  28.5 0.7 collective-permute-start.5
  29.2 2.0 collective-permute-start.4
  31.4 0.7 broadcast_in_dim_reshape.3.skip_ref
  32.0 0.6 select_maximum_fusion.1.taps_ref
  32.7 24.6 %collective-permute-done.2.refs_1_ = bf16[256,1536]{1,0:T(8,128)(2,1)S(1)} collective-permute-done((bf16[256,1536]{1,0:T(8,128)(2,1)S(1)}, bf16[256,1536]{1,0:T(8,128)(2,1)S(1)}, u32[]{:S(2)}, u32[]{:S(2)}) %collective-permute-start.2) | collective-permute-done | bytes 786464 | tf_op jit(solution)/shard_map/ppermute | solution.py:826
  57.2 3.4 %collective-permute-start.6 = (bf16[256,1536]{1,0:T(8,128)(2,1)}, bf16[256,1536]{1,0:T(8,128)(2,1)}, u32[]{:S(2)}, u32[]{:S(2)}) collective-permute-start(bf16[256,1536]{1,0:T(8,128)(2,1)} %cot_ref.1), channel_id=1, source_target_pairs={{0,0},{1,64},{2,2},{3,66},{64,1},{65,65},{66,3},{67,67},{4,4},{5,6... | collective-permute-start | bytes 2359304 | tf_op jit(solution)/shard_map/ppermute | solution.py:826
  60.8 0.6 copy-done.6
  61.4 5.4 %place_normed.1 = (bf16[1024,1536]{1,0:T(8,128)(2,1)}, bf16[1536,1024]{1,0:T(8,128)(2,1)S(1)}) custom-call(s32[6]{0:T(128)S(1)} %copy-done.6, f32[1,1536]{1,0:T(1,128)S(1)} %broadcast_in_dim.23.gain_ref, bf16[256,1536]{1,0:T(8,128)(2,1)} %copy-done.23, bf16[256,1536]{1,0:T(8,128)(2,1)} %copy-done.22, bf16[256,1536]{1,0:T(8,128)(2,1)} %collective-permute-done.4.refs_2_, ...), custom_call_target="tpu_custom_call" | custom-call | flops 6899999744 | bytes 1024 | tf_op jit(solution)/shard_map/place_normed/pallas_call | solution.py:319
  66.8 5.6 %collective-permute-done.6.refs_0_ = bf16[256,1536]{1,0:T(8,128)(2,1)} collective-permute-done((bf16[256,1536]{1,0:T(8,128)(2,1)}, bf16[256,1536]{1,0:T(8,128)(2,1)}, u32[]{:S(2)}, u32[]{:S(2)}) %collective-permute-start.6) | collective-permute-done | bytes 786464 | tf_op jit(solution)/shard_map/ppermute | solution.py:826
  72.5 1.4 collective-permute-start.10
  73.9 2.8 %collective-permute-start.9 = (bf16[256,1536]{1,0:T(8,128)(2,1)}, bf16[256,1536]{1,0:T(8,128)(2,1)S(1)}, u32[]{:S(2)}, u32[]{:S(2)}) collective-permute-start(bf16[256,1536]{1,0:T(8,128)(2,1)} %cot_ref.1), channel_id=1, source_target_pairs={{0,64},{1,0},{2,66},{3,2},{64,65},{65,1},{66,67},{67,3},{4,68},{5,... | collective-permute-start | bytes 2359304 | tf_op jit(solution)/shard_map/ppermute | solution.py:826
  76.7 3.1 %collective-permute-done.7.xo_ref.zo_ref.oo_ref = bf16[768,2688]{1,0:T(8,128)(2,1)S(1)} collective-permute-done((bf16[768,2688]{1,0:T(8,128)(2,1)}, bf16[768,2688]{1,0:T(8,128)(2,1)S(1)}, u32[]{:S(2)}, u32[]{:S(2)}) %collective-permute-start.7) | collective-permute-done | bytes 4128800 | tf_op jit(solution)/shard_map/ppermute | solution.py:836
  79.7 10.7 %project_in.1 = (f32[1024,1152]{1,0:T(8,128)S(1)}, f32[1024,768]{1,0:T(8,128)S(1)}) custom-call(bf16[1024,1536]{1,0:T(8,128)(2,1)} %get-tuple-element.110.tokens_ref, bf16[768,2688]{1,0:T(8,128)(2,1)} %bitcast.9.xm_ref.zm_ref.om_ref, bf16[768,2688]{1,0:T(8,128)(2,1)S(1)} %collective-permute-done.7.xo_ref.zo_ref.oo_ref, ...), custom_call_target="tpu_custom_call" | custom-call | flops 6899999744 | bytes 1024 | tf_op jit(solution)/shard_map/project_in/pallas_call | solution.py:352
  90.4 11.7 %mixer_forward.1 = (f32[1024,768]{1,0:T(8,128)S(1)}, bf16[1024,768]{1,0:T(8,128)(2,1)}, f32[1024,1024]{1,0:T(8,128)}) custom-call(f32[1024,1152]{1,0:T(8,128)S(1)} %get-tuple-element.112.pre_ref, f32[8,1024]{1,0:T(8,128)S(1)} %copy-done.2, f32[8,128]{1,0:T(8,128)S(1)} %select_maximum_fusion.4.head_ref, f32[1,768]{1,0:T(1,128)S(1)} %copy-done.4, ...), custom_call_target="tpu_custom_call" | custom-call | flops 14949999616 | bytes 1024 | tf_op jit(solution)/shard_map/mixer_forward/pallas_call | solution.py:756
  102.2 0.5 collective-permute-done.8.refs_1_
  102.7 0.3 copy-done.26
  103.0 0.3 copy-done.27
  103.6 3.0 %place_cotangent.1 = (bf16[1024,1536]{1,0:T(8,128)(2,1)S(1)}, bf16[1536,1024]{1,0:T(8,128)(2,1)S(1)}) custom-call(s32[6]{0:T(128)S(1)} %copy-done.7, f32[1,1536]{1,0:T(1,128)S(1)} %broadcast_in_dim.23.gain_ref, bf16[256,1536]{1,0:T(8,128)(2,1)} %collective-permute-done.6.refs_0_, bf16[256,1536]{1,0:T(8,128)(2,1)} %copy-done.28, ...), custom_call_target="tpu_custom_call" | custom-call | flops 6899999744 | bytes 1024 | tf_op jit(solution)/shard_map/place_cotangent/pallas_call | solution.py:319
  106.6 7.4 %gate_sums.1 = (f32[1024,768]{1,0:T(8,128)S(1)}, f32[8,1024]{1,0:T(8,128)S(1)}) custom-call(bf16[1024,1536]{1,0:T(8,128)(2,1)S(1)} %get-tuple-element.124.cot_ref, bf16[768,2688]{1,0:T(8,128)(2,1)} %bitcast.9.xm_ref.zm_ref.om_ref, bf16[768,2688]{1,0:T(8,128)(2,1)} %copy-done, f32[1024,768]{1,0:T(8,128)S(1)} %get-tuple-element.125.y_ref, ...), custom_call_target="tpu_custom_call" | custom-call | flops 6899999744 | bytes 1024 | tf_op jit(solution)/shard_map/gate_sums/pallas_call | solution.py:399
  114.0 3.5 %collective-permute-start.13 = (f32[8,1024]{1,0:T(8,128)S(1)}, f32[8,1024]{1,0:T(8,128)S(1)}, u32[]{:S(2)}, u32[]{:S(2)}) collective-permute-start(f32[8,1024]{1,0:T(8,128)S(1)} %get-tuple-element.128.s0), channel_id=1, source_target_pairs={{0,66},{1,67},{2,64},{3,65},{64,2},{65,3},{66,0},{67,1},{4,70},{5,... | collective-permute-start | bytes 98312 | tf_op jit(solution)/shard_map/ppermute | solution.py:826
  117.5 0.7 collective-permute-start.11
  118.1 0.6 collective-permute-done.13.s3
  118.8 3.0 %collective-permute-done.12.s2 = f32[8,1024]{1,0:T(8,128)S(1)} collective-permute-done((f32[8,1024]{1,0:T(8,128)S(1)}, f32[8,1024]{1,0:T(8,128)S(1)}, u32[]{:S(2)}, u32[]{:S(2)}) %collective-permute-start.12) | collective-permute-done | bytes 32800 | tf_op jit(solution)/shard_map/ppermute | solution.py:826
  121.7 9.9 %gate_back.1 = (bf16[1024,768]{1,0:T(8,128)(2,1)}, bf16[1024,768]{1,0:T(8,128)(2,1)}, f32[1024,768]{1,0:T(8,128)}, f32[8,768]{1,0:T(8,128)S(1)}, bf16[16,2,48,76...) custom-call(f32[8,1024]{1,0:T(8,128)S(1)} %get-tuple-element.128.s0, f32[8,1024]{1,0:T(8,128)S(1)} %collective-permute-done.11.s1, ...), custom_call_target="tpu_custom_call" | custom-call | flops 13799999488 | bytes 1024 | tf_op jit(solution)/shard_map/gate_back/pallas_call | solution.py:455
  131.7 2.3 collective-permute-start.14
  134.0 7.7 %project_out.1 = (bf16[256,1536]{1,0:T(8,128)(2,1)}, bf16[256,1536]{1,0:T(8,128)(2,1)}, bf16[256,1536]{1,0:T(8,128)(2,1)}, bf16[256,1536]{1,0:T(8,128)(2,1)}) custom-call(s32[6]{0:T(128)S(1)} %copy-done.7, bf16[1024,768]{1,0:T(8,128)(2,1)} %get-tuple-element.134.normed_ref, bf16[768,2688]{1,0:T(8,128)(2,1)} %bitcast.9.xm_ref.zm_ref.om_ref, ...), custom_call_target="tpu_custom_call" | custom-call | flops 6899999744 | bytes 1024 | tf_op jit(solution)/shard_map/project_out/pallas_call | solution.py:513
  141.7 2.2 add_convert_fusion
  143.9 7.1 %all-to-all-start.1 = ((bf16[16,2,48,768]{3,2,1,0:T(8,128)(2,1)}), bf16[16,2,48,768]{3,2,1,0:T(8,128)(2,1)}, u32[]{:S(2)}, u32[]{:S(2)}) async-start(bf16[16,2,48,768]{3,2,1,0:T(8,128)(2,1)} %add_convert_fusion), calls=%async_computation.1 | async-start | bytes 4718592 | tf_op jit(solution)/shard_map/all_to_all | solution.py:866
  150.9 4.1 %collective-permute-start.15 = (bf16[256,1536]{1,0:T(8,128)(2,1)}, bf16[256,1536]{1,0:T(8,128)(2,1)S(1)}, u32[]{:S(2)}, u32[]{:S(2)}) collective-permute-start(bf16[256,1536]{1,0:T(8,128)(2,1)} %get-tuple-element.147), channel_id=1, source_target_pairs={{0,0},{1,64},{2,2},{3,66},{64,1},{65,65},{66,3},{67,67},{4,4},{5,6... | collective-permute-start | bytes 2359304 | tf_op jit(solution)/shard_map/ppermute | solution.py:826
  155.2 3.0 %collective-permute-start.18 = (bf16[256,1536]{1,0:T(8,128)(2,1)S(1)}, bf16[256,1536]{1,0:T(8,128)(2,1)S(1)}, u32[]{:S(2)}, u32[]{:S(2)}) collective-permute-start(bf16[256,1536]{1,0:T(8,128)(2,1)S(1)} %copy-done.24), channel_id=1, source_target_pairs={{0,3},{1,67},{2,1},{3,65},{64,2},{65,66},{66,0},{67,64},{4,7},{5,7... | collective-permute-start | bytes 2359304 | tf_op jit(solution)/shard_map/ppermute | solution.py:826
  158.2 26.8 %mixer_backward.1 = (bf16[1024,1152]{1,0:T(8,128)(2,1)S(1)}, f32[8,1024]{1,0:T(8,128)S(1)}, f32[8,128]{1,0:T(8,128)S(1)}) custom-call(f32[1024,1152]{1,0:T(8,128)} %copy-done.10, f32[1024,1024]{1,0:T(8,128)} %get-tuple-element.117.conv_ref, f32[1024,768]{1,0:T(8,128)} %get-tuple-element.139.dy_ref, bf16[1024,768]{1,0:T(8,128)(2,1)} %get-tuple-element.140.kept_ref, ...), custom_call_target="tpu_custom_call" | custom-call | flops 34500001792 | bytes 1024 | tf_op jit(solution)/shard_map/mixer_backward/pallas_call | solution.py:786
  185.0 11.8 %project_back.1 = (bf16[256,1536]{1,0:T(8,128)(2,1)}, bf16[256,1536]{1,0:T(8,128)(2,1)}, bf16[256,1536]{1,0:T(8,128)(2,1)}, bf16[256,1536]{1,0:T(8,128)(2,1)}, f32[8,1536]{1,0:T(8,128)S(1)}) custom-call(s32[6]{0:T(128)S(1)} %copy-done.8, bf16[1024,1152]{1,0:T(8,128)(2,1)S(1)} %get-tuple-element.151.late_ref, bf16[1024,768]{1,0:T(8,128)(2,1)} %get-tuple-element.142.gate_ref, ...), custom_call_target="tpu_custom_call" | custom-call | flops 575000000 | bytes 1024 | tf_op jit(solution)/shard_map/project_back/pallas_call | solution.py:556
  196.8 2.3 collective-permute-start.19
  199.1 0.7 slice.60
  199.9 8.4 %weight_grad.1 = (f32[768,1152]{1,0:T(8,128)}, bf16[784,1152]{1,0:T(8,128)(2,1)}) custom-call(bf16[1536,1024]{1,0:T(8,128)(2,1)} %copy-done.1, bf16[1024,1152]{1,0:T(8,128)(2,1)S(1)} %get-tuple-element.151.late_ref, f32[16,1152]{1,0:T(8,128)S(1)} %pad.29.vector_ref), custom_call_target="tpu_custom_call" | custom-call | flops 575000000 | bytes 1024 | tf_op jit(solution)/shard_map/weight_grad/pallas_call | solution.py:587
  208.3 3.5 %collective-permute-done.19.b0 = bf16[256,1536]{1,0:T(8,128)(2,1)S(1)} collective-permute-done((bf16[256,1536]{1,0:T(8,128)(2,1)}, bf16[256,1536]{1,0:T(8,128)(2,1)S(1)}, u32[]{:S(2)}, u32[]{:S(2)}) %collective-permute-start.19) | collective-permute-done | bytes 786464 | tf_op jit(solution)/shard_map/ppermute | solution.py:826
  211.8 4.0 %collective-permute-done.20 = bf16[784,1152]{1,0:T(8,128)(2,1)S(1)} collective-permute-done((bf16[784,1152]{1,0:T(8,128)(2,1)}, bf16[784,1152]{1,0:T(8,128)(2,1)S(1)}, u32[]{:S(2)}, u32[]{:S(2)}) %collective-permute-start.20) | collective-permute-done | bytes 1806368 | tf_op jit(solution)/shard_map/ppermute | solution.py:836
  216.1 0.6 fusion
  216.7 1.5 pad_maximum_fusion
  218.1 6.9 %all-to-all-start.2 = ((bf16[16,56,1152]{2,1,0:T(8,128)(2,1)}), bf16[16,56,1152]{2,1,0:T(8,128)(2,1)S(1)}, u32[]{:S(2)}, u32[]{:S(2)}) async-start(bf16[16,56,1152]{2,1,0:T(8,128)(2,1)} %pad_maximum_fusion), calls=%async_computation.2 | async-start | bytes 4128768 | tf_op jit(solution)/shard_map/all_to_all | solution.py:866
  225.0 0.8 collective-permute-start.22
  225.7 0.6 collective-permute-start.23
  226.4 1.8 collective-permute-start.24
  228.1 2.0 convert_reduce_fusion
  230.2 3.0 %collective-permute-start.21 = (f32[2,48,768]{2,1,0:T(8,128)S(1)}, f32[2,48,768]{2,1,0:T(8,128)S(1)}, u32[]{:S(2)}, u32[]{:S(2)}) collective-permute-start(f32[2,48,768]{2,1,0:T(8,128)S(1)} %convert_reduce_fusion), channel_id=1, source_target_pairs={{0,0},{1,64},{2,2},{3,66},{64,1},{65,65},{66,3},{67,67},{4,4},{5,6... | collective-permute-start | bytes 884744 | tf_op jit(solution)/shard_map/ppermute | solution.py:826
  233.1 3.5 %finish_output.1 = bf16[256,1536]{1,0:T(8,128)(2,1)} custom-call(s32[6]{0:T(128)S(1)} %copy-done.8, bf16[256,1536]{1,0:T(8,128)(2,1)} %copy-done.18, bf16[256,1536]{1,0:T(8,128)(2,1)} %copy-done.19, bf16[256,1536]{1,0:T(8,128)(2,1)} %copy-done.20, bf16[256,1536]{1,0:T(8,128)(2,1)} %copy-done.21, bf16[256,1536]{1,0:T(8,128)(2,1)} %hidden_ref.3), custom_call_target="tpu_custom_call" | custom-call | flops 3449999872 | bytes 1024 | tf_op jit(solution)/shard_map/finish_output/pallas_call | solution.py:707
  236.6 17.1 %collective-permute-done.21 = f32[2,48,768]{2,1,0:T(8,128)S(1)} collective-permute-done((f32[2,48,768]{2,1,0:T(8,128)S(1)}, f32[2,48,768]{2,1,0:T(8,128)S(1)}, u32[]{:S(2)}, u32[]{:S(2)}) %collective-permute-start.21) | collective-permute-done | bytes 294944 | tf_op jit(solution)/shard_map/ppermute | solution.py:826
  253.8 0.3 late_total.1
  254.1 0.2 collective-permute-start.29
  254.3 3.6 %collective-permute-start.28 = (f32[62,256]{1,0:T(8,128)S(1)}, f32[62,256]{1,0:T(8,128)S(1)}, u32[]{:S(2)}, u32[]{:S(2)}) collective-permute-start(f32[62,256]{1,0:T(8,128)S(1)} %get-tuple-element.178), channel_id=1, source_target_pairs={{0,1},{1,65},{2,3},{3,67},{64,0},{65,64},{66,2},{67,66},{4,5},{5,6... | collective-permute-start | bytes 190472 | tf_op jit(solution)/shard_map/ppermute | solution.py:826
  257.9 1.1 collective-permute-start.27
  259.0 2.3 collective-permute-start.26
  261.3 4.8 %collective-permute-start.25 = (f32[56,896]{1,0:T(8,128)S(1)}, f32[56,896]{1,0:T(8,128)S(1)}, u32[]{:S(2)}, u32[]{:S(2)}) collective-permute-start(f32[56,896]{1,0:T(8,128)S(1)} %get-tuple-element.177), channel_id=1, source_target_pairs={{0,0},{1,64},{2,2},{3,66},{64,1},{65,65},{66,3},{67,67},{4,4},{5,6... | collective-permute-start | bytes 602120 | tf_op jit(solution)/shard_map/ppermute | solution.py:826
  266.1 4.4 %finish_input.1 = f32[256,1536]{1,0:T(8,128)} custom-call(s32[6]{0:T(128)S(1)} %copy-done.8, bf16[256,1536]{1,0:T(8,128)(2,1)S(1)} %collective-permute-done.19.b0, bf16[256,1536]{1,0:T(8,128)(2,1)} %collective-permute-done.22.b1, bf16[256,1536]{1,0:T(8,128)(2,1)} %collective-permute-done.23.b2, bf16[256,1536]{1,0:T(8,128)(2,1)} %collective-permute-done.24.b3, ...), custom_call_target="tpu_custom_call" | custom-call | flops 3449999872 | bytes 1024 | tf_op jit(solution)/shard_map/finish_input/pallas_call | solution.py:728
  270.5 0.7 slice_bitcast_fusion
  271.3 0.7 deliver_late.1
  (108 shorter events, 1.5 us)
Async XLA Ops:
  0.6 7.2 %copy-start.16 = (f32[3,12]{1,0:T(4,128)S(1)}, f32[3,12]{1,0:T(4,128)}, u32[]{:S(2)}) copy-start(f32[3,12]{1,0:T(4,128)} %param.21) | copy-start | bytes 436
  0.7 7.2 %copy-start.15 = (f32[768]{0:T(1024)S(1)}, f32[768]{0:T(1024)}, u32[]{:S(2)}) copy-start(f32[768]{0:T(1024)} %param.22) | copy-start | bytes 9220
  0.7 7.2 %copy-start.12 = (f32[5,768]{1,0:T(8,128)S(1)}, f32[5,768]{1,0:T(8,128)}, u32[]{:S(2)}) copy-start(f32[5,768]{1,0:T(8,128)} %param.19) | copy-start | bytes 46084
  1.8 10.0 %collective-permute-start = (bf16[48,2688]{1,0:T(8,128)(2,1)S(1)}, bf16[48,2688]{1,0:T(8,128)(2,1)S(1)}, u32[]{:S(2)}, u32[]{:S(2)}) collective-permute-start(bf16[48,2688]{1,0:T(8,128)(2,1)S(1)} %pack_weights.1), channel_id=1, source_target_pairs={{0,0},{1,64},{2,2},{3,66},{64,1},{65,65},{66,3},{67,67},{4,4},{5,6... | collective-permute-start | bytes 774152 | tf_op jit(solution)/shard_map/ppermute | solution.py:826
  14.1 8.0 %copy-start.17 = (bf16[256,1536]{1,0:T(8,128)(2,1)S(1)}, bf16[256,1536]{1,0:T(8,128)(2,1)}, u32[]{:S(2)}) copy-start(bf16[256,1536]{1,0:T(8,128)(2,1)} %hidden_ref.3) | copy-start | bytes 2359300
  14.1 13.8 %copy-start.13 = (f32[1536]{0:T(1024)S(1)}, f32[1536]{0:T(1024)}, u32[]{:S(2)}) copy-start(f32[1536]{0:T(1024)} %param.14) | copy-start | bytes 18436
  14.1 18.0 %copy-start.14 = (f32[5,256]{1,0:T(8,128)S(1)}, f32[5,256]{1,0:T(8,128)}, u32[]{:S(2)}) copy-start(f32[5,256]{1,0:T(8,128)} %param.20) | copy-start | bytes 15364
  14.1 58.3 %all-to-all-start = ((bf16[16,48,2688]{2,1,0:T(8,128)(2,1)}), bf16[16,48,2688]{2,1,0:T(8,128)(2,1)}, u32[]{:S(2)}, u32[]{:S(2)}) async-start(bf16[16,48,2688]{2,1,0:T(8,128)(2,1)} %broadcast_in_dim.24), calls=%async_computation | async-start | bytes 8257536 | tf_op jit(solution)/shard_map/all_to_all | solution.py:861
  22.1 35.2 %collective-permute-start.2 = (bf16[256,1536]{1,0:T(8,128)(2,1)S(1)}, bf16[256,1536]{1,0:T(8,128)(2,1)S(1)}, u32[]{:S(2)}, u32[]{:S(2)}) collective-permute-start(bf16[256,1536]{1,0:T(8,128)(2,1)S(1)} %copy-done.17), channel_id=1, source_target_pairs={{0,2},{1,66},{2,0},{3,64},{64,3},{65,67},{66,1},{67,65},{4,6},{5,7... | collective-permute-start | bytes 2359304 | tf_op jit(solution)/shard_map/ppermute | solution.py:826
  25.4 31.8 %collective-permute-start.1 = (bf16[256,1536]{1,0:T(8,128)(2,1)S(1)}, bf16[256,1536]{1,0:T(8,128)(2,1)S(1)}, u32[]{:S(2)}, u32[]{:S(2)}) collective-permute-start(bf16[256,1536]{1,0:T(8,128)(2,1)S(1)} %copy-done.17), channel_id=1, source_target_pairs={{0,0},{1,64},{2,2},{3,66},{64,1},{65,65},{66,3},{67,67},{4,4},{5,6... | collective-permute-start | bytes 2359304 | tf_op jit(solution)/shard_map/ppermute | solution.py:826
  27.6 3.6 %collective-permute-start.3 = (f32[16,768]{1,0:T(8,128)S(1)}, f32[16,768]{1,0:T(8,128)S(1)}, u32[]{:S(2)}, u32[]{:S(2)}) collective-permute-start(f32[16,768]{1,0:T(8,128)S(1)} %select_maximum_fusion), channel_id=1, source_target_pairs={{0,1},{1,0},{2,3},{3,2},{4,5},{5,4},{6,7},{7,6},{8,9},{9,8},{10,11... | collective-permute-start | bytes 147464 | tf_op jit(solution)/shard_map/ppermute | solution.py:836
  28.5 32.2 %collective-permute-start.5 = (bf16[256,1536]{1,0:T(8,128)(2,1)S(1)}, bf16[256,1536]{1,0:T(8,128)(2,1)}, u32[]{:S(2)}, u32[]{:S(2)}) collective-permute-start(bf16[256,1536]{1,0:T(8,128)(2,1)S(1)} %copy-done.17), channel_id=1, source_target_pairs={{0,66},{1,2},{2,64},{3,0},{64,67},{65,3},{66,65},{67,1},{4,70},{5,... | collective-permute-start | bytes 2359304 | tf_op jit(solution)/shard_map/ppermute | solution.py:826
  29.2 31.5 %collective-permute-start.4 = (bf16[256,1536]{1,0:T(8,128)(2,1)S(1)}, bf16[256,1536]{1,0:T(8,128)(2,1)}, u32[]{:S(2)}, u32[]{:S(2)}) collective-permute-start(bf16[256,1536]{1,0:T(8,128)(2,1)S(1)} %copy-done.17), channel_id=1, source_target_pairs={{0,64},{1,0},{2,66},{3,2},{64,65},{65,1},{66,67},{67,3},{4,68},{5,... | collective-permute-start | bytes 2359304 | tf_op jit(solution)/shard_map/ppermute | solution.py:826
  57.2 3.5 %copy-start.22 = (bf16[256,1536]{1,0:T(8,128)(2,1)}, bf16[256,1536]{1,0:T(8,128)(2,1)S(1)}, u32[]{:S(2)}) copy-start(bf16[256,1536]{1,0:T(8,128)(2,1)S(1)} %collective-permute-done.2.refs_1_) | copy-start | bytes 2359300
  57.2 3.5 %copy-start.23 = (bf16[256,1536]{1,0:T(8,128)(2,1)}, bf16[256,1536]{1,0:T(8,128)(2,1)S(1)}, u32[]{:S(2)}) copy-start(bf16[256,1536]{1,0:T(8,128)(2,1)S(1)} %collective-permute-done.1.refs_0_) | copy-start | bytes 2359300
  57.2 15.1 %collective-permute-start.6 = (bf16[256,1536]{1,0:T(8,128)(2,1)}, bf16[256,1536]{1,0:T(8,128)(2,1)}, u32[]{:S(2)}, u32[]{:S(2)}) collective-permute-start(bf16[256,1536]{1,0:T(8,128)(2,1)} %cot_ref.1), channel_id=1, source_target_pairs={{0,0},{1,64},{2,2},{3,66},{64,1},{65,65},{66,3},{67,67},{4,4},{5,6... | collective-permute-start | bytes 2359304 | tf_op jit(solution)/shard_map/ppermute | solution.py:826
  60.7 0.7 copy-start.6
  66.8 54.9 %copy-start.1 = (bf16[1536,1024]{1,0:T(8,128)(2,1)}, bf16[1536,1024]{1,0:T(8,128)(2,1)S(1)}, u32[]{:S(2)}) copy-start(bf16[1536,1024]{1,0:T(8,128)(2,1)S(1)} %get-tuple-element.107.tokens_t_ref) | copy-start | bytes 9437188
  72.4 18.0 %copy-start.2 = (f32[8,1024]{1,0:T(8,128)S(1)}, f32[8,1024]{1,0:T(8,128)}, u32[]{:S(2)}) copy-start(f32[8,1024]{1,0:T(8,128)} %select_maximum_fusion.1.taps_ref) | copy-start | bytes 98308
  72.4 18.0 %copy-start.4 = (f32[1,768]{1,0:T(1,128)S(1)}, f32[1,768]{1,0:T(1,128)}, u32[]{:S(2)}) copy-start(f32[1,768]{1,0:T(1,128)} %broadcast_in_dim_reshape.3.skip_ref) | copy-start | bytes 9220
  72.4 7.4 %collective-permute-start.7 = (bf16[768,2688]{1,0:T(8,128)(2,1)}, bf16[768,2688]{1,0:T(8,128)(2,1)S(1)}, u32[]{:S(2)}, u32[]{:S(2)}) collective-permute-start(bf16[768,2688]{1,0:T(8,128)(2,1)} %bitcast.9.xm_ref.zm_ref.om_ref), channel_id=1, source_target_pairs={{0,1},{1,0},{2,3},{3,2},{4,5},{5,4},{6,7},{7,6},{8,9},{9,8},{10,11... | collective-permute-start | bytes 12386312 | tf_op jit(solution)/shard_map/ppermute | solution.py:836
  72.5 29.7 %collective-permute-start.10 = (bf16[256,1536]{1,0:T(8,128)(2,1)}, bf16[256,1536]{1,0:T(8,128)(2,1)S(1)}, u32[]{:S(2)}, u32[]{:S(2)}) collective-permute-start(bf16[256,1536]{1,0:T(8,128)(2,1)} %cot_ref.1), channel_id=1, source_target_pairs={{0,66},{1,2},{2,64},{3,0},{64,67},{65,3},{66,65},{67,1},{4,70},{5,... | collective-permute-start | bytes 2359304 | tf_op jit(solution)/shard_map/ppermute | solution.py:826
  73.9 28.3 %collective-permute-start.9 = (bf16[256,1536]{1,0:T(8,128)(2,1)}, bf16[256,1536]{1,0:T(8,128)(2,1)S(1)}, u32[]{:S(2)}, u32[]{:S(2)}) collective-permute-start(bf16[256,1536]{1,0:T(8,128)(2,1)} %cot_ref.1), channel_id=1, source_target_pairs={{0,64},{1,0},{2,66},{3,2},{64,65},{65,1},{66,67},{67,3},{4,68},{5,... | collective-permute-start | bytes 2359304 | tf_op jit(solution)/shard_map/ppermute | solution.py:826
  76.6 26.1 %collective-permute-start.8 = (bf16[256,1536]{1,0:T(8,128)(2,1)}, bf16[256,1536]{1,0:T(8,128)(2,1)S(1)}, u32[]{:S(2)}, u32[]{:S(2)}) collective-permute-start(bf16[256,1536]{1,0:T(8,128)(2,1)} %cot_ref.1), channel_id=1, source_target_pairs={{0,2},{1,66},{2,0},{3,64},{64,3},{65,67},{66,1},{67,65},{4,6},{5,7... | collective-permute-start | bytes 2359304 | tf_op jit(solution)/shard_map/ppermute | solution.py:826
  79.7 10.7 %copy-start = (bf16[768,2688]{1,0:T(8,128)(2,1)}, bf16[768,2688]{1,0:T(8,128)(2,1)S(1)}, u32[]{:S(2)}) copy-start(bf16[768,2688]{1,0:T(8,128)(2,1)S(1)} %collective-permute-done.7.xo_ref.zo_ref.oo_ref) | copy-start | bytes 12386308
  90.4 11.7 %copy-start.10 = (f32[1024,1152]{1,0:T(8,128)}, f32[1024,1152]{1,0:T(8,128)S(1)}, u32[]{:S(2)}) copy-start(f32[1024,1152]{1,0:T(8,128)S(1)} %get-tuple-element.112.pre_ref) | copy-start | bytes 14155780
  90.4 13.2 %copy-start.7 = (s32[6]{0:T(128)S(1)}, s32[6]{0:T(128)}, u32[]{:S(2)}) copy-start(s32[6]{0:T(128)} %stack.32.meta_ref) | copy-start | bytes 76
  102.1 0.9 copy-start.26
  102.2 1.2 copy-start.27
  102.7 0.9 copy-start.28
  114.0 4.8 %collective-permute-start.13 = (f32[8,1024]{1,0:T(8,128)S(1)}, f32[8,1024]{1,0:T(8,128)S(1)}, u32[]{:S(2)}, u32[]{:S(2)}) collective-permute-start(f32[8,1024]{1,0:T(8,128)S(1)} %get-tuple-element.128.s0), channel_id=1, source_target_pairs={{0,66},{1,67},{2,64},{3,65},{64,2},{65,3},{66,0},{67,1},{4,70},{5,... | collective-permute-start | bytes 98312 | tf_op jit(solution)/shard_map/ppermute | solution.py:826
  117.5 4.3 %collective-permute-start.12 = (f32[8,1024]{1,0:T(8,128)S(1)}, f32[8,1024]{1,0:T(8,128)S(1)}, u32[]{:S(2)}, u32[]{:S(2)}) collective-permute-start(f32[8,1024]{1,0:T(8,128)S(1)} %get-tuple-element.128.s0), channel_id=1, source_target_pairs={{0,64},{1,65},{2,66},{3,67},{64,0},{65,1},{66,2},{67,3},{4,68},{5,... | collective-permute-start | bytes 98312 | tf_op jit(solution)/shard_map/ppermute | solution.py:826
  117.5 4.3 %collective-permute-start.11 = (f32[8,1024]{1,0:T(8,128)S(1)}, f32[8,1024]{1,0:T(8,128)S(1)}, u32[]{:S(2)}, u32[]{:S(2)}) collective-permute-start(f32[8,1024]{1,0:T(8,128)S(1)} %get-tuple-element.128.s0), channel_id=1, source_target_pairs={{0,2},{1,3},{2,0},{3,1},{64,66},{65,67},{66,64},{67,65},{4,6},{5,7... | collective-permute-start | bytes 98312 | tf_op jit(solution)/shard_map/ppermute | solution.py:826
  131.7 10.0 %copy-start.9 = (f32[8,768]{1,0:T(8,128)}, f32[8,768]{1,0:T(8,128)S(1)}, u32[]{:S(2)}) copy-start(f32[8,768]{1,0:T(8,128)S(1)} %get-tuple-element.154) | copy-start | bytes 73732
  131.7 10.0 %collective-permute-start.14 = (bf16[16,2,48,768]{3,2,1,0:T(8,128)(2,1)}, bf16[16,2,48,768]{3,2,1,0:T(8,128)(2,1)S(1)}, u32[]{:S(2)}, u32[]{:S(2)}) collective-permute-start(bf16[16,2,48,768]{3,2,1,0:T(8,128)(2,1)} %get-tuple-element.133), channel_id=1, source_target_pairs={{0,1},{1,0},{2,3},{3,2},{4,5},{5,4},{6,7},{7,6},{8,9},{9,8},{10,11... | collective-permute-start | bytes 7077896 | tf_op jit(solution)/shard_map/ppermute | solution.py:836
  143.8 11.3 %copy-start.25 = (bf16[256,1536]{1,0:T(8,128)(2,1)S(1)}, bf16[256,1536]{1,0:T(8,128)(2,1)}, u32[]{:S(2)}) copy-start(bf16[256,1536]{1,0:T(8,128)(2,1)} %get-tuple-element.149) | copy-start | bytes 2359300
  143.8 11.4 %copy-start.24 = (bf16[256,1536]{1,0:T(8,128)(2,1)S(1)}, bf16[256,1536]{1,0:T(8,128)(2,1)}, u32[]{:S(2)}) copy-start(bf16[256,1536]{1,0:T(8,128)(2,1)} %get-tuple-element.150) | copy-start | bytes 2359300
  143.8 14.3 %copy-start.3 = (f32[8,1024]{1,0:T(8,128)S(1)}, f32[8,1024]{1,0:T(8,128)}, u32[]{:S(2)}) copy-start(f32[8,1024]{1,0:T(8,128)} %select_maximum_fusion.1.taps_ref) | copy-start | bytes 98308
  143.9 14.3 %copy-start.5 = (f32[1,768]{1,0:T(1,128)S(1)}, f32[1,768]{1,0:T(1,128)}, u32[]{:S(2)}) copy-start(f32[1,768]{1,0:T(1,128)} %broadcast_in_dim_reshape.3.skip_ref) | copy-start | bytes 9220
  143.9 68.0 %all-to-all-start.1 = ((bf16[16,2,48,768]{3,2,1,0:T(8,128)(2,1)}), bf16[16,2,48,768]{3,2,1,0:T(8,128)(2,1)}, u32[]{:S(2)}, u32[]{:S(2)}) async-start(bf16[16,2,48,768]{3,2,1,0:T(8,128)(2,1)} %add_convert_fusion), calls=%async_computation.1 | async-start | bytes 4718592 | tf_op jit(solution)/shard_map/all_to_all | solution.py:866
  150.9 45.8 %collective-permute-start.15 = (bf16[256,1536]{1,0:T(8,128)(2,1)}, bf16[256,1536]{1,0:T(8,128)(2,1)S(1)}, u32[]{:S(2)}, u32[]{:S(2)}) collective-permute-start(bf16[256,1536]{1,0:T(8,128)(2,1)} %get-tuple-element.147), channel_id=1, source_target_pairs={{0,0},{1,64},{2,2},{3,66},{64,1},{65,65},{66,3},{67,67},{4,4},{5,6... | collective-permute-start | bytes 2359304 | tf_op jit(solution)/shard_map/ppermute | solution.py:826
  155.0 41.7 %collective-permute-start.16 = (bf16[256,1536]{1,0:T(8,128)(2,1)}, bf16[256,1536]{1,0:T(8,128)(2,1)S(1)}, u32[]{:S(2)}, u32[]{:S(2)}) collective-permute-start(bf16[256,1536]{1,0:T(8,128)(2,1)} %get-tuple-element.148), channel_id=1, source_target_pairs={{0,2},{1,66},{2,0},{3,64},{64,3},{65,67},{66,1},{67,65},{4,6},{5,7... | collective-permute-start | bytes 2359304 | tf_op jit(solution)/shard_map/ppermute | solution.py:826
  155.1 41.6 %collective-permute-start.17 = (bf16[256,1536]{1,0:T(8,128)(2,1)S(1)}, bf16[256,1536]{1,0:T(8,128)(2,1)S(1)}, u32[]{:S(2)}, u32[]{:S(2)}) collective-permute-start(bf16[256,1536]{1,0:T(8,128)(2,1)S(1)} %copy-done.25), channel_id=1, source_target_pairs={{0,1},{1,65},{2,3},{3,67},{64,0},{65,64},{66,2},{67,66},{4,5},{5,6... | collective-permute-start | bytes 2359304 | tf_op jit(solution)/shard_map/ppermute | solution.py:826
  155.2 41.6 %collective-permute-start.18 = (bf16[256,1536]{1,0:T(8,128)(2,1)S(1)}, bf16[256,1536]{1,0:T(8,128)(2,1)S(1)}, u32[]{:S(2)}, u32[]{:S(2)}) collective-permute-start(bf16[256,1536]{1,0:T(8,128)(2,1)S(1)} %copy-done.24), channel_id=1, source_target_pairs={{0,3},{1,67},{2,1},{3,65},{64,2},{65,66},{66,0},{67,64},{4,7},{5,7... | collective-permute-start | bytes 2359304 | tf_op jit(solution)/shard_map/ppermute | solution.py:826
  158.2 26.8 %copy-start.8 = (s32[6]{0:T(128)S(1)}, s32[6]{0:T(128)}, u32[]{:S(2)}) copy-start(s32[6]{0:T(128)} %stack.32.meta_ref) | copy-start | bytes 76
  196.7 11.5 %copy-start.18 = (bf16[256,1536]{1,0:T(8,128)(2,1)}, bf16[256,1536]{1,0:T(8,128)(2,1)S(1)}, u32[]{:S(2)}) copy-start(bf16[256,1536]{1,0:T(8,128)(2,1)S(1)} %collective-permute-done.15.b0) | copy-start | bytes 2359300
  196.8 11.5 %copy-start.19 = (bf16[256,1536]{1,0:T(8,128)(2,1)}, bf16[256,1536]{1,0:T(8,128)(2,1)S(1)}, u32[]{:S(2)}) copy-start(bf16[256,1536]{1,0:T(8,128)(2,1)S(1)} %collective-permute-done.16.b1) | copy-start | bytes 2359300
  196.8 11.5 %copy-start.20 = (bf16[256,1536]{1,0:T(8,128)(2,1)}, bf16[256,1536]{1,0:T(8,128)(2,1)S(1)}, u32[]{:S(2)}) copy-start(bf16[256,1536]{1,0:T(8,128)(2,1)S(1)} %collective-permute-done.17.b2) | copy-start | bytes 2359300
  196.8 11.5 %copy-start.21 = (bf16[256,1536]{1,0:T(8,128)(2,1)}, bf16[256,1536]{1,0:T(8,128)(2,1)S(1)}, u32[]{:S(2)}) copy-start(bf16[256,1536]{1,0:T(8,128)(2,1)S(1)} %collective-permute-done.18.b3) | copy-start | bytes 2359300
  196.8 15.0 %collective-permute-start.19 = (bf16[256,1536]{1,0:T(8,128)(2,1)}, bf16[256,1536]{1,0:T(8,128)(2,1)S(1)}, u32[]{:S(2)}, u32[]{:S(2)}) collective-permute-start(bf16[256,1536]{1,0:T(8,128)(2,1)} %get-tuple-element.159), channel_id=1, source_target_pairs={{0,0},{1,64},{2,2},{3,66},{64,1},{65,65},{66,3},{67,67},{4,4},{5,6... | collective-permute-start | bytes 2359304 | tf_op jit(solution)/shard_map/ppermute | solution.py:826
  211.8 4.2 %copy-start.11 = (f32[768,1152]{1,0:T(8,128)S(1)}, f32[768,1152]{1,0:T(8,128)}, u32[]{:S(2)}) copy-start(f32[768,1152]{1,0:T(8,128)} %get-tuple-element.156) | copy-start | bytes 10616836
  211.8 4.0 %collective-permute-start.20 = (bf16[784,1152]{1,0:T(8,128)(2,1)}, bf16[784,1152]{1,0:T(8,128)(2,1)S(1)}, u32[]{:S(2)}, u32[]{:S(2)}) collective-permute-start(bf16[784,1152]{1,0:T(8,128)(2,1)} %get-tuple-element.160), channel_id=1, source_target_pairs={{0,1},{1,0},{2,3},{3,2},{4,5},{5,4},{6,7},{7,6},{8,9},{9,8},{10,11... | collective-permute-start | bytes 5419016 | tf_op jit(solution)/shard_map/ppermute | solution.py:836
  218.1 35.7 %all-to-all-start.2 = ((bf16[16,56,1152]{2,1,0:T(8,128)(2,1)}), bf16[16,56,1152]{2,1,0:T(8,128)(2,1)S(1)}, u32[]{:S(2)}, u32[]{:S(2)}) async-start(bf16[16,56,1152]{2,1,0:T(8,128)(2,1)} %pad_maximum_fusion), calls=%async_computation.2 | async-start | bytes 4128768 | tf_op jit(solution)/shard_map/all_to_all | solution.py:866
  225.0 32.9 %collective-permute-start.22 = (bf16[256,1536]{1,0:T(8,128)(2,1)}, bf16[256,1536]{1,0:T(8,128)(2,1)}, u32[]{:S(2)}, u32[]{:S(2)}) collective-permute-start(bf16[256,1536]{1,0:T(8,128)(2,1)} %get-tuple-element.170), channel_id=1, source_target_pairs={{0,2},{1,66},{2,0},{3,64},{64,3},{65,67},{66,1},{67,65},{4,6},{5,7... | collective-permute-start | bytes 2359304 | tf_op jit(solution)/shard_map/ppermute | solution.py:826
  225.7 33.3 %collective-permute-start.23 = (bf16[256,1536]{1,0:T(8,128)(2,1)}, bf16[256,1536]{1,0:T(8,128)(2,1)}, u32[]{:S(2)}, u32[]{:S(2)}) collective-permute-start(bf16[256,1536]{1,0:T(8,128)(2,1)} %get-tuple-element.171), channel_id=1, source_target_pairs={{0,1},{1,65},{2,3},{3,67},{64,0},{65,64},{66,2},{67,66},{4,5},{5,6... | collective-permute-start | bytes 2359304 | tf_op jit(solution)/shard_map/ppermute | solution.py:826
  226.4 34.9 %collective-permute-start.24 = (bf16[256,1536]{1,0:T(8,128)(2,1)}, bf16[256,1536]{1,0:T(8,128)(2,1)}, u32[]{:S(2)}, u32[]{:S(2)}) collective-permute-start(bf16[256,1536]{1,0:T(8,128)(2,1)} %get-tuple-element.172), channel_id=1, source_target_pairs={{0,3},{1,67},{2,1},{3,65},{64,2},{65,66},{66,0},{67,64},{4,7},{5,7... | collective-permute-start | bytes 2359304 | tf_op jit(solution)/shard_map/ppermute | solution.py:826
  230.2 23.6 %collective-permute-start.21 = (f32[2,48,768]{2,1,0:T(8,128)S(1)}, f32[2,48,768]{2,1,0:T(8,128)S(1)}, u32[]{:S(2)}, u32[]{:S(2)}) collective-permute-start(f32[2,48,768]{2,1,0:T(8,128)S(1)} %convert_reduce_fusion), channel_id=1, source_target_pairs={{0,0},{1,64},{2,2},{3,66},{64,1},{65,65},{66,3},{67,67},{4,4},{5,6... | collective-permute-start | bytes 884744 | tf_op jit(solution)/shard_map/ppermute | solution.py:826
  254.1 17.2 %collective-permute-start.29 = (f32[62,256]{1,0:T(8,128)S(1)}, f32[62,256]{1,0:T(8,128)S(1)}, u32[]{:S(2)}, u32[]{:S(2)}) collective-permute-start(f32[62,256]{1,0:T(8,128)S(1)} %get-tuple-element.178), channel_id=1, source_target_pairs={{0,3},{1,67},{2,1},{3,65},{64,2},{65,66},{66,0},{67,64},{4,7},{5,7... | collective-permute-start | bytes 190472 | tf_op jit(solution)/shard_map/ppermute | solution.py:826
  254.3 16.9 %collective-permute-start.28 = (f32[62,256]{1,0:T(8,128)S(1)}, f32[62,256]{1,0:T(8,128)S(1)}, u32[]{:S(2)}, u32[]{:S(2)}) collective-permute-start(f32[62,256]{1,0:T(8,128)S(1)} %get-tuple-element.178), channel_id=1, source_target_pairs={{0,1},{1,65},{2,3},{3,67},{64,0},{65,64},{66,2},{67,66},{4,5},{5,6... | collective-permute-start | bytes 190472 | tf_op jit(solution)/shard_map/ppermute | solution.py:826
  257.9 13.3 %collective-permute-start.27 = (f32[62,256]{1,0:T(8,128)S(1)}, f32[62,256]{1,0:T(8,128)S(1)}, u32[]{:S(2)}, u32[]{:S(2)}) collective-permute-start(f32[62,256]{1,0:T(8,128)S(1)} %get-tuple-element.178), channel_id=1, source_target_pairs={{0,2},{1,66},{2,0},{3,64},{64,3},{65,67},{66,1},{67,65},{4,6},{5,7... | collective-permute-start | bytes 190472 | tf_op jit(solution)/shard_map/ppermute | solution.py:826
  259.0 12.2 %collective-permute-start.26 = (f32[62,256]{1,0:T(8,128)S(1)}, f32[62,256]{1,0:T(8,128)S(1)}, u32[]{:S(2)}, u32[]{:S(2)}) collective-permute-start(f32[62,256]{1,0:T(8,128)S(1)} %get-tuple-element.178), channel_id=1, source_target_pairs={{0,0},{1,64},{2,2},{3,66},{64,1},{65,65},{66,3},{67,67},{4,4},{5,6... | collective-permute-start | bytes 190472 | tf_op jit(solution)/shard_map/ppermute | solution.py:826
  261.3 9.9 %collective-permute-start.25 = (f32[56,896]{1,0:T(8,128)S(1)}, f32[56,896]{1,0:T(8,128)S(1)}, u32[]{:S(2)}, u32[]{:S(2)}) collective-permute-start(f32[56,896]{1,0:T(8,128)S(1)} %get-tuple-element.177), channel_id=1, source_target_pairs={{0,0},{1,64},{2,2},{3,66},{64,1},{65,65},{66,3},{67,67},{4,4},{5,6... | collective-permute-start | bytes 602120 | tf_op jit(solution)/shard_map/ppermute | solution.py:826

commit v3 on v2

--- a/solution.py
+++ b/solution.py
@@ -14,7 +14,6 @@
 PLANE = ("y", "z")
 BF = jnp.bfloat16
 F32 = jnp.float32
-HI = lax.Precision.HIGHEST
 SPAN = 128
 LIMIT = 36
 
@@ -37,24 +36,26 @@
 
 def nt(left, right):
     return lax.dot_general(left, right, (((1,), (1,)), ((), ())), preferred_element_type=F32)
-
-
-def exact(left, right):
-    return lax.dot_general(
-        left, right, (((1,), (0,)), ((), ())), precision=HI, preferred_element_type=F32
-    )
-
-
-def exact_nt(left, right):
-    return lax.dot_general(
-        left, right, (((1,), (1,)), ((), ())), precision=HI, preferred_element_type=F32
-    )
 
 
 def halves(value):
     high = value.astype(BF)
     low = (value - high.astype(F32)).astype(BF)
     return high, low
+
+
+def running(mask, value):
+    high, low = halves(value)
+    return nn(jnp.concatenate([mask, mask], axis=1), jnp.concatenate([high, low], axis=0))
+
+
+def close_nt(left, right):
+    left_high, left_low = halves(left)
+    right_high, right_low = halves(right)
+    return nt(
+        jnp.concatenate([left_high, left_high, left_low], axis=1),
+        jnp.concatenate([right_high, right_low, right_high], axis=1),
+    )
 
 
 def expand(value, spread):
@@ -92,7 +93,7 @@
     xbc = conv * sig
     raw = pre_dt + head[1:2]
     step = softplus(raw)
-    decay = exact(tri, step * head[0:1])
+    decay = running(tri, step * head[0:1])
     last = decay[SPAN - 1 : SPAN]
     grown = expand(jnp.concatenate([step, jnp.exp(decay), jnp.exp(last - decay)], axis=0), spread)
     step_x, start_x, end_x = grown[:SPAN], grown[SPAN : 2 * SPAN], grown[2 * SPAN :]
@@ -114,7 +115,7 @@
     rows = lax.broadcasted_iota(jnp.int32, (SPAN, SPAN), 0)
     cols = lax.broadcasted_iota(jnp.int32, (SPAN, SPAN), 1)
     keep = rows >= cols
-    tri = jnp.where(keep, 1.0, 0.0).astype(F32)
+    tri = jnp.where(keep, 1.0, 0.0).astype(BF)
     spread = spread_ref[...]
     conv = conv_rows(ext_ref, taps_ref[...])
     conv_ref[...] = conv
@@ -129,7 +130,7 @@
     decay_t = decay.T
     scaled = x * step_x
     low = scaled.astype(BF)
-    scores = exact_nt(c, b)
+    scores = close_nt(c, b)
     state = state_ref[...]
     state_low = state.astype(BF)
     kept_ref[...] = state_low
@@ -169,8 +170,8 @@
 
     rows = lax.broadcasted_iota(jnp.int32, (SPAN, SPAN), 0)
     cols = lax.broadcasted_iota(jnp.int32, (SPAN, SPAN), 1)
-    tri = jnp.where(rows >= cols, 1.0, 0.0).astype(F32)
-    upper = jnp.where(cols >= rows, 1.0, 0.0).astype(F32)
+    tri = jnp.where(rows >= cols, 1.0, 0.0).astype(BF)
+    upper = jnp.where(cols >= rows, 1.0, 0.0).astype(BF)
     keep = cols >= rows
     spread = spread_ref[...]
     taps = taps_ref[...]
@@ -187,7 +188,7 @@
     decay_t = decay.T
     scaled = x * step_x
     low = scaled.astype(BF)
-    scores = exact_nt(b, c)
+    scores = close_nt(b, c)
     dy = dy_ref[...].astype(F32)
     dy_low = dy.astype(BF)
     kept = kept_ref[...]
@@ -233,7 +234,7 @@
     at_end = jnp.sum(pair_end, axis=0, keepdims=True) + through
     d_decay = into.T - out_of + pair_start - pair_end
     d_decay = d_decay + jnp.where(rows == SPAN - 1, at_end, 0.0)
-    d_log = exact(upper, d_decay)
+    d_log = running(upper, d_decay)
     d_step = by_head(d_scaled * x, spread) + d_log * head[0:1]
     d_raw = d_step * logistic(raw)
     dstate_ref[...] = dstate * start_x[SPAN - 1 : SPAN] + nn(c.T.astype(BF), dy_start_low)

time: 273 us -> 271 us (level)
  Pallas kernels: 113 us -> 109 us
    pallas_call x1, Pallas kernels: 26.8 us -> 24 us  [mixer_backward(): pl.pallas_call(backward_kernel, grid=(steps,), in_specs=[pl.BlockSpec((SP...]
  transfers between devices with their start and end apart: 33 -> 33, of which waited for: 11 -> 11; matrix products, arithmetic and copies ran while one was open for 2% -> 2% of each run, Pallas kernels for 33% -> 32%
where the time goes in v3:
time: 271 us; the launch traced here: 269 us
  Pallas kernels  109 us (40%)
  starting transfers between devices  78.1 us (29%)
  waiting for transfers between devices  66.7 us (25%)
  other arithmetic  7.35 us (3%)
  local copies, waits for them, and re-layouts  6.74 us (2%)
    ppermute x26, waiting for transfers between devices, permute(): return lax.ppermute(value, GROUP, moves(rule))  59.6 us
    ppermute x26, starting transfers between devices, permute(): return lax.ppermute(value, GROUP, moves(rule))  52.9 us
    pallas_call x1, Pallas kernels, mixer_backward(): pl.pallas_call(backward_kernel, grid=(steps,), in_specs=[pl.BlockSpec((SP...  24 us
    all_to_all x2, starting transfers between devices, exchange(): return lax.all_to_all(blocks, PLANE, 0, 0, tiled=True)  14 us
    pallas_call x1, Pallas kernels, project_back(): pl.pallas_call(project_back_kernel, grid=(2 * per,), in_specs=[pl.BlockSp...  11.8 us
    pallas_call x1, Pallas kernels, mixer_forward(): pl.pallas_call(forward_kernel, grid=(steps,), in_specs=[pl.BlockSpec((SPA...  10.9 us
    pallas_call x1, Pallas kernels, project(): pl.pallas_call(project_kernel, grid=(length // rows,), in_specs=[pl.Block...  10.7 us
    pallas_call x1, Pallas kernels, gate_back(): pl.pallas_call(functools.partial(gate_back_kernel, width_all), grid=(inne...  9.94 us
  transfers between devices with their start and end apart: 33, of which 11 were waited for; matrix products, arithmetic and copies ran while one was open for 2% of the time, Pallas kernels for 32%

profile of v3, /device:TPU:1, one launch (start us, length us, event | category | flops | bytes accessed | tf_op | source)
XLA Modules:
  0.0 269.2 jit_solution(11575740822081854542)
XLA Ops:
  0.7 1.1 pack_weights.1
  1.8 6.0 %collective-permute-start = (bf16[48,2688]{1,0:T(8,128)(2,1)S(1)}, bf16[48,2688]{1,0:T(8,128)(2,1)S(1)}, u32[]{:S(2)}, u32[]{:S(2)}) collective-permute-start(bf16[48,2688]{1,0:T(8,128)(2,1)S(1)} %pack_weights.1), channel_id=1, source_target_pairs={{0,0},{1,64},{2,2},{3,66},{64,1},{65,65},{66,3},{67,67},{4,4},{5,6... | collective-permute-start | bytes 774152 | tf_op jit(solution)/shard_map/ppermute | solution.py:827
  7.9 3.9 %collective-permute-done = bf16[48,2688]{1,0:T(8,128)(2,1)S(1)} collective-permute-done((bf16[48,2688]{1,0:T(8,128)(2,1)S(1)}, bf16[48,2688]{1,0:T(8,128)(2,1)S(1)}, u32[]{:S(2)}, u32[]{:S(2)}) %collective-permute-start) | collective-permute-done | bytes 258080 | tf_op jit(solution)/shard_map/ppermute | solution.py:827
  11.8 2.2 broadcast_in_dim.24
  14.1 7.9 %all-to-all-start = ((bf16[16,48,2688]{2,1,0:T(8,128)(2,1)}), bf16[16,48,2688]{2,1,0:T(8,128)(2,1)}, u32[]{:S(2)}, u32[]{:S(2)}) async-start(bf16[16,48,2688]{2,1,0:T(8,128)(2,1)} %broadcast_in_dim.24), calls=%async_computation | async-start | bytes 8257536 | tf_op jit(solution)/shard_map/all_to_all | solution.py:862
  22.1 3.3 %collective-permute-start.2 = (bf16[256,1536]{1,0:T(8,128)(2,1)S(1)}, bf16[256,1536]{1,0:T(8,128)(2,1)S(1)}, u32[]{:S(2)}, u32[]{:S(2)}) collective-permute-start(bf16[256,1536]{1,0:T(8,128)(2,1)S(1)} %copy-done.17), channel_id=1, source_target_pairs={{0,2},{1,66},{2,0},{3,64},{64,3},{65,67},{66,1},{67,65},{4,6},{5,7... | collective-permute-start | bytes 2359304 | tf_op jit(solution)/shard_map/ppermute | solution.py:827
  25.4 2.2 collective-permute-start.1
  27.9 0.6 stack.32.meta_ref
  28.5 0.7 collective-permute-start.5
  29.2 2.0 collective-permute-start.4
  31.4 0.7 broadcast_in_dim_reshape.3.skip_ref
  32.0 0.6 select_maximum_fusion.1.taps_ref
  32.7 24.6 %collective-permute-done.2.refs_1_ = bf16[256,1536]{1,0:T(8,128)(2,1)S(1)} collective-permute-done((bf16[256,1536]{1,0:T(8,128)(2,1)S(1)}, bf16[256,1536]{1,0:T(8,128)(2,1)S(1)}, u32[]{:S(2)}, u32[]{:S(2)}) %collective-permute-start.2) | collective-permute-done | bytes 786464 | tf_op jit(solution)/shard_map/ppermute | solution.py:827
  57.2 3.4 %collective-permute-start.6 = (bf16[256,1536]{1,0:T(8,128)(2,1)}, bf16[256,1536]{1,0:T(8,128)(2,1)}, u32[]{:S(2)}, u32[]{:S(2)}) collective-permute-start(bf16[256,1536]{1,0:T(8,128)(2,1)} %cot_ref.1), channel_id=1, source_target_pairs={{0,0},{1,64},{2,2},{3,66},{64,1},{65,65},{66,3},{67,67},{4,4},{5,6... | collective-permute-start | bytes 2359304 | tf_op jit(solution)/shard_map/ppermute | solution.py:827
  60.8 0.6 copy-done.6
  61.4 5.4 %place_normed.1 = (bf16[1024,1536]{1,0:T(8,128)(2,1)}, bf16[1536,1024]{1,0:T(8,128)(2,1)S(1)}) custom-call(s32[6]{0:T(128)S(1)} %copy-done.6, f32[1,1536]{1,0:T(1,128)S(1)} %broadcast_in_dim.23.gain_ref, bf16[256,1536]{1,0:T(8,128)(2,1)} %copy-done.23, bf16[256,1536]{1,0:T(8,128)(2,1)} %copy-done.22, bf16[256,1536]{1,0:T(8,128)(2,1)} %collective-permute-done.4.refs_2_, ...), custom_call_target="tpu_custom_call" | custom-call | flops 6899999744 | bytes 1024 | tf_op jit(solution)/shard_map/place_normed/pallas_call | solution.py:320
  66.8 5.6 %collective-permute-done.6.refs_0_ = bf16[256,1536]{1,0:T(8,128)(2,1)} collective-permute-done((bf16[256,1536]{1,0:T(8,128)(2,1)}, bf16[256,1536]{1,0:T(8,128)(2,1)}, u32[]{:S(2)}, u32[]{:S(2)}) %collective-permute-start.6) | collective-permute-done | bytes 786464 | tf_op jit(solution)/shard_map/ppermute | solution.py:827
  72.5 1.4 collective-permute-start.10
  73.9 2.8 %collective-permute-start.9 = (bf16[256,1536]{1,0:T(8,128)(2,1)}, bf16[256,1536]{1,0:T(8,128)(2,1)S(1)}, u32[]{:S(2)}, u32[]{:S(2)}) collective-permute-start(bf16[256,1536]{1,0:T(8,128)(2,1)} %cot_ref.1), channel_id=1, source_target_pairs={{0,64},{1,0},{2,66},{3,2},{64,65},{65,1},{66,67},{67,3},{4,68},{5,... | collective-permute-start | bytes 2359304 | tf_op jit(solution)/shard_map/ppermute | solution.py:827
  76.7 3.1 %collective-permute-done.7.xo_ref.zo_ref.oo_ref = bf16[768,2688]{1,0:T(8,128)(2,1)S(1)} collective-permute-done((bf16[768,2688]{1,0:T(8,128)(2,1)}, bf16[768,2688]{1,0:T(8,128)(2,1)S(1)}, u32[]{:S(2)}, u32[]{:S(2)}) %collective-permute-start.7) | collective-permute-done | bytes 4128800 | tf_op jit(solution)/shard_map/ppermute | solution.py:837
  79.7 10.7 %project_in.1 = (f32[1024,1152]{1,0:T(8,128)S(1)}, f32[1024,768]{1,0:T(8,128)S(1)}) custom-call(bf16[1024,1536]{1,0:T(8,128)(2,1)} %get-tuple-element.110.tokens_ref, bf16[768,2688]{1,0:T(8,128)(2,1)} %bitcast.9.xm_ref.zm_ref.om_ref, bf16[768,2688]{1,0:T(8,128)(2,1)S(1)} %collective-permute-done.7.xo_ref.zo_ref.oo_ref, ...), custom_call_target="tpu_custom_call" | custom-call | flops 6899999744 | bytes 1024 | tf_op jit(solution)/shard_map/project_in/pallas_call | solution.py:353
  90.4 10.9 %mixer_forward.1 = (f32[1024,768]{1,0:T(8,128)S(1)}, bf16[1024,768]{1,0:T(8,128)(2,1)}, f32[1024,1024]{1,0:T(8,128)}) custom-call(f32[1024,1152]{1,0:T(8,128)S(1)} %get-tuple-element.112.pre_ref, f32[8,1024]{1,0:T(8,128)S(1)} %copy-done.2, f32[8,128]{1,0:T(8,128)S(1)} %select_maximum_fusion.4.head_ref, f32[1,768]{1,0:T(1,128)S(1)} %copy-done.4, ...), custom_call_target="tpu_custom_call" | custom-call | flops 14949999616 | bytes 1024 | tf_op jit(solution)/shard_map/mixer_forward/pallas_call | solution.py:757
  101.4 1.3 collective-permute-done.8.refs_1_
  102.7 0.9 copy-done.28
  103.6 3.0 %place_cotangent.1 = (bf16[1024,1536]{1,0:T(8,128)(2,1)S(1)}, bf16[1536,1024]{1,0:T(8,128)(2,1)S(1)}) custom-call(s32[6]{0:T(128)S(1)} %copy-done.7, f32[1,1536]{1,0:T(1,128)S(1)} %broadcast_in_dim.23.gain_ref, bf16[256,1536]{1,0:T(8,128)(2,1)} %collective-permute-done.6.refs_0_, bf16[256,1536]{1,0:T(8,128)(2,1)} %copy-done.28, ...), custom_call_target="tpu_custom_call" | custom-call | flops 6899999744 | bytes 1024 | tf_op jit(solution)/shard_map/place_cotangent/pallas_call | solution.py:320
  106.6 7.4 %gate_sums.1 = (f32[1024,768]{1,0:T(8,128)S(1)}, f32[8,1024]{1,0:T(8,128)S(1)}) custom-call(bf16[1024,1536]{1,0:T(8,128)(2,1)S(1)} %get-tuple-element.124.cot_ref, bf16[768,2688]{1,0:T(8,128)(2,1)} %bitcast.9.xm_ref.zm_ref.om_ref, bf16[768,2688]{1,0:T(8,128)(2,1)} %copy-done, f32[1024,768]{1,0:T(8,128)S(1)} %get-tuple-element.125.y_ref, ...), custom_call_target="tpu_custom_call" | custom-call | flops 6899999744 | bytes 1024 | tf_op jit(solution)/shard_map/gate_sums/pallas_call | solution.py:400
  114.0 2.7 collective-permute-start.13
  116.7 0.7 collective-permute-start.11
  117.4 0.7 collective-permute-done.13.s3
  118.1 2.9 %collective-permute-done.12.s2 = f32[8,1024]{1,0:T(8,128)S(1)} collective-permute-done((f32[8,1024]{1,0:T(8,128)S(1)}, f32[8,1024]{1,0:T(8,128)S(1)}, u32[]{:S(2)}, u32[]{:S(2)}) %collective-permute-start.12) | collective-permute-done | bytes 32800 | tf_op jit(solution)/shard_map/ppermute | solution.py:827
  121.0 9.9 %gate_back.1 = (bf16[1024,768]{1,0:T(8,128)(2,1)}, bf16[1024,768]{1,0:T(8,128)(2,1)}, f32[1024,768]{1,0:T(8,128)}, f32[8,768]{1,0:T(8,128)S(1)}, bf16[16,2,48,76...) custom-call(f32[8,1024]{1,0:T(8,128)S(1)} %get-tuple-element.128.s0, f32[8,1024]{1,0:T(8,128)S(1)} %collective-permute-done.11.s1, ...), custom_call_target="tpu_custom_call" | custom-call | flops 13799999488 | bytes 1024 | tf_op jit(solution)/shard_map/gate_back/pallas_call | solution.py:456
  130.9 3.1 %collective-permute-start.14 = (bf16[16,2,48,768]{3,2,1,0:T(8,128)(2,1)}, bf16[16,2,48,768]{3,2,1,0:T(8,128)(2,1)S(1)}, u32[]{:S(2)}, u32[]{:S(2)}) collective-permute-start(bf16[16,2,48,768]{3,2,1,0:T(8,128)(2,1)} %get-tuple-element.133), channel_id=1, source_target_pairs={{0,1},{1,0},{2,3},{3,2},{4,5},{5,4},{6,7},{7,6},{8,9},{9,8},{10,11... | collective-permute-start | bytes 7077896 | tf_op jit(solution)/shard_map/ppermute | solution.py:837
  134.0 7.7 %project_out.1 = (bf16[256,1536]{1,0:T(8,128)(2,1)}, bf16[256,1536]{1,0:T(8,128)(2,1)}, bf16[256,1536]{1,0:T(8,128)(2,1)}, bf16[256,1536]{1,0:T(8,128)(2,1)}) custom-call(s32[6]{0:T(128)S(1)} %copy-done.7, bf16[1024,768]{1,0:T(8,128)(2,1)} %get-tuple-element.134.normed_ref, bf16[768,2688]{1,0:T(8,128)(2,1)} %bitcast.9.xm_ref.zm_ref.om_ref, ...), custom_call_target="tpu_custom_call" | custom-call | flops 6899999744 | bytes 1024 | tf_op jit(solution)/shard_map/project_out/pallas_call | solution.py:514
  141.7 2.2 add_convert_fusion
  143.9 7.1 %all-to-all-start.1 = ((bf16[16,2,48,768]{3,2,1,0:T(8,128)(2,1)}), bf16[16,2,48,768]{3,2,1,0:T(8,128)(2,1)}, u32[]{:S(2)}, u32[]{:S(2)}) async-start(bf16[16,2,48,768]{3,2,1,0:T(8,128)(2,1)} %add_convert_fusion), calls=%async_computation.1 | async-start | bytes 4718592 | tf_op jit(solution)/shard_map/all_to_all | solution.py:867
  150.9 3.8 %collective-permute-start.15 = (bf16[256,1536]{1,0:T(8,128)(2,1)}, bf16[256,1536]{1,0:T(8,128)(2,1)S(1)}, u32[]{:S(2)}, u32[]{:S(2)}) collective-permute-start(bf16[256,1536]{1,0:T(8,128)(2,1)} %get-tuple-element.147), channel_id=1, source_target_pairs={{0,0},{1,64},{2,2},{3,66},{64,1},{65,65},{66,3},{67,67},{4,4},{5,6... | collective-permute-start | bytes 2359304 | tf_op jit(solution)/shard_map/ppermute | solution.py:827
  154.8 0.3 collective-permute-start.16
  155.2 3.0 %collective-permute-start.18 = (bf16[256,1536]{1,0:T(8,128)(2,1)S(1)}, bf16[256,1536]{1,0:T(8,128)(2,1)S(1)}, u32[]{:S(2)}, u32[]{:S(2)}) collective-permute-start(bf16[256,1536]{1,0:T(8,128)(2,1)S(1)} %copy-done.24), channel_id=1, source_target_pairs={{0,3},{1,67},{2,1},{3,65},{64,2},{65,66},{66,0},{67,64},{4,7},{5,7... | collective-permute-start | bytes 2359304 | tf_op jit(solution)/shard_map/ppermute | solution.py:827
  158.2 24.0 %mixer_backward.1 = (bf16[1024,1152]{1,0:T(8,128)(2,1)S(1)}, f32[8,1024]{1,0:T(8,128)S(1)}, f32[8,128]{1,0:T(8,128)S(1)}) custom-call(f32[1024,1152]{1,0:T(8,128)} %copy-done.10, f32[1024,1024]{1,0:T(8,128)} %get-tuple-element.117.conv_ref, f32[1024,768]{1,0:T(8,128)} %get-tuple-element.139.dy_ref, bf16[1024,768]{1,0:T(8,128)(2,1)} %get-tuple-element.140.kept_ref, ...), custom_call_target="tpu_custom_call" | custom-call | flops 34500001792 | bytes 1024 | tf_op jit(solution)/shard_map/mixer_backward/pallas_call | solution.py:787
  182.2 11.8 %project_back.1 = (bf16[256,1536]{1,0:T(8,128)(2,1)}, bf16[256,1536]{1,0:T(8,128)(2,1)}, bf16[256,1536]{1,0:T(8,128)(2,1)}, bf16[256,1536]{1,0:T(8,128)(2,1)}, f32[8,1536]{1,0:T(8,128)S(1)}) custom-call(s32[6]{0:T(128)S(1)} %copy-done.8, bf16[1024,1152]{1,0:T(8,128)(2,1)S(1)} %get-tuple-element.151.late_ref, bf16[1024,768]{1,0:T(8,128)(2,1)} %get-tuple-element.142.gate_ref, ...), custom_call_target="tpu_custom_call" | custom-call | flops 575000000 | bytes 1024 | tf_op jit(solution)/shard_map/project_back/pallas_call | solution.py:557
  194.0 2.3 collective-permute-start.19
  196.3 0.7 slice.60
  197.1 8.4 %weight_grad.1 = (f32[768,1152]{1,0:T(8,128)}, bf16[784,1152]{1,0:T(8,128)(2,1)}) custom-call(bf16[1536,1024]{1,0:T(8,128)(2,1)} %copy-done.1, bf16[1024,1152]{1,0:T(8,128)(2,1)S(1)} %get-tuple-element.151.late_ref, f32[16,1152]{1,0:T(8,128)S(1)} %pad.29.vector_ref), custom_call_target="tpu_custom_call" | custom-call | flops 575000000 | bytes 1024 | tf_op jit(solution)/shard_map/weight_grad/pallas_call | solution.py:588
  205.5 3.5 %collective-permute-done.19.b0 = bf16[256,1536]{1,0:T(8,128)(2,1)S(1)} collective-permute-done((bf16[256,1536]{1,0:T(8,128)(2,1)}, bf16[256,1536]{1,0:T(8,128)(2,1)S(1)}, u32[]{:S(2)}, u32[]{:S(2)}) %collective-permute-start.19) | collective-permute-done | bytes 786464 | tf_op jit(solution)/shard_map/ppermute | solution.py:827
  209.1 4.0 %collective-permute-done.20 = bf16[784,1152]{1,0:T(8,128)(2,1)S(1)} collective-permute-done((bf16[784,1152]{1,0:T(8,128)(2,1)}, bf16[784,1152]{1,0:T(8,128)(2,1)S(1)}, u32[]{:S(2)}, u32[]{:S(2)}) %collective-permute-start.20) | collective-permute-done | bytes 1806368 | tf_op jit(solution)/shard_map/ppermute | solution.py:837
  213.0 0.2 convert_element_type.40
  213.3 0.6 fusion
  213.9 1.5 pad_maximum_fusion
  215.4 6.9 %all-to-all-start.2 = ((bf16[16,56,1152]{2,1,0:T(8,128)(2,1)}), bf16[16,56,1152]{2,1,0:T(8,128)(2,1)S(1)}, u32[]{:S(2)}, u32[]{:S(2)}) async-start(bf16[16,56,1152]{2,1,0:T(8,128)(2,1)} %pad_maximum_fusion), calls=%async_computation.2 | async-start | bytes 4128768 | tf_op jit(solution)/shard_map/all_to_all | solution.py:867
  222.3 0.7 collective-permute-start.22
  223.0 0.6 collective-permute-start.23
  223.6 1.8 collective-permute-start.24
  225.4 2.0 convert_reduce_fusion
  227.4 3.0 %collective-permute-start.21 = (f32[2,48,768]{2,1,0:T(8,128)S(1)}, f32[2,48,768]{2,1,0:T(8,128)S(1)}, u32[]{:S(2)}, u32[]{:S(2)}) collective-permute-start(f32[2,48,768]{2,1,0:T(8,128)S(1)} %convert_reduce_fusion), channel_id=1, source_target_pairs={{0,0},{1,64},{2,2},{3,66},{64,1},{65,65},{66,3},{67,67},{4,4},{5,6... | collective-permute-start | bytes 884744 | tf_op jit(solution)/shard_map/ppermute | solution.py:827
  230.4 3.5 %finish_output.1 = bf16[256,1536]{1,0:T(8,128)(2,1)} custom-call(s32[6]{0:T(128)S(1)} %copy-done.8, bf16[256,1536]{1,0:T(8,128)(2,1)} %copy-done.18, bf16[256,1536]{1,0:T(8,128)(2,1)} %copy-done.19, bf16[256,1536]{1,0:T(8,128)(2,1)} %copy-done.20, bf16[256,1536]{1,0:T(8,128)(2,1)} %copy-done.21, bf16[256,1536]{1,0:T(8,128)(2,1)} %hidden_ref.3), custom_call_target="tpu_custom_call" | custom-call | flops 3449999872 | bytes 1024 | tf_op jit(solution)/shard_map/finish_output/pallas_call | solution.py:708
  233.9 17.1 %collective-permute-done.21 = f32[2,48,768]{2,1,0:T(8,128)S(1)} collective-permute-done((f32[2,48,768]{2,1,0:T(8,128)S(1)}, f32[2,48,768]{2,1,0:T(8,128)S(1)}, u32[]{:S(2)}, u32[]{:S(2)}) %collective-permute-start.21) | collective-permute-done | bytes 294944 | tf_op jit(solution)/shard_map/ppermute | solution.py:827
  251.1 0.3 late_total.1
  251.5 3.6 %collective-permute-start.28 = (f32[62,256]{1,0:T(8,128)S(1)}, f32[62,256]{1,0:T(8,128)S(1)}, u32[]{:S(2)}, u32[]{:S(2)}) collective-permute-start(f32[62,256]{1,0:T(8,128)S(1)} %get-tuple-element.178), channel_id=1, source_target_pairs={{0,1},{1,65},{2,3},{3,67},{64,0},{65,64},{66,2},{67,66},{4,5},{5,6... | collective-permute-start | bytes 190472 | tf_op jit(solution)/shard_map/ppermute | solution.py:827
  255.2 1.1 collective-permute-start.27
  256.3 2.3 collective-permute-start.26
  258.6 4.8 %collective-permute-start.25 = (f32[56,896]{1,0:T(8,128)S(1)}, f32[56,896]{1,0:T(8,128)S(1)}, u32[]{:S(2)}, u32[]{:S(2)}) collective-permute-start(f32[56,896]{1,0:T(8,128)S(1)} %get-tuple-element.177), channel_id=1, source_target_pairs={{0,0},{1,64},{2,2},{3,66},{64,1},{65,65},{66,3},{67,67},{4,4},{5,6... | collective-permute-start | bytes 602120 | tf_op jit(solution)/shard_map/ppermute | solution.py:827
  263.4 4.4 %finish_input.1 = f32[256,1536]{1,0:T(8,128)} custom-call(s32[6]{0:T(128)S(1)} %copy-done.8, bf16[256,1536]{1,0:T(8,128)(2,1)S(1)} %collective-permute-done.19.b0, bf16[256,1536]{1,0:T(8,128)(2,1)} %collective-permute-done.22.b1, bf16[256,1536]{1,0:T(8,128)(2,1)} %collective-permute-done.23.b2, bf16[256,1536]{1,0:T(8,128)(2,1)} %collective-permute-done.24.b3, ...), custom_call_target="tpu_custom_call" | custom-call | flops 3449999872 | bytes 1024 | tf_op jit(solution)/shard_map/finish_input/pallas_call | solution.py:729
  267.8 0.7 slice_bitcast_fusion
  268.5 0.7 deliver_late.1
  (108 shorter events, 1.2 us)
Async XLA Ops:
  0.6 7.2 %copy-start.16 = (f32[3,12]{1,0:T(4,128)S(1)}, f32[3,12]{1,0:T(4,128)}, u32[]{:S(2)}) copy-start(f32[3,12]{1,0:T(4,128)} %param.21) | copy-start | bytes 436
  0.7 7.2 %copy-start.15 = (f32[768]{0:T(1024)S(1)}, f32[768]{0:T(1024)}, u32[]{:S(2)}) copy-start(f32[768]{0:T(1024)} %param.22) | copy-start | bytes 9220
  0.7 7.2 %copy-start.12 = (f32[5,768]{1,0:T(8,128)S(1)}, f32[5,768]{1,0:T(8,128)}, u32[]{:S(2)}) copy-start(f32[5,768]{1,0:T(8,128)} %param.19) | copy-start | bytes 46084
  1.8 10.0 %collective-permute-start = (bf16[48,2688]{1,0:T(8,128)(2,1)S(1)}, bf16[48,2688]{1,0:T(8,128)(2,1)S(1)}, u32[]{:S(2)}, u32[]{:S(2)}) collective-permute-start(bf16[48,2688]{1,0:T(8,128)(2,1)S(1)} %pack_weights.1), channel_id=1, source_target_pairs={{0,0},{1,64},{2,2},{3,66},{64,1},{65,65},{66,3},{67,67},{4,4},{5,6... | collective-permute-start | bytes 774152 | tf_op jit(solution)/shard_map/ppermute | solution.py:827
  14.1 8.0 %copy-start.17 = (bf16[256,1536]{1,0:T(8,128)(2,1)S(1)}, bf16[256,1536]{1,0:T(8,128)(2,1)}, u32[]{:S(2)}) copy-start(bf16[256,1536]{1,0:T(8,128)(2,1)} %hidden_ref.3) | copy-start | bytes 2359300
  14.1 13.8 %copy-start.13 = (f32[1536]{0:T(1024)S(1)}, f32[1536]{0:T(1024)}, u32[]{:S(2)}) copy-start(f32[1536]{0:T(1024)} %param.14) | copy-start | bytes 18436
  14.1 18.0 %copy-start.14 = (f32[5,256]{1,0:T(8,128)S(1)}, f32[5,256]{1,0:T(8,128)}, u32[]{:S(2)}) copy-start(f32[5,256]{1,0:T(8,128)} %param.20) | copy-start | bytes 15364
  14.1 58.3 %all-to-all-start = ((bf16[16,48,2688]{2,1,0:T(8,128)(2,1)}), bf16[16,48,2688]{2,1,0:T(8,128)(2,1)}, u32[]{:S(2)}, u32[]{:S(2)}) async-start(bf16[16,48,2688]{2,1,0:T(8,128)(2,1)} %broadcast_in_dim.24), calls=%async_computation | async-start | bytes 8257536 | tf_op jit(solution)/shard_map/all_to_all | solution.py:862
  22.1 35.2 %collective-permute-start.2 = (bf16[256,1536]{1,0:T(8,128)(2,1)S(1)}, bf16[256,1536]{1,0:T(8,128)(2,1)S(1)}, u32[]{:S(2)}, u32[]{:S(2)}) collective-permute-start(bf16[256,1536]{1,0:T(8,128)(2,1)S(1)} %copy-done.17), channel_id=1, source_target_pairs={{0,2},{1,66},{2,0},{3,64},{64,3},{65,67},{66,1},{67,65},{4,6},{5,7... | collective-permute-start | bytes 2359304 | tf_op jit(solution)/shard_map/ppermute | solution.py:827
  25.4 31.8 %collective-permute-start.1 = (bf16[256,1536]{1,0:T(8,128)(2,1)S(1)}, bf16[256,1536]{1,0:T(8,128)(2,1)S(1)}, u32[]{:S(2)}, u32[]{:S(2)}) collective-permute-start(bf16[256,1536]{1,0:T(8,128)(2,1)S(1)} %copy-done.17), channel_id=1, source_target_pairs={{0,0},{1,64},{2,2},{3,66},{64,1},{65,65},{66,3},{67,67},{4,4},{5,6... | collective-permute-start | bytes 2359304 | tf_op jit(solution)/shard_map/ppermute | solution.py:827
  27.6 3.6 %collective-permute-start.3 = (f32[16,768]{1,0:T(8,128)S(1)}, f32[16,768]{1,0:T(8,128)S(1)}, u32[]{:S(2)}, u32[]{:S(2)}) collective-permute-start(f32[16,768]{1,0:T(8,128)S(1)} %select_maximum_fusion), channel_id=1, source_target_pairs={{0,1},{1,0},{2,3},{3,2},{4,5},{5,4},{6,7},{7,6},{8,9},{9,8},{10,11... | collective-permute-start | bytes 147464 | tf_op jit(solution)/shard_map/ppermute | solution.py:837
  28.5 32.2 %collective-permute-start.5 = (bf16[256,1536]{1,0:T(8,128)(2,1)S(1)}, bf16[256,1536]{1,0:T(8,128)(2,1)}, u32[]{:S(2)}, u32[]{:S(2)}) collective-permute-start(bf16[256,1536]{1,0:T(8,128)(2,1)S(1)} %copy-done.17), channel_id=1, source_target_pairs={{0,66},{1,2},{2,64},{3,0},{64,67},{65,3},{66,65},{67,1},{4,70},{5,... | collective-permute-start | bytes 2359304 | tf_op jit(solution)/shard_map/ppermute | solution.py:827
  29.2 31.5 %collective-permute-start.4 = (bf16[256,1536]{1,0:T(8,128)(2,1)S(1)}, bf16[256,1536]{1,0:T(8,128)(2,1)}, u32[]{:S(2)}, u32[]{:S(2)}) collective-permute-start(bf16[256,1536]{1,0:T(8,128)(2,1)S(1)} %copy-done.17), channel_id=1, source_target_pairs={{0,64},{1,0},{2,66},{3,2},{64,65},{65,1},{66,67},{67,3},{4,68},{5,... | collective-permute-start | bytes 2359304 | tf_op jit(solution)/shard_map/ppermute | solution.py:827
  57.2 3.5 %copy-start.22 = (bf16[256,1536]{1,0:T(8,128)(2,1)}, bf16[256,1536]{1,0:T(8,128)(2,1)S(1)}, u32[]{:S(2)}) copy-start(bf16[256,1536]{1,0:T(8,128)(2,1)S(1)} %collective-permute-done.2.refs_1_) | copy-start | bytes 2359300
  57.2 3.5 %copy-start.23 = (bf16[256,1536]{1,0:T(8,128)(2,1)}, bf16[256,1536]{1,0:T(8,128)(2,1)S(1)}, u32[]{:S(2)}) copy-start(bf16[256,1536]{1,0:T(8,128)(2,1)S(1)} %collective-permute-done.1.refs_0_) | copy-start | bytes 2359300
  57.2 15.1 %collective-permute-start.6 = (bf16[256,1536]{1,0:T(8,128)(2,1)}, bf16[256,1536]{1,0:T(8,128)(2,1)}, u32[]{:S(2)}, u32[]{:S(2)}) collective-permute-start(bf16[256,1536]{1,0:T(8,128)(2,1)} %cot_ref.1), channel_id=1, source_target_pairs={{0,0},{1,64},{2,2},{3,66},{64,1},{65,65},{66,3},{67,67},{4,4},{5,6... | collective-permute-start | bytes 2359304 | tf_op jit(solution)/shard_map/ppermute | solution.py:827
  60.7 0.7 copy-start.6
  66.8 54.1 %copy-start.1 = (bf16[1536,1024]{1,0:T(8,128)(2,1)}, bf16[1536,1024]{1,0:T(8,128)(2,1)S(1)}, u32[]{:S(2)}) copy-start(bf16[1536,1024]{1,0:T(8,128)(2,1)S(1)} %get-tuple-element.107.tokens_t_ref) | copy-start | bytes 9437188
  72.4 18.0 %copy-start.2 = (f32[8,1024]{1,0:T(8,128)S(1)}, f32[8,1024]{1,0:T(8,128)}, u32[]{:S(2)}) copy-start(f32[8,1024]{1,0:T(8,128)} %select_maximum_fusion.1.taps_ref) | copy-start | bytes 98308
  72.4 18.0 %copy-start.4 = (f32[1,768]{1,0:T(1,128)S(1)}, f32[1,768]{1,0:T(1,128)}, u32[]{:S(2)}) copy-start(f32[1,768]{1,0:T(1,128)} %broadcast_in_dim_reshape.3.skip_ref) | copy-start | bytes 9220
  72.4 7.4 %collective-permute-start.7 = (bf16[768,2688]{1,0:T(8,128)(2,1)}, bf16[768,2688]{1,0:T(8,128)(2,1)S(1)}, u32[]{:S(2)}, u32[]{:S(2)}) collective-permute-start(bf16[768,2688]{1,0:T(8,128)(2,1)} %bitcast.9.xm_ref.zm_ref.om_ref), channel_id=1, source_target_pairs={{0,1},{1,0},{2,3},{3,2},{4,5},{5,4},{6,7},{7,6},{8,9},{9,8},{10,11... | collective-permute-start | bytes 12386312 | tf_op jit(solution)/shard_map/ppermute | solution.py:837
  72.5 28.9 %collective-permute-start.10 = (bf16[256,1536]{1,0:T(8,128)(2,1)}, bf16[256,1536]{1,0:T(8,128)(2,1)S(1)}, u32[]{:S(2)}, u32[]{:S(2)}) collective-permute-start(bf16[256,1536]{1,0:T(8,128)(2,1)} %cot_ref.1), channel_id=1, source_target_pairs={{0,66},{1,2},{2,64},{3,0},{64,67},{65,3},{66,65},{67,1},{4,70},{5,... | collective-permute-start | bytes 2359304 | tf_op jit(solution)/shard_map/ppermute | solution.py:827
  73.9 27.5 %collective-permute-start.9 = (bf16[256,1536]{1,0:T(8,128)(2,1)}, bf16[256,1536]{1,0:T(8,128)(2,1)S(1)}, u32[]{:S(2)}, u32[]{:S(2)}) collective-permute-start(bf16[256,1536]{1,0:T(8,128)(2,1)} %cot_ref.1), channel_id=1, source_target_pairs={{0,64},{1,0},{2,66},{3,2},{64,65},{65,1},{66,67},{67,3},{4,68},{5,... | collective-permute-start | bytes 2359304 | tf_op jit(solution)/shard_map/ppermute | solution.py:827
  76.6 26.1 %collective-permute-start.8 = (bf16[256,1536]{1,0:T(8,128)(2,1)}, bf16[256,1536]{1,0:T(8,128)(2,1)S(1)}, u32[]{:S(2)}, u32[]{:S(2)}) collective-permute-start(bf16[256,1536]{1,0:T(8,128)(2,1)} %cot_ref.1), channel_id=1, source_target_pairs={{0,2},{1,66},{2,0},{3,64},{64,3},{65,67},{66,1},{67,65},{4,6},{5,7... | collective-permute-start | bytes 2359304 | tf_op jit(solution)/shard_map/ppermute | solution.py:827
  79.7 10.7 %copy-start = (bf16[768,2688]{1,0:T(8,128)(2,1)}, bf16[768,2688]{1,0:T(8,128)(2,1)S(1)}, u32[]{:S(2)}) copy-start(bf16[768,2688]{1,0:T(8,128)(2,1)S(1)} %collective-permute-done.7.xo_ref.zo_ref.oo_ref) | copy-start | bytes 12386308
  90.4 10.9 %copy-start.10 = (f32[1024,1152]{1,0:T(8,128)}, f32[1024,1152]{1,0:T(8,128)S(1)}, u32[]{:S(2)}) copy-start(f32[1024,1152]{1,0:T(8,128)S(1)} %get-tuple-element.112.pre_ref) | copy-start | bytes 14155780
  90.4 13.2 %copy-start.7 = (s32[6]{0:T(128)S(1)}, s32[6]{0:T(128)}, u32[]{:S(2)}) copy-start(s32[6]{0:T(128)} %stack.32.meta_ref) | copy-start | bytes 76
  101.3 1.4 copy-start.26
  101.4 1.3 copy-start.27
  102.7 0.9 copy-start.28
  114.0 4.1 %collective-permute-start.13 = (f32[8,1024]{1,0:T(8,128)S(1)}, f32[8,1024]{1,0:T(8,128)S(1)}, u32[]{:S(2)}, u32[]{:S(2)}) collective-permute-start(f32[8,1024]{1,0:T(8,128)S(1)} %get-tuple-element.128.s0), channel_id=1, source_target_pairs={{0,66},{1,67},{2,64},{3,65},{64,2},{65,3},{66,0},{67,1},{4,70},{5,... | collective-permute-start | bytes 98312 | tf_op jit(solution)/shard_map/ppermute | solution.py:827
  116.7 4.3 %collective-permute-start.12 = (f32[8,1024]{1,0:T(8,128)S(1)}, f32[8,1024]{1,0:T(8,128)S(1)}, u32[]{:S(2)}, u32[]{:S(2)}) collective-permute-start(f32[8,1024]{1,0:T(8,128)S(1)} %get-tuple-element.128.s0), channel_id=1, source_target_pairs={{0,64},{1,65},{2,66},{3,67},{64,0},{65,1},{66,2},{67,3},{4,68},{5,... | collective-permute-start | bytes 98312 | tf_op jit(solution)/shard_map/ppermute | solution.py:827
  116.7 4.3 %collective-permute-start.11 = (f32[8,1024]{1,0:T(8,128)S(1)}, f32[8,1024]{1,0:T(8,128)S(1)}, u32[]{:S(2)}, u32[]{:S(2)}) collective-permute-start(f32[8,1024]{1,0:T(8,128)S(1)} %get-tuple-element.128.s0), channel_id=1, source_target_pairs={{0,2},{1,3},{2,0},{3,1},{64,66},{65,67},{66,64},{67,65},{4,6},{5,7... | collective-permute-start | bytes 98312 | tf_op jit(solution)/shard_map/ppermute | solution.py:827
  130.9 10.8 %copy-start.9 = (f32[8,768]{1,0:T(8,128)}, f32[8,768]{1,0:T(8,128)S(1)}, u32[]{:S(2)}) copy-start(f32[8,768]{1,0:T(8,128)S(1)} %get-tuple-element.154) | copy-start | bytes 73732
  130.9 10.8 %collective-permute-start.14 = (bf16[16,2,48,768]{3,2,1,0:T(8,128)(2,1)}, bf16[16,2,48,768]{3,2,1,0:T(8,128)(2,1)S(1)}, u32[]{:S(2)}, u32[]{:S(2)}) collective-permute-start(bf16[16,2,48,768]{3,2,1,0:T(8,128)(2,1)} %get-tuple-element.133), channel_id=1, source_target_pairs={{0,1},{1,0},{2,3},{3,2},{4,5},{5,4},{6,7},{7,6},{8,9},{9,8},{10,11... | collective-permute-start | bytes 7077896 | tf_op jit(solution)/shard_map/ppermute | solution.py:837
  143.8 11.3 %copy-start.25 = (bf16[256,1536]{1,0:T(8,128)(2,1)S(1)}, bf16[256,1536]{1,0:T(8,128)(2,1)}, u32[]{:S(2)}) copy-start(bf16[256,1536]{1,0:T(8,128)(2,1)} %get-tuple-element.149) | copy-start | bytes 2359300
  143.8 11.4 %copy-start.24 = (bf16[256,1536]{1,0:T(8,128)(2,1)S(1)}, bf16[256,1536]{1,0:T(8,128)(2,1)}, u32[]{:S(2)}) copy-start(bf16[256,1536]{1,0:T(8,128)(2,1)} %get-tuple-element.150) | copy-start | bytes 2359300
  143.8 14.3 %copy-start.3 = (f32[8,1024]{1,0:T(8,128)S(1)}, f32[8,1024]{1,0:T(8,128)}, u32[]{:S(2)}) copy-start(f32[8,1024]{1,0:T(8,128)} %select_maximum_fusion.1.taps_ref) | copy-start | bytes 98308
  143.9 14.3 %copy-start.5 = (f32[1,768]{1,0:T(1,128)S(1)}, f32[1,768]{1,0:T(1,128)}, u32[]{:S(2)}) copy-start(f32[1,768]{1,0:T(1,128)} %broadcast_in_dim_reshape.3.skip_ref) | copy-start | bytes 9220
  143.9 65.2 %all-to-all-start.1 = ((bf16[16,2,48,768]{3,2,1,0:T(8,128)(2,1)}), bf16[16,2,48,768]{3,2,1,0:T(8,128)(2,1)}, u32[]{:S(2)}, u32[]{:S(2)}) async-start(bf16[16,2,48,768]{3,2,1,0:T(8,128)(2,1)} %add_convert_fusion), calls=%async_computation.1 | async-start | bytes 4718592 | tf_op jit(solution)/shard_map/all_to_all | solution.py:867
  150.9 43.0 %collective-permute-start.15 = (bf16[256,1536]{1,0:T(8,128)(2,1)}, bf16[256,1536]{1,0:T(8,128)(2,1)S(1)}, u32[]{:S(2)}, u32[]{:S(2)}) collective-permute-start(bf16[256,1536]{1,0:T(8,128)(2,1)} %get-tuple-element.147), channel_id=1, source_target_pairs={{0,0},{1,64},{2,2},{3,66},{64,1},{65,65},{66,3},{67,67},{4,4},{5,6... | collective-permute-start | bytes 2359304 | tf_op jit(solution)/shard_map/ppermute | solution.py:827
  154.8 39.2 %collective-permute-start.16 = (bf16[256,1536]{1,0:T(8,128)(2,1)}, bf16[256,1536]{1,0:T(8,128)(2,1)S(1)}, u32[]{:S(2)}, u32[]{:S(2)}) collective-permute-start(bf16[256,1536]{1,0:T(8,128)(2,1)} %get-tuple-element.148), channel_id=1, source_target_pairs={{0,2},{1,66},{2,0},{3,64},{64,3},{65,67},{66,1},{67,65},{4,6},{5,7... | collective-permute-start | bytes 2359304 | tf_op jit(solution)/shard_map/ppermute | solution.py:827
  155.1 38.9 %collective-permute-start.17 = (bf16[256,1536]{1,0:T(8,128)(2,1)S(1)}, bf16[256,1536]{1,0:T(8,128)(2,1)S(1)}, u32[]{:S(2)}, u32[]{:S(2)}) collective-permute-start(bf16[256,1536]{1,0:T(8,128)(2,1)S(1)} %copy-done.25), channel_id=1, source_target_pairs={{0,1},{1,65},{2,3},{3,67},{64,0},{65,64},{66,2},{67,66},{4,5},{5,6... | collective-permute-start | bytes 2359304 | tf_op jit(solution)/shard_map/ppermute | solution.py:827
  155.2 38.8 %collective-permute-start.18 = (bf16[256,1536]{1,0:T(8,128)(2,1)S(1)}, bf16[256,1536]{1,0:T(8,128)(2,1)S(1)}, u32[]{:S(2)}, u32[]{:S(2)}) collective-permute-start(bf16[256,1536]{1,0:T(8,128)(2,1)S(1)} %copy-done.24), channel_id=1, source_target_pairs={{0,3},{1,67},{2,1},{3,65},{64,2},{65,66},{66,0},{67,64},{4,7},{5,7... | collective-permute-start | bytes 2359304 | tf_op jit(solution)/shard_map/ppermute | solution.py:827
  158.2 24.0 %copy-start.8 = (s32[6]{0:T(128)S(1)}, s32[6]{0:T(128)}, u32[]{:S(2)}) copy-start(s32[6]{0:T(128)} %stack.32.meta_ref) | copy-start | bytes 76
  194.0 11.6 %copy-start.18 = (bf16[256,1536]{1,0:T(8,128)(2,1)}, bf16[256,1536]{1,0:T(8,128)(2,1)S(1)}, u32[]{:S(2)}) copy-start(bf16[256,1536]{1,0:T(8,128)(2,1)S(1)} %collective-permute-done.15.b0) | copy-start | bytes 2359300
  194.0 11.5 %copy-start.19 = (bf16[256,1536]{1,0:T(8,128)(2,1)}, bf16[256,1536]{1,0:T(8,128)(2,1)S(1)}, u32[]{:S(2)}) copy-start(bf16[256,1536]{1,0:T(8,128)(2,1)S(1)} %collective-permute-done.16.b1) | copy-start | bytes 2359300
  194.0 11.5 %copy-start.20 = (bf16[256,1536]{1,0:T(8,128)(2,1)}, bf16[256,1536]{1,0:T(8,128)(2,1)S(1)}, u32[]{:S(2)}) copy-start(bf16[256,1536]{1,0:T(8,128)(2,1)S(1)} %collective-permute-done.17.b2) | copy-start | bytes 2359300
  194.0 11.5 %copy-start.21 = (bf16[256,1536]{1,0:T(8,128)(2,1)}, bf16[256,1536]{1,0:T(8,128)(2,1)S(1)}, u32[]{:S(2)}) copy-start(bf16[256,1536]{1,0:T(8,128)(2,1)S(1)} %collective-permute-done.18.b3) | copy-start | bytes 2359300
  194.0 15.0 %collective-permute-start.19 = (bf16[256,1536]{1,0:T(8,128)(2,1)}, bf16[256,1536]{1,0:T(8,128)(2,1)S(1)}, u32[]{:S(2)}, u32[]{:S(2)}) collective-permute-start(bf16[256,1536]{1,0:T(8,128)(2,1)} %get-tuple-element.159), channel_id=1, source_target_pairs={{0,0},{1,64},{2,2},{3,66},{64,1},{65,65},{66,3},{67,67},{4,4},{5,6... | collective-permute-start | bytes 2359304 | tf_op jit(solution)/shard_map/ppermute | solution.py:827
  209.1 4.2 %copy-start.11 = (f32[768,1152]{1,0:T(8,128)S(1)}, f32[768,1152]{1,0:T(8,128)}, u32[]{:S(2)}) copy-start(f32[768,1152]{1,0:T(8,128)} %get-tuple-element.156) | copy-start | bytes 10616836
  209.1 4.0 %collective-permute-start.20 = (bf16[784,1152]{1,0:T(8,128)(2,1)}, bf16[784,1152]{1,0:T(8,128)(2,1)S(1)}, u32[]{:S(2)}, u32[]{:S(2)}) collective-permute-start(bf16[784,1152]{1,0:T(8,128)(2,1)} %get-tuple-element.160), channel_id=1, source_target_pairs={{0,1},{1,0},{2,3},{3,2},{4,5},{5,4},{6,7},{7,6},{8,9},{9,8},{10,11... | collective-permute-start | bytes 5419016 | tf_op jit(solution)/shard_map/ppermute | solution.py:837
  215.4 35.7 %all-to-all-start.2 = ((bf16[16,56,1152]{2,1,0:T(8,128)(2,1)}), bf16[16,56,1152]{2,1,0:T(8,128)(2,1)S(1)}, u32[]{:S(2)}, u32[]{:S(2)}) async-start(bf16[16,56,1152]{2,1,0:T(8,128)(2,1)} %pad_maximum_fusion), calls=%async_computation.2 | async-start | bytes 4128768 | tf_op jit(solution)/shard_map/all_to_all | solution.py:867
  222.3 32.9 %collective-permute-start.22 = (bf16[256,1536]{1,0:T(8,128)(2,1)}, bf16[256,1536]{1,0:T(8,128)(2,1)}, u32[]{:S(2)}, u32[]{:S(2)}) collective-permute-start(bf16[256,1536]{1,0:T(8,128)(2,1)} %get-tuple-element.170), channel_id=1, source_target_pairs={{0,2},{1,66},{2,0},{3,64},{64,3},{65,67},{66,1},{67,65},{4,6},{5,7... | collective-permute-start | bytes 2359304 | tf_op jit(solution)/shard_map/ppermute | solution.py:827
  223.0 33.3 %collective-permute-start.23 = (bf16[256,1536]{1,0:T(8,128)(2,1)}, bf16[256,1536]{1,0:T(8,128)(2,1)}, u32[]{:S(2)}, u32[]{:S(2)}) collective-permute-start(bf16[256,1536]{1,0:T(8,128)(2,1)} %get-tuple-element.171), channel_id=1, source_target_pairs={{0,1},{1,65},{2,3},{3,67},{64,0},{65,64},{66,2},{67,66},{4,5},{5,6... | collective-permute-start | bytes 2359304 | tf_op jit(solution)/shard_map/ppermute | solution.py:827
  223.6 34.9 %collective-permute-start.24 = (bf16[256,1536]{1,0:T(8,128)(2,1)}, bf16[256,1536]{1,0:T(8,128)(2,1)}, u32[]{:S(2)}, u32[]{:S(2)}) collective-permute-start(bf16[256,1536]{1,0:T(8,128)(2,1)} %get-tuple-element.172), channel_id=1, source_target_pairs={{0,3},{1,67},{2,1},{3,65},{64,2},{65,66},{66,0},{67,64},{4,7},{5,7... | collective-permute-start | bytes 2359304 | tf_op jit(solution)/shard_map/ppermute | solution.py:827
  227.4 23.6 %collective-permute-start.21 = (f32[2,48,768]{2,1,0:T(8,128)S(1)}, f32[2,48,768]{2,1,0:T(8,128)S(1)}, u32[]{:S(2)}, u32[]{:S(2)}) collective-permute-start(f32[2,48,768]{2,1,0:T(8,128)S(1)} %convert_reduce_fusion), channel_id=1, source_target_pairs={{0,0},{1,64},{2,2},{3,66},{64,1},{65,65},{66,3},{67,67},{4,4},{5,6... | collective-permute-start | bytes 884744 | tf_op jit(solution)/shard_map/ppermute | solution.py:827
  251.3 17.2 %collective-permute-start.29 = (f32[62,256]{1,0:T(8,128)S(1)}, f32[62,256]{1,0:T(8,128)S(1)}, u32[]{:S(2)}, u32[]{:S(2)}) collective-permute-start(f32[62,256]{1,0:T(8,128)S(1)} %get-tuple-element.178), channel_id=1, source_target_pairs={{0,3},{1,67},{2,1},{3,65},{64,2},{65,66},{66,0},{67,64},{4,7},{5,7... | collective-permute-start | bytes 190472 | tf_op jit(solution)/shard_map/ppermute | solution.py:827
  251.5 17.0 %collective-permute-start.28 = (f32[62,256]{1,0:T(8,128)S(1)}, f32[62,256]{1,0:T(8,128)S(1)}, u32[]{:S(2)}, u32[]{:S(2)}) collective-permute-start(f32[62,256]{1,0:T(8,128)S(1)} %get-tuple-element.178), channel_id=1, source_target_pairs={{0,1},{1,65},{2,3},{3,67},{64,0},{65,64},{66,2},{67,66},{4,5},{5,6... | collective-permute-start | bytes 190472 | tf_op jit(solution)/shard_map/ppermute | solution.py:827
  255.2 13.3 %collective-permute-start.27 = (f32[62,256]{1,0:T(8,128)S(1)}, f32[62,256]{1,0:T(8,128)S(1)}, u32[]{:S(2)}, u32[]{:S(2)}) collective-permute-start(f32[62,256]{1,0:T(8,128)S(1)} %get-tuple-element.178), channel_id=1, source_target_pairs={{0,2},{1,66},{2,0},{3,64},{64,3},{65,67},{66,1},{67,65},{4,6},{5,7... | collective-permute-start | bytes 190472 | tf_op jit(solution)/shard_map/ppermute | solution.py:827
  256.3 12.2 %collective-permute-start.26 = (f32[62,256]{1,0:T(8,128)S(1)}, f32[62,256]{1,0:T(8,128)S(1)}, u32[]{:S(2)}, u32[]{:S(2)}) collective-permute-start(f32[62,256]{1,0:T(8,128)S(1)} %get-tuple-element.178), channel_id=1, source_target_pairs={{0,0},{1,64},{2,2},{3,66},{64,1},{65,65},{66,3},{67,67},{4,4},{5,6... | collective-permute-start | bytes 190472 | tf_op jit(solution)/shard_map/ppermute | solution.py:827
  258.6 9.9 %collective-permute-start.25 = (f32[56,896]{1,0:T(8,128)S(1)}, f32[56,896]{1,0:T(8,128)S(1)}, u32[]{:S(2)}, u32[]{:S(2)}) collective-permute-start(f32[56,896]{1,0:T(8,128)S(1)} %get-tuple-element.177), channel_id=1, source_target_pairs={{0,0},{1,64},{2,2},{3,66},{64,1},{65,65},{66,3},{67,67},{4,4},{5,6... | collective-permute-start | bytes 602120 | tf_op jit(solution)/shard_map/ppermute | solution.py:827

commit v4 on v3

--- a/solution.py
+++ b/solution.py
@@ -622,19 +622,21 @@
     )(*[far(part) for part in parts])
 
 
-def total_kernel(states, got_ref, own_ref, shared_ref):
+def total_kernel(states, got_ref, joint_ref, shared_ref):
     total = jnp.sum(got_ref[...].astype(F32), axis=0)
     rows = total.shape[0]
-    inner = own_ref.shape[1] - 128
+    inner = joint_ref.shape[1] - 128 - states
     both = inner + states
-    own_ref[:, :inner] = total[:, :inner]
-    own_ref[:, inner:] = total[:, both:]
+    joint_ref[...] = jnp.zeros_like(joint_ref)
+    joint_ref[:rows, :inner] = total[:, :inner]
+    joint_ref[:rows, inner : inner + 128] = total[:, both:]
     shared_ref[:rows] = total[:, inner:both]
     per = inner // states
     for k in range(2 * per):
         line = rows - 3 + k // per
         at = states * (k % per)
         shared_ref[rows + k : rows + k + 1] = total[line : line + 1, at : at + states]
+    joint_ref[:, inner + 128 :] = shared_ref[...]
 
 
 def total_of(got, states):
@@ -645,7 +647,7 @@
         functools.partial(total_kernel, states),
         in_specs=[vmem],
         out_specs=[vmem, vmem],
-        out_shape=[shape_of((rows, columns - states), F32), shape_of((extra, states), F32)],
+        out_shape=[shape_of((extra, columns), F32), shape_of((extra, states), F32)],
         compiler_params=params(16),
         cost_estimate=lasting(3),
         name="late_total",
@@ -653,12 +655,12 @@
 
 
 def deliver_kernel(
-    own_ref, s0, s1, s2, s3,
+    joint_ref, s1, s2, s3,
     norm_ref, x_ref, bc_ref, dt_ref, conv_x_ref, conv_bc_ref, head_ref, gate_ref,
 ):
-    shared = (s0[...] + s1[...]) + (s2[...] + s3[...])
-    own = own_ref[...]
     block, inner = x_ref.shape
+    own = joint_ref[:, : inner + 128]
+    shared = (joint_ref[:, inner + 128 :] + s1[...]) + (s2[...] + s3[...])
     heads = dt_ref.shape[0]
     x_ref[...] = own[:block, :inner]
     dt_ref[...] = own[:block, inner:].T[:heads]
@@ -674,15 +676,15 @@
 
 def deliver(own, shared, block, heads):
     vmem = pl.BlockSpec()
-    inner = own.shape[1] - 128
     states = shared[0].shape[1]
+    inner = own.shape[1] - 128 - states
     shapes = [
         (2 * inner,), (block, inner), (block, states), (heads, block),
         (5, inner), (5, states), (3, heads), (inner,),
     ]
     return pl.pallas_call(
         deliver_kernel,
-        in_specs=[vmem] * 5,
+        in_specs=[vmem] * 4,
         out_specs=[vmem] * 8,
         out_shape=[shape_of(shape, F32) for shape in shapes],
         compiler_params=params(16),
@@ -957,11 +959,8 @@
     got, early, output = after(exchange(late_sum), early, output)
     own, shared = total_of(got, states)
     own, back_blocks = after(own, back_blocks)
-    own = trade(own)
-
-    shared = [
-        permute(shared, lambda xh, xl, core, a=a, b=b: (core, xl ^ b, xh ^ a)) for a, b in TURNS
-    ]
+
+    own, *shared = to_owners([own] + [shared] * 3)
     input_grad = finish_input(meta, back_blocks, hidden_in, cotangent, gain)
     norm_grad, x_grad, bc_grad, dt_grad, conv_x_grad, conv_bc_grad, head_part, gate_part = deliver(
         own, shared, block, heads

time: 271 us -> 268 us (0.989)
  starting transfers between devices: 78.1 us -> 73.3 us
    ppermute x26 -> x25, starting transfers between devices: 52.9 us -> 48.1 us  [permute(): return lax.ppermute(value, GROUP, moves(rule))]
    ppermute x26 -> x25, waiting for transfers between devices: 59.6 us -> 61.7 us  [permute(): return lax.ppermute(value, GROUP, moves(rule))]
  transfers between devices with their start and end apart: 33 -> 32, of which waited for: 11 -> 12; matrix products, arithmetic and copies ran while one was open for 2% -> 2% of each run, Pallas kernels for 32% -> 33%
where the time goes in v4:
time: 268 us; the launch traced here: 267 us
  Pallas kernels  109 us (41%)
  starting transfers between devices  73.3 us (27%)
  waiting for transfers between devices  68.8 us (26%)
  other arithmetic  7.36 us (3%)
  local copies, waits for them, and re-layouts  6.74 us (3%)
    ppermute x25, waiting for transfers between devices, permute(): return lax.ppermute(value, GROUP, moves(rule))  61.7 us
    ppermute x25, starting transfers between devices, permute(): return lax.ppermute(value, GROUP, moves(rule))  48.1 us
    pallas_call x1, Pallas kernels, mixer_backward(): pl.pallas_call(backward_kernel, grid=(steps,), in_specs=[pl.BlockSpec((SP...  24 us
    all_to_all x2, starting transfers between devices, exchange(): return lax.all_to_all(blocks, PLANE, 0, 0, tiled=True)  14 us
    pallas_call x1, Pallas kernels, project_back(): pl.pallas_call(project_back_kernel, grid=(2 * per,), in_specs=[pl.BlockSp...  11.8 us
    pallas_call x1, Pallas kernels, mixer_forward(): pl.pallas_call(forward_kernel, grid=(steps,), in_specs=[pl.BlockSpec((SPA...  10.9 us
    pallas_call x1, Pallas kernels, project(): pl.pallas_call(project_kernel, grid=(length // rows,), in_specs=[pl.Block...  10.7 us
    pallas_call x1, Pallas kernels, gate_back(): pl.pallas_call(functools.partial(gate_back_kernel, width_all), grid=(inne...  10 us
  transfers between devices with their start and end apart: 32, of which 12 were waited for; matrix products, arithmetic and copies ran while one was open for 2% of the time, Pallas kernels for 33%

profile of v4, /device:TPU:1, one launch (start us, length us, event | category | flops | bytes accessed | tf_op | source)
XLA Modules:
  0.0 266.8 jit_solution(13635054046994772954)
XLA Ops:
  0.7 1.1 pack_weights.1
  1.8 6.0 %collective-permute-start = (bf16[48,2688]{1,0:T(8,128)(2,1)S(1)}, bf16[48,2688]{1,0:T(8,128)(2,1)S(1)}, u32[]{:S(2)}, u32[]{:S(2)}) collective-permute-start(bf16[48,2688]{1,0:T(8,128)(2,1)S(1)} %pack_weights.1), channel_id=1, source_target_pairs={{0,0},{1,64},{2,2},{3,66},{64,1},{65,65},{66,3},{67,67},{4,4},{5,6... | collective-permute-start | bytes 774152 | tf_op jit(solution)/shard_map/ppermute | solution.py:829
  7.9 3.9 %collective-permute-done = bf16[48,2688]{1,0:T(8,128)(2,1)S(1)} collective-permute-done((bf16[48,2688]{1,0:T(8,128)(2,1)S(1)}, bf16[48,2688]{1,0:T(8,128)(2,1)S(1)}, u32[]{:S(2)}, u32[]{:S(2)}) %collective-permute-start) | collective-permute-done | bytes 258080 | tf_op jit(solution)/shard_map/ppermute | solution.py:829
  11.8 2.2 broadcast_in_dim.24
  14.1 7.9 %all-to-all-start = ((bf16[16,48,2688]{2,1,0:T(8,128)(2,1)}), bf16[16,48,2688]{2,1,0:T(8,128)(2,1)}, u32[]{:S(2)}, u32[]{:S(2)}) async-start(bf16[16,48,2688]{2,1,0:T(8,128)(2,1)} %broadcast_in_dim.24), calls=%async_computation | async-start | bytes 8257536 | tf_op jit(solution)/shard_map/all_to_all | solution.py:864
  22.1 3.3 %collective-permute-start.2 = (bf16[256,1536]{1,0:T(8,128)(2,1)S(1)}, bf16[256,1536]{1,0:T(8,128)(2,1)S(1)}, u32[]{:S(2)}, u32[]{:S(2)}) collective-permute-start(bf16[256,1536]{1,0:T(8,128)(2,1)S(1)} %copy-done.17), channel_id=1, source_target_pairs={{0,2},{1,66},{2,0},{3,64},{64,3},{65,67},{66,1},{67,65},{4,6},{5,7... | collective-permute-start | bytes 2359304 | tf_op jit(solution)/shard_map/ppermute | solution.py:829
  25.4 2.2 collective-permute-start.1
  27.9 0.6 stack.32.meta_ref
  28.5 0.7 collective-permute-start.5
  29.2 2.0 collective-permute-start.4
  31.4 0.7 broadcast_in_dim_reshape.3.skip_ref
  32.0 0.6 select_maximum_fusion.1.taps_ref
  32.7 24.6 %collective-permute-done.2.refs_1_ = bf16[256,1536]{1,0:T(8,128)(2,1)S(1)} collective-permute-done((bf16[256,1536]{1,0:T(8,128)(2,1)S(1)}, bf16[256,1536]{1,0:T(8,128)(2,1)S(1)}, u32[]{:S(2)}, u32[]{:S(2)}) %collective-permute-start.2) | collective-permute-done | bytes 786464 | tf_op jit(solution)/shard_map/ppermute | solution.py:829
  57.3 3.4 %collective-permute-start.6 = (bf16[256,1536]{1,0:T(8,128)(2,1)}, bf16[256,1536]{1,0:T(8,128)(2,1)}, u32[]{:S(2)}, u32[]{:S(2)}) collective-permute-start(bf16[256,1536]{1,0:T(8,128)(2,1)} %cot_ref.1), channel_id=1, source_target_pairs={{0,0},{1,64},{2,2},{3,66},{64,1},{65,65},{66,3},{67,67},{4,4},{5,6... | collective-permute-start | bytes 2359304 | tf_op jit(solution)/shard_map/ppermute | solution.py:829
  60.8 0.6 copy-done.6
  61.4 5.4 %place_normed.1 = (bf16[1024,1536]{1,0:T(8,128)(2,1)}, bf16[1536,1024]{1,0:T(8,128)(2,1)S(1)}) custom-call(s32[6]{0:T(128)S(1)} %copy-done.6, f32[1,1536]{1,0:T(1,128)S(1)} %broadcast_in_dim.23.gain_ref, bf16[256,1536]{1,0:T(8,128)(2,1)} %copy-done.23, bf16[256,1536]{1,0:T(8,128)(2,1)} %copy-done.22, bf16[256,1536]{1,0:T(8,128)(2,1)} %collective-permute-done.4.refs_2_, ...), custom_call_target="tpu_custom_call" | custom-call | flops 6899999744 | bytes 1024 | tf_op jit(solution)/shard_map/place_normed/pallas_call | solution.py:320
  66.8 5.6 %collective-permute-done.6.refs_0_ = bf16[256,1536]{1,0:T(8,128)(2,1)} collective-permute-done((bf16[256,1536]{1,0:T(8,128)(2,1)}, bf16[256,1536]{1,0:T(8,128)(2,1)}, u32[]{:S(2)}, u32[]{:S(2)}) %collective-permute-start.6) | collective-permute-done | bytes 786464 | tf_op jit(solution)/shard_map/ppermute | solution.py:829
  72.5 1.4 collective-permute-start.10
  73.9 2.8 %collective-permute-start.9 = (bf16[256,1536]{1,0:T(8,128)(2,1)}, bf16[256,1536]{1,0:T(8,128)(2,1)S(1)}, u32[]{:S(2)}, u32[]{:S(2)}) collective-permute-start(bf16[256,1536]{1,0:T(8,128)(2,1)} %cot_ref.1), channel_id=1, source_target_pairs={{0,64},{1,0},{2,66},{3,2},{64,65},{65,1},{66,67},{67,3},{4,68},{5,... | collective-permute-start | bytes 2359304 | tf_op jit(solution)/shard_map/ppermute | solution.py:829
  76.7 3.1 %collective-permute-done.7.xo_ref.zo_ref.oo_ref = bf16[768,2688]{1,0:T(8,128)(2,1)S(1)} collective-permute-done((bf16[768,2688]{1,0:T(8,128)(2,1)}, bf16[768,2688]{1,0:T(8,128)(2,1)S(1)}, u32[]{:S(2)}, u32[]{:S(2)}) %collective-permute-start.7) | collective-permute-done | bytes 4128800 | tf_op jit(solution)/shard_map/ppermute | solution.py:839
  79.7 10.7 %project_in.1 = (f32[1024,1152]{1,0:T(8,128)S(1)}, f32[1024,768]{1,0:T(8,128)S(1)}) custom-call(bf16[1024,1536]{1,0:T(8,128)(2,1)} %get-tuple-element.110.tokens_ref, bf16[768,2688]{1,0:T(8,128)(2,1)} %bitcast.9.xm_ref.zm_ref.om_ref, bf16[768,2688]{1,0:T(8,128)(2,1)S(1)} %collective-permute-done.7.xo_ref.zo_ref.oo_ref, ...), custom_call_target="tpu_custom_call" | custom-call | flops 6899999744 | bytes 1024 | tf_op jit(solution)/shard_map/project_in/pallas_call | solution.py:353
  90.5 10.9 %mixer_forward.1 = (f32[1024,768]{1,0:T(8,128)S(1)}, bf16[1024,768]{1,0:T(8,128)(2,1)}, f32[1024,1024]{1,0:T(8,128)}) custom-call(f32[1024,1152]{1,0:T(8,128)S(1)} %get-tuple-element.112.pre_ref, f32[8,1024]{1,0:T(8,128)S(1)} %copy-done.2, f32[8,128]{1,0:T(8,128)S(1)} %select_maximum_fusion.4.head_ref, f32[1,768]{1,0:T(1,128)S(1)} %copy-done.4, ...), custom_call_target="tpu_custom_call" | custom-call | flops 14949999616 | bytes 1024 | tf_op jit(solution)/shard_map/mixer_forward/pallas_call | solution.py:759
  101.4 1.3 collective-permute-done.8.refs_1_
  102.7 0.9 copy-done.28
  103.6 3.0 %place_cotangent.1 = (bf16[1024,1536]{1,0:T(8,128)(2,1)S(1)}, bf16[1536,1024]{1,0:T(8,128)(2,1)S(1)}) custom-call(s32[6]{0:T(128)S(1)} %copy-done.7, f32[1,1536]{1,0:T(1,128)S(1)} %broadcast_in_dim.23.gain_ref, bf16[256,1536]{1,0:T(8,128)(2,1)} %collective-permute-done.6.refs_0_, bf16[256,1536]{1,0:T(8,128)(2,1)} %copy-done.28, ...), custom_call_target="tpu_custom_call" | custom-call | flops 6899999744 | bytes 1024 | tf_op jit(solution)/shard_map/place_cotangent/pallas_call | solution.py:320
  106.6 7.4 %gate_sums.1 = (f32[1024,768]{1,0:T(8,128)S(1)}, f32[8,1024]{1,0:T(8,128)S(1)}) custom-call(bf16[1024,1536]{1,0:T(8,128)(2,1)S(1)} %get-tuple-element.124.cot_ref, bf16[768,2688]{1,0:T(8,128)(2,1)} %bitcast.9.xm_ref.zm_ref.om_ref, bf16[768,2688]{1,0:T(8,128)(2,1)} %copy-done, f32[1024,768]{1,0:T(8,128)S(1)} %get-tuple-element.125.y_ref, ...), custom_call_target="tpu_custom_call" | custom-call | flops 6899999744 | bytes 1024 | tf_op jit(solution)/shard_map/gate_sums/pallas_call | solution.py:400
  114.0 2.7 %collective-permute-start.13 = (f32[8,1024]{1,0:T(8,128)S(1)}, f32[8,1024]{1,0:T(8,128)S(1)}, u32[]{:S(2)}, u32[]{:S(2)}) collective-permute-start(f32[8,1024]{1,0:T(8,128)S(1)} %get-tuple-element.128.s0), channel_id=1, source_target_pairs={{0,66},{1,67},{2,64},{3,65},{64,2},{65,3},{66,0},{67,1},{4,70},{5,... | collective-permute-start | bytes 98312 | tf_op jit(solution)/shard_map/ppermute | solution.py:829
  116.7 0.7 collective-permute-start.11
  117.4 0.7 collective-permute-done.13.s3
  118.1 2.9 %collective-permute-done.12.s2 = f32[8,1024]{1,0:T(8,128)S(1)} collective-permute-done((f32[8,1024]{1,0:T(8,128)S(1)}, f32[8,1024]{1,0:T(8,128)S(1)}, u32[]{:S(2)}, u32[]{:S(2)}) %collective-permute-start.12) | collective-permute-done | bytes 32800 | tf_op jit(solution)/shard_map/ppermute | solution.py:829
  121.0 10.0 %gate_back.1 = (bf16[1024,768]{1,0:T(8,128)(2,1)}, bf16[1024,768]{1,0:T(8,128)(2,1)}, f32[1024,768]{1,0:T(8,128)}, f32[8,768]{1,0:T(8,128)S(1)}, bf16[16,2,48,76...) custom-call(f32[8,1024]{1,0:T(8,128)S(1)} %get-tuple-element.128.s0, f32[8,1024]{1,0:T(8,128)S(1)} %collective-permute-done.11.s1, ...), custom_call_target="tpu_custom_call" | custom-call | flops 13799999488 | bytes 1024 | tf_op jit(solution)/shard_map/gate_back/pallas_call | solution.py:456
  131.0 3.1 %collective-permute-start.14 = (bf16[16,2,48,768]{3,2,1,0:T(8,128)(2,1)}, bf16[16,2,48,768]{3,2,1,0:T(8,128)(2,1)S(1)}, u32[]{:S(2)}, u32[]{:S(2)}) collective-permute-start(bf16[16,2,48,768]{3,2,1,0:T(8,128)(2,1)} %get-tuple-element.133), channel_id=1, source_target_pairs={{0,1},{1,0},{2,3},{3,2},{4,5},{5,4},{6,7},{7,6},{8,9},{9,8},{10,11... | collective-permute-start | bytes 7077896 | tf_op jit(solution)/shard_map/ppermute | solution.py:839
  134.1 7.7 %project_out.1 = (bf16[256,1536]{1,0:T(8,128)(2,1)}, bf16[256,1536]{1,0:T(8,128)(2,1)}, bf16[256,1536]{1,0:T(8,128)(2,1)}, bf16[256,1536]{1,0:T(8,128)(2,1)}) custom-call(s32[6]{0:T(128)S(1)} %copy-done.7, bf16[1024,768]{1,0:T(8,128)(2,1)} %get-tuple-element.134.normed_ref, bf16[768,2688]{1,0:T(8,128)(2,1)} %bitcast.9.xm_ref.zm_ref.om_ref, ...), custom_call_target="tpu_custom_call" | custom-call | flops 6899999744 | bytes 1024 | tf_op jit(solution)/shard_map/project_out/pallas_call | solution.py:514
  141.8 2.2 add_convert_fusion
  144.0 7.1 %all-to-all-start.1 = ((bf16[16,2,48,768]{3,2,1,0:T(8,128)(2,1)}), bf16[16,2,48,768]{3,2,1,0:T(8,128)(2,1)}, u32[]{:S(2)}, u32[]{:S(2)}) async-start(bf16[16,2,48,768]{3,2,1,0:T(8,128)(2,1)} %add_convert_fusion), calls=%async_computation.1 | async-start | bytes 4718592 | tf_op jit(solution)/shard_map/all_to_all | solution.py:869
  151.1 3.9 %collective-permute-start.15 = (bf16[256,1536]{1,0:T(8,128)(2,1)}, bf16[256,1536]{1,0:T(8,128)(2,1)S(1)}, u32[]{:S(2)}, u32[]{:S(2)}) collective-permute-start(bf16[256,1536]{1,0:T(8,128)(2,1)} %get-tuple-element.147), channel_id=1, source_target_pairs={{0,0},{1,64},{2,2},{3,66},{64,1},{65,65},{66,3},{67,67},{4,4},{5,6... | collective-permute-start | bytes 2359304 | tf_op jit(solution)/shard_map/ppermute | solution.py:829
  154.9 0.3 collective-permute-start.16
  155.3 3.0 %collective-permute-start.18 = (bf16[256,1536]{1,0:T(8,128)(2,1)S(1)}, bf16[256,1536]{1,0:T(8,128)(2,1)S(1)}, u32[]{:S(2)}, u32[]{:S(2)}) collective-permute-start(bf16[256,1536]{1,0:T(8,128)(2,1)S(1)} %copy-done.24), channel_id=1, source_target_pairs={{0,3},{1,67},{2,1},{3,65},{64,2},{65,66},{66,0},{67,64},{4,7},{5,7... | collective-permute-start | bytes 2359304 | tf_op jit(solution)/shard_map/ppermute | solution.py:829
  158.3 24.0 %mixer_backward.1 = (bf16[1024,1152]{1,0:T(8,128)(2,1)S(1)}, f32[8,1024]{1,0:T(8,128)S(1)}, f32[8,128]{1,0:T(8,128)S(1)}) custom-call(f32[1024,1152]{1,0:T(8,128)} %copy-done.10, f32[1024,1024]{1,0:T(8,128)} %get-tuple-element.117.conv_ref, f32[1024,768]{1,0:T(8,128)} %get-tuple-element.139.dy_ref, bf16[1024,768]{1,0:T(8,128)(2,1)} %get-tuple-element.140.kept_ref, ...), custom_call_target="tpu_custom_call" | custom-call | flops 34500001792 | bytes 1024 | tf_op jit(solution)/shard_map/mixer_backward/pallas_call | solution.py:789
  182.3 11.8 %project_back.1 = (bf16[256,1536]{1,0:T(8,128)(2,1)}, bf16[256,1536]{1,0:T(8,128)(2,1)}, bf16[256,1536]{1,0:T(8,128)(2,1)}, bf16[256,1536]{1,0:T(8,128)(2,1)}, f32[8,1536]{1,0:T(8,128)S(1)}) custom-call(s32[6]{0:T(128)S(1)} %copy-done.8, bf16[1024,1152]{1,0:T(8,128)(2,1)S(1)} %get-tuple-element.151.late_ref, bf16[1024,768]{1,0:T(8,128)(2,1)} %get-tuple-element.142.gate_ref, ...), custom_call_target="tpu_custom_call" | custom-call | flops 575000000 | bytes 1024 | tf_op jit(solution)/shard_map/project_back/pallas_call | solution.py:557
  194.2 2.3 collective-permute-start.19
  196.5 0.7 slice.60
  197.3 8.4 %weight_grad.1 = (f32[768,1152]{1,0:T(8,128)}, bf16[784,1152]{1,0:T(8,128)(2,1)}) custom-call(bf16[1536,1024]{1,0:T(8,128)(2,1)} %copy-done.1, bf16[1024,1152]{1,0:T(8,128)(2,1)S(1)} %get-tuple-element.151.late_ref, f32[16,1152]{1,0:T(8,128)S(1)} %pad.29.vector_ref), custom_call_target="tpu_custom_call" | custom-call | flops 575000000 | bytes 1024 | tf_op jit(solution)/shard_map/weight_grad/pallas_call | solution.py:588
  205.6 3.6 %collective-permute-done.19.b0 = bf16[256,1536]{1,0:T(8,128)(2,1)S(1)} collective-permute-done((bf16[256,1536]{1,0:T(8,128)(2,1)}, bf16[256,1536]{1,0:T(8,128)(2,1)S(1)}, u32[]{:S(2)}, u32[]{:S(2)}) %collective-permute-start.19) | collective-permute-done | bytes 786464 | tf_op jit(solution)/shard_map/ppermute | solution.py:829
  209.2 4.0 %collective-permute-done.20 = bf16[784,1152]{1,0:T(8,128)(2,1)S(1)} collective-permute-done((bf16[784,1152]{1,0:T(8,128)(2,1)}, bf16[784,1152]{1,0:T(8,128)(2,1)S(1)}, u32[]{:S(2)}, u32[]{:S(2)}) %collective-permute-start.20) | collective-permute-done | bytes 1806368 | tf_op jit(solution)/shard_map/ppermute | solution.py:839
  213.2 0.2 convert_element_type.40
  213.4 0.6 fusion
  214.1 1.5 pad_maximum_fusion
  215.5 6.9 %all-to-all-start.2 = ((bf16[16,56,1152]{2,1,0:T(8,128)(2,1)}), bf16[16,56,1152]{2,1,0:T(8,128)(2,1)S(1)}, u32[]{:S(2)}, u32[]{:S(2)}) async-start(bf16[16,56,1152]{2,1,0:T(8,128)(2,1)} %pad_maximum_fusion), calls=%async_computation.2 | async-start | bytes 4128768 | tf_op jit(solution)/shard_map/all_to_all | solution.py:869
  222.4 0.7 collective-permute-start.22
  223.1 0.6 collective-permute-start.23
  223.8 1.8 collective-permute-start.24
  225.6 2.0 convert_reduce_fusion
  227.6 3.0 %collective-permute-start.21 = (f32[2,48,768]{2,1,0:T(8,128)S(1)}, f32[2,48,768]{2,1,0:T(8,128)S(1)}, u32[]{:S(2)}, u32[]{:S(2)}) collective-permute-start(f32[2,48,768]{2,1,0:T(8,128)S(1)} %convert_reduce_fusion), channel_id=1, source_target_pairs={{0,0},{1,64},{2,2},{3,66},{64,1},{65,65},{66,3},{67,67},{4,4},{5,6... | collective-permute-start | bytes 884744 | tf_op jit(solution)/shard_map/ppermute | solution.py:829
  230.5 3.5 %finish_output.1 = bf16[256,1536]{1,0:T(8,128)(2,1)} custom-call(s32[6]{0:T(128)S(1)} %copy-done.8, bf16[256,1536]{1,0:T(8,128)(2,1)} %copy-done.18, bf16[256,1536]{1,0:T(8,128)(2,1)} %copy-done.19, bf16[256,1536]{1,0:T(8,128)(2,1)} %copy-done.20, bf16[256,1536]{1,0:T(8,128)(2,1)} %copy-done.21, bf16[256,1536]{1,0:T(8,128)(2,1)} %hidden_ref.3), custom_call_target="tpu_custom_call" | custom-call | flops 3449999872 | bytes 1024 | tf_op jit(solution)/shard_map/finish_output/pallas_call | solution.py:710
  234.1 17.1 %collective-permute-done.21 = f32[2,48,768]{2,1,0:T(8,128)S(1)} collective-permute-done((f32[2,48,768]{2,1,0:T(8,128)S(1)}, f32[2,48,768]{2,1,0:T(8,128)S(1)}, u32[]{:S(2)}, u32[]{:S(2)}) %collective-permute-start.21) | collective-permute-done | bytes 294944 | tf_op jit(solution)/shard_map/ppermute | solution.py:829
  251.2 0.4 late_total.1
  251.8 3.6 %collective-permute-start.27 = (f32[62,256]{1,0:T(8,128)S(1)}, f32[62,256]{1,0:T(8,128)S(1)}, u32[]{:S(2)}, u32[]{:S(2)}) collective-permute-start(f32[62,256]{1,0:T(8,128)S(1)} %get-tuple-element.178), channel_id=1, source_target_pairs={{0,1},{1,65},{2,3},{3,67},{64,0},{65,64},{66,2},{67,66},{4,5},{5,6... | collective-permute-start | bytes 190472 | tf_op jit(solution)/shard_map/ppermute | solution.py:829
  255.4 1.1 collective-permute-start.26
  256.5 2.3 collective-permute-start.25
  258.9 4.4 %finish_input.1 = f32[256,1536]{1,0:T(8,128)} custom-call(s32[6]{0:T(128)S(1)} %copy-done.8, bf16[256,1536]{1,0:T(8,128)(2,1)S(1)} %collective-permute-done.19.b0, bf16[256,1536]{1,0:T(8,128)(2,1)} %collective-permute-done.22.b1, bf16[256,1536]{1,0:T(8,128)(2,1)} %collective-permute-done.23.b2, bf16[256,1536]{1,0:T(8,128)(2,1)} %collective-permute-done.24.b3, ...), custom_call_target="tpu_custom_call" | custom-call | flops 3449999872 | bytes 1024 | tf_op jit(solution)/shard_map/finish_input/pallas_call | solution.py:731
  263.3 0.7 slice_bitcast_fusion
  264.0 2.1 collective-permute-done.25.joint_ref
  266.1 0.7 deliver_late.1
  (106 shorter events, 1.2 us)
Async XLA Ops:
  0.6 7.2 %copy-start.16 = (f32[3,12]{1,0:T(4,128)S(1)}, f32[3,12]{1,0:T(4,128)}, u32[]{:S(2)}) copy-start(f32[3,12]{1,0:T(4,128)} %param.21) | copy-start | bytes 436
  0.7 7.2 %copy-start.15 = (f32[768]{0:T(1024)S(1)}, f32[768]{0:T(1024)}, u32[]{:S(2)}) copy-start(f32[768]{0:T(1024)} %param.22) | copy-start | bytes 9220
  0.7 7.2 %copy-start.12 = (f32[5,768]{1,0:T(8,128)S(1)}, f32[5,768]{1,0:T(8,128)}, u32[]{:S(2)}) copy-start(f32[5,768]{1,0:T(8,128)} %param.19) | copy-start | bytes 46084
  1.8 10.0 %collective-permute-start = (bf16[48,2688]{1,0:T(8,128)(2,1)S(1)}, bf16[48,2688]{1,0:T(8,128)(2,1)S(1)}, u32[]{:S(2)}, u32[]{:S(2)}) collective-permute-start(bf16[48,2688]{1,0:T(8,128)(2,1)S(1)} %pack_weights.1), channel_id=1, source_target_pairs={{0,0},{1,64},{2,2},{3,66},{64,1},{65,65},{66,3},{67,67},{4,4},{5,6... | collective-permute-start | bytes 774152 | tf_op jit(solution)/shard_map/ppermute | solution.py:829
  14.1 8.0 %copy-start.17 = (bf16[256,1536]{1,0:T(8,128)(2,1)S(1)}, bf16[256,1536]{1,0:T(8,128)(2,1)}, u32[]{:S(2)}) copy-start(bf16[256,1536]{1,0:T(8,128)(2,1)} %hidden_ref.3) | copy-start | bytes 2359300
  14.1 13.8 %copy-start.13 = (f32[1536]{0:T(1024)S(1)}, f32[1536]{0:T(1024)}, u32[]{:S(2)}) copy-start(f32[1536]{0:T(1024)} %param.14) | copy-start | bytes 18436
  14.1 18.0 %copy-start.14 = (f32[5,256]{1,0:T(8,128)S(1)}, f32[5,256]{1,0:T(8,128)}, u32[]{:S(2)}) copy-start(f32[5,256]{1,0:T(8,128)} %param.20) | copy-start | bytes 15364
  14.1 58.3 %all-to-all-start = ((bf16[16,48,2688]{2,1,0:T(8,128)(2,1)}), bf16[16,48,2688]{2,1,0:T(8,128)(2,1)}, u32[]{:S(2)}, u32[]{:S(2)}) async-start(bf16[16,48,2688]{2,1,0:T(8,128)(2,1)} %broadcast_in_dim.24), calls=%async_computation | async-start | bytes 8257536 | tf_op jit(solution)/shard_map/all_to_all | solution.py:864
  22.1 35.2 %collective-permute-start.2 = (bf16[256,1536]{1,0:T(8,128)(2,1)S(1)}, bf16[256,1536]{1,0:T(8,128)(2,1)S(1)}, u32[]{:S(2)}, u32[]{:S(2)}) collective-permute-start(bf16[256,1536]{1,0:T(8,128)(2,1)S(1)} %copy-done.17), channel_id=1, source_target_pairs={{0,2},{1,66},{2,0},{3,64},{64,3},{65,67},{66,1},{67,65},{4,6},{5,7... | collective-permute-start | bytes 2359304 | tf_op jit(solution)/shard_map/ppermute | solution.py:829
  25.4 31.8 %collective-permute-start.1 = (bf16[256,1536]{1,0:T(8,128)(2,1)S(1)}, bf16[256,1536]{1,0:T(8,128)(2,1)S(1)}, u32[]{:S(2)}, u32[]{:S(2)}) collective-permute-start(bf16[256,1536]{1,0:T(8,128)(2,1)S(1)} %copy-done.17), channel_id=1, source_target_pairs={{0,0},{1,64},{2,2},{3,66},{64,1},{65,65},{66,3},{67,67},{4,4},{5,6... | collective-permute-start | bytes 2359304 | tf_op jit(solution)/shard_map/ppermute | solution.py:829
  27.6 3.6 %collective-permute-start.3 = (f32[16,768]{1,0:T(8,128)S(1)}, f32[16,768]{1,0:T(8,128)S(1)}, u32[]{:S(2)}, u32[]{:S(2)}) collective-permute-start(f32[16,768]{1,0:T(8,128)S(1)} %select_maximum_fusion), channel_id=1, source_target_pairs={{0,1},{1,0},{2,3},{3,2},{4,5},{5,4},{6,7},{7,6},{8,9},{9,8},{10,11... | collective-permute-start | bytes 147464 | tf_op jit(solution)/shard_map/ppermute | solution.py:839
  28.5 32.2 %collective-permute-start.5 = (bf16[256,1536]{1,0:T(8,128)(2,1)S(1)}, bf16[256,1536]{1,0:T(8,128)(2,1)}, u32[]{:S(2)}, u32[]{:S(2)}) collective-permute-start(bf16[256,1536]{1,0:T(8,128)(2,1)S(1)} %copy-done.17), channel_id=1, source_target_pairs={{0,66},{1,2},{2,64},{3,0},{64,67},{65,3},{66,65},{67,1},{4,70},{5,... | collective-permute-start | bytes 2359304 | tf_op jit(solution)/shard_map/ppermute | solution.py:829
  29.2 31.5 %collective-permute-start.4 = (bf16[256,1536]{1,0:T(8,128)(2,1)S(1)}, bf16[256,1536]{1,0:T(8,128)(2,1)}, u32[]{:S(2)}, u32[]{:S(2)}) collective-permute-start(bf16[256,1536]{1,0:T(8,128)(2,1)S(1)} %copy-done.17), channel_id=1, source_target_pairs={{0,64},{1,0},{2,66},{3,2},{64,65},{65,1},{66,67},{67,3},{4,68},{5,... | collective-permute-start | bytes 2359304 | tf_op jit(solution)/shard_map/ppermute | solution.py:829
  57.2 3.5 %copy-start.22 = (bf16[256,1536]{1,0:T(8,128)(2,1)}, bf16[256,1536]{1,0:T(8,128)(2,1)S(1)}, u32[]{:S(2)}) copy-start(bf16[256,1536]{1,0:T(8,128)(2,1)S(1)} %collective-permute-done.2.refs_1_) | copy-start | bytes 2359300
  57.3 3.5 %copy-start.23 = (bf16[256,1536]{1,0:T(8,128)(2,1)}, bf16[256,1536]{1,0:T(8,128)(2,1)S(1)}, u32[]{:S(2)}) copy-start(bf16[256,1536]{1,0:T(8,128)(2,1)S(1)} %collective-permute-done.1.refs_0_) | copy-start | bytes 2359300
  57.3 15.1 %collective-permute-start.6 = (bf16[256,1536]{1,0:T(8,128)(2,1)}, bf16[256,1536]{1,0:T(8,128)(2,1)}, u32[]{:S(2)}, u32[]{:S(2)}) collective-permute-start(bf16[256,1536]{1,0:T(8,128)(2,1)} %cot_ref.1), channel_id=1, source_target_pairs={{0,0},{1,64},{2,2},{3,66},{64,1},{65,65},{66,3},{67,67},{4,4},{5,6... | collective-permute-start | bytes 2359304 | tf_op jit(solution)/shard_map/ppermute | solution.py:829
  60.7 0.7 copy-start.6
  66.8 54.1 %copy-start.1 = (bf16[1536,1024]{1,0:T(8,128)(2,1)}, bf16[1536,1024]{1,0:T(8,128)(2,1)S(1)}, u32[]{:S(2)}) copy-start(bf16[1536,1024]{1,0:T(8,128)(2,1)S(1)} %get-tuple-element.107.tokens_t_ref) | copy-start | bytes 9437188
  72.4 18.0 %copy-start.2 = (f32[8,1024]{1,0:T(8,128)S(1)}, f32[8,1024]{1,0:T(8,128)}, u32[]{:S(2)}) copy-start(f32[8,1024]{1,0:T(8,128)} %select_maximum_fusion.1.taps_ref) | copy-start | bytes 98308
  72.4 18.0 %copy-start.4 = (f32[1,768]{1,0:T(1,128)S(1)}, f32[1,768]{1,0:T(1,128)}, u32[]{:S(2)}) copy-start(f32[1,768]{1,0:T(1,128)} %broadcast_in_dim_reshape.3.skip_ref) | copy-start | bytes 9220
  72.4 7.4 %collective-permute-start.7 = (bf16[768,2688]{1,0:T(8,128)(2,1)}, bf16[768,2688]{1,0:T(8,128)(2,1)S(1)}, u32[]{:S(2)}, u32[]{:S(2)}) collective-permute-start(bf16[768,2688]{1,0:T(8,128)(2,1)} %bitcast.9.xm_ref.zm_ref.om_ref), channel_id=1, source_target_pairs={{0,1},{1,0},{2,3},{3,2},{4,5},{5,4},{6,7},{7,6},{8,9},{9,8},{10,11... | collective-permute-start | bytes 12386312 | tf_op jit(solution)/shard_map/ppermute | solution.py:839
  72.5 28.9 %collective-permute-start.10 = (bf16[256,1536]{1,0:T(8,128)(2,1)}, bf16[256,1536]{1,0:T(8,128)(2,1)S(1)}, u32[]{:S(2)}, u32[]{:S(2)}) collective-permute-start(bf16[256,1536]{1,0:T(8,128)(2,1)} %cot_ref.1), channel_id=1, source_target_pairs={{0,66},{1,2},{2,64},{3,0},{64,67},{65,3},{66,65},{67,1},{4,70},{5,... | collective-permute-start | bytes 2359304 | tf_op jit(solution)/shard_map/ppermute | solution.py:829
  73.9 27.5 %collective-permute-start.9 = (bf16[256,1536]{1,0:T(8,128)(2,1)}, bf16[256,1536]{1,0:T(8,128)(2,1)S(1)}, u32[]{:S(2)}, u32[]{:S(2)}) collective-permute-start(bf16[256,1536]{1,0:T(8,128)(2,1)} %cot_ref.1), channel_id=1, source_target_pairs={{0,64},{1,0},{2,66},{3,2},{64,65},{65,1},{66,67},{67,3},{4,68},{5,... | collective-permute-start | bytes 2359304 | tf_op jit(solution)/shard_map/ppermute | solution.py:829
  76.6 26.1 %collective-permute-start.8 = (bf16[256,1536]{1,0:T(8,128)(2,1)}, bf16[256,1536]{1,0:T(8,128)(2,1)S(1)}, u32[]{:S(2)}, u32[]{:S(2)}) collective-permute-start(bf16[256,1536]{1,0:T(8,128)(2,1)} %cot_ref.1), channel_id=1, source_target_pairs={{0,2},{1,66},{2,0},{3,64},{64,3},{65,67},{66,1},{67,65},{4,6},{5,7... | collective-permute-start | bytes 2359304 | tf_op jit(solution)/shard_map/ppermute | solution.py:829
  79.7 10.7 %copy-start = (bf16[768,2688]{1,0:T(8,128)(2,1)}, bf16[768,2688]{1,0:T(8,128)(2,1)S(1)}, u32[]{:S(2)}) copy-start(bf16[768,2688]{1,0:T(8,128)(2,1)S(1)} %collective-permute-done.7.xo_ref.zo_ref.oo_ref) | copy-start | bytes 12386308
  90.4 10.9 %copy-start.10 = (f32[1024,1152]{1,0:T(8,128)}, f32[1024,1152]{1,0:T(8,128)S(1)}, u32[]{:S(2)}) copy-start(f32[1024,1152]{1,0:T(8,128)S(1)} %get-tuple-element.112.pre_ref) | copy-start | bytes 14155780
  90.4 13.2 %copy-start.7 = (s32[6]{0:T(128)S(1)}, s32[6]{0:T(128)}, u32[]{:S(2)}) copy-start(s32[6]{0:T(128)} %stack.32.meta_ref) | copy-start | bytes 76
  101.4 1.4 copy-start.26
  101.4 1.4 copy-start.27
  102.7 0.9 copy-start.28
  114.0 4.1 %collective-permute-start.13 = (f32[8,1024]{1,0:T(8,128)S(1)}, f32[8,1024]{1,0:T(8,128)S(1)}, u32[]{:S(2)}, u32[]{:S(2)}) collective-permute-start(f32[8,1024]{1,0:T(8,128)S(1)} %get-tuple-element.128.s0), channel_id=1, source_target_pairs={{0,66},{1,67},{2,64},{3,65},{64,2},{65,3},{66,0},{67,1},{4,70},{5,... | collective-permute-start | bytes 98312 | tf_op jit(solution)/shard_map/ppermute | solution.py:829
  116.7 4.3 %collective-permute-start.12 = (f32[8,1024]{1,0:T(8,128)S(1)}, f32[8,1024]{1,0:T(8,128)S(1)}, u32[]{:S(2)}, u32[]{:S(2)}) collective-permute-start(f32[8,1024]{1,0:T(8,128)S(1)} %get-tuple-element.128.s0), channel_id=1, source_target_pairs={{0,64},{1,65},{2,66},{3,67},{64,0},{65,1},{66,2},{67,3},{4,68},{5,... | collective-permute-start | bytes 98312 | tf_op jit(solution)/shard_map/ppermute | solution.py:829
  116.7 4.3 %collective-permute-start.11 = (f32[8,1024]{1,0:T(8,128)S(1)}, f32[8,1024]{1,0:T(8,128)S(1)}, u32[]{:S(2)}, u32[]{:S(2)}) collective-permute-start(f32[8,1024]{1,0:T(8,128)S(1)} %get-tuple-element.128.s0), channel_id=1, source_target_pairs={{0,2},{1,3},{2,0},{3,1},{64,66},{65,67},{66,64},{67,65},{4,6},{5,7... | collective-permute-start | bytes 98312 | tf_op jit(solution)/shard_map/ppermute | solution.py:829
  131.0 10.8 %copy-start.9 = (f32[8,768]{1,0:T(8,128)}, f32[8,768]{1,0:T(8,128)S(1)}, u32[]{:S(2)}) copy-start(f32[8,768]{1,0:T(8,128)S(1)} %get-tuple-element.154) | copy-start | bytes 73732
  131.0 10.8 %collective-permute-start.14 = (bf16[16,2,48,768]{3,2,1,0:T(8,128)(2,1)}, bf16[16,2,48,768]{3,2,1,0:T(8,128)(2,1)S(1)}, u32[]{:S(2)}, u32[]{:S(2)}) collective-permute-start(bf16[16,2,48,768]{3,2,1,0:T(8,128)(2,1)} %get-tuple-element.133), channel_id=1, source_target_pairs={{0,1},{1,0},{2,3},{3,2},{4,5},{5,4},{6,7},{7,6},{8,9},{9,8},{10,11... | collective-permute-start | bytes 7077896 | tf_op jit(solution)/shard_map/ppermute | solution.py:839
  144.0 11.3 %copy-start.25 = (bf16[256,1536]{1,0:T(8,128)(2,1)S(1)}, bf16[256,1536]{1,0:T(8,128)(2,1)}, u32[]{:S(2)}) copy-start(bf16[256,1536]{1,0:T(8,128)(2,1)} %get-tuple-element.149) | copy-start | bytes 2359300
  144.0 11.4 %copy-start.24 = (bf16[256,1536]{1,0:T(8,128)(2,1)S(1)}, bf16[256,1536]{1,0:T(8,128)(2,1)}, u32[]{:S(2)}) copy-start(bf16[256,1536]{1,0:T(8,128)(2,1)} %get-tuple-element.150) | copy-start | bytes 2359300
  144.0 14.3 %copy-start.3 = (f32[8,1024]{1,0:T(8,128)S(1)}, f32[8,1024]{1,0:T(8,128)}, u32[]{:S(2)}) copy-start(f32[8,1024]{1,0:T(8,128)} %select_maximum_fusion.1.taps_ref) | copy-start | bytes 98308
  144.0 14.3 %copy-start.5 = (f32[1,768]{1,0:T(1,128)S(1)}, f32[1,768]{1,0:T(1,128)}, u32[]{:S(2)}) copy-start(f32[1,768]{1,0:T(1,128)} %broadcast_in_dim_reshape.3.skip_ref) | copy-start | bytes 9220
  144.0 65.2 %all-to-all-start.1 = ((bf16[16,2,48,768]{3,2,1,0:T(8,128)(2,1)}), bf16[16,2,48,768]{3,2,1,0:T(8,128)(2,1)}, u32[]{:S(2)}, u32[]{:S(2)}) async-start(bf16[16,2,48,768]{3,2,1,0:T(8,128)(2,1)} %add_convert_fusion), calls=%async_computation.1 | async-start | bytes 4718592 | tf_op jit(solution)/shard_map/all_to_all | solution.py:869
  151.1 43.1 %collective-permute-start.15 = (bf16[256,1536]{1,0:T(8,128)(2,1)}, bf16[256,1536]{1,0:T(8,128)(2,1)S(1)}, u32[]{:S(2)}, u32[]{:S(2)}) collective-permute-start(bf16[256,1536]{1,0:T(8,128)(2,1)} %get-tuple-element.147), channel_id=1, source_target_pairs={{0,0},{1,64},{2,2},{3,66},{64,1},{65,65},{66,3},{67,67},{4,4},{5,6... | collective-permute-start | bytes 2359304 | tf_op jit(solution)/shard_map/ppermute | solution.py:829
  154.9 39.2 %collective-permute-start.16 = (bf16[256,1536]{1,0:T(8,128)(2,1)}, bf16[256,1536]{1,0:T(8,128)(2,1)S(1)}, u32[]{:S(2)}, u32[]{:S(2)}) collective-permute-start(bf16[256,1536]{1,0:T(8,128)(2,1)} %get-tuple-element.148), channel_id=1, source_target_pairs={{0,2},{1,66},{2,0},{3,64},{64,3},{65,67},{66,1},{67,65},{4,6},{5,7... | collective-permute-start | bytes 2359304 | tf_op jit(solution)/shard_map/ppermute | solution.py:829
  155.2 38.9 %collective-permute-start.17 = (bf16[256,1536]{1,0:T(8,128)(2,1)S(1)}, bf16[256,1536]{1,0:T(8,128)(2,1)S(1)}, u32[]{:S(2)}, u32[]{:S(2)}) collective-permute-start(bf16[256,1536]{1,0:T(8,128)(2,1)S(1)} %copy-done.25), channel_id=1, source_target_pairs={{0,1},{1,65},{2,3},{3,67},{64,0},{65,64},{66,2},{67,66},{4,5},{5,6... | collective-permute-start | bytes 2359304 | tf_op jit(solution)/shard_map/ppermute | solution.py:829
  155.3 38.8 %collective-permute-start.18 = (bf16[256,1536]{1,0:T(8,128)(2,1)S(1)}, bf16[256,1536]{1,0:T(8,128)(2,1)S(1)}, u32[]{:S(2)}, u32[]{:S(2)}) collective-permute-start(bf16[256,1536]{1,0:T(8,128)(2,1)S(1)} %copy-done.24), channel_id=1, source_target_pairs={{0,3},{1,67},{2,1},{3,65},{64,2},{65,66},{66,0},{67,64},{4,7},{5,7... | collective-permute-start | bytes 2359304 | tf_op jit(solution)/shard_map/ppermute | solution.py:829
  158.3 24.0 %copy-start.8 = (s32[6]{0:T(128)S(1)}, s32[6]{0:T(128)}, u32[]{:S(2)}) copy-start(s32[6]{0:T(128)} %stack.32.meta_ref) | copy-start | bytes 76
  194.1 11.5 %copy-start.18 = (bf16[256,1536]{1,0:T(8,128)(2,1)}, bf16[256,1536]{1,0:T(8,128)(2,1)S(1)}, u32[]{:S(2)}) copy-start(bf16[256,1536]{1,0:T(8,128)(2,1)S(1)} %collective-permute-done.15.b0) | copy-start | bytes 2359300
  194.1 11.5 %copy-start.19 = (bf16[256,1536]{1,0:T(8,128)(2,1)}, bf16[256,1536]{1,0:T(8,128)(2,1)S(1)}, u32[]{:S(2)}) copy-start(bf16[256,1536]{1,0:T(8,128)(2,1)S(1)} %collective-permute-done.16.b1) | copy-start | bytes 2359300
  194.1 11.5 %copy-start.20 = (bf16[256,1536]{1,0:T(8,128)(2,1)}, bf16[256,1536]{1,0:T(8,128)(2,1)S(1)}, u32[]{:S(2)}) copy-start(bf16[256,1536]{1,0:T(8,128)(2,1)S(1)} %collective-permute-done.17.b2) | copy-start | bytes 2359300
  194.2 11.5 %copy-start.21 = (bf16[256,1536]{1,0:T(8,128)(2,1)}, bf16[256,1536]{1,0:T(8,128)(2,1)S(1)}, u32[]{:S(2)}) copy-start(bf16[256,1536]{1,0:T(8,128)(2,1)S(1)} %collective-permute-done.18.b3) | copy-start | bytes 2359300
  194.2 15.0 %collective-permute-start.19 = (bf16[256,1536]{1,0:T(8,128)(2,1)}, bf16[256,1536]{1,0:T(8,128)(2,1)S(1)}, u32[]{:S(2)}, u32[]{:S(2)}) collective-permute-start(bf16[256,1536]{1,0:T(8,128)(2,1)} %get-tuple-element.159), channel_id=1, source_target_pairs={{0,0},{1,64},{2,2},{3,66},{64,1},{65,65},{66,3},{67,67},{4,4},{5,6... | collective-permute-start | bytes 2359304 | tf_op jit(solution)/shard_map/ppermute | solution.py:829
  209.2 4.2 %copy-start.11 = (f32[768,1152]{1,0:T(8,128)S(1)}, f32[768,1152]{1,0:T(8,128)}, u32[]{:S(2)}) copy-start(f32[768,1152]{1,0:T(8,128)} %get-tuple-element.156) | copy-start | bytes 10616836
  209.2 4.0 %collective-permute-start.20 = (bf16[784,1152]{1,0:T(8,128)(2,1)}, bf16[784,1152]{1,0:T(8,128)(2,1)S(1)}, u32[]{:S(2)}, u32[]{:S(2)}) collective-permute-start(bf16[784,1152]{1,0:T(8,128)(2,1)} %get-tuple-element.160), channel_id=1, source_target_pairs={{0,1},{1,0},{2,3},{3,2},{4,5},{5,4},{6,7},{7,6},{8,9},{9,8},{10,11... | collective-permute-start | bytes 5419016 | tf_op jit(solution)/shard_map/ppermute | solution.py:839
  215.5 35.7 %all-to-all-start.2 = ((bf16[16,56,1152]{2,1,0:T(8,128)(2,1)}), bf16[16,56,1152]{2,1,0:T(8,128)(2,1)S(1)}, u32[]{:S(2)}, u32[]{:S(2)}) async-start(bf16[16,56,1152]{2,1,0:T(8,128)(2,1)} %pad_maximum_fusion), calls=%async_computation.2 | async-start | bytes 4128768 | tf_op jit(solution)/shard_map/all_to_all | solution.py:869
  222.4 33.0 %collective-permute-start.22 = (bf16[256,1536]{1,0:T(8,128)(2,1)}, bf16[256,1536]{1,0:T(8,128)(2,1)}, u32[]{:S(2)}, u32[]{:S(2)}) collective-permute-start(bf16[256,1536]{1,0:T(8,128)(2,1)} %get-tuple-element.170), channel_id=1, source_target_pairs={{0,2},{1,66},{2,0},{3,64},{64,3},{65,67},{66,1},{67,65},{4,6},{5,7... | collective-permute-start | bytes 2359304 | tf_op jit(solution)/shard_map/ppermute | solution.py:829
  223.1 33.4 %collective-permute-start.23 = (bf16[256,1536]{1,0:T(8,128)(2,1)}, bf16[256,1536]{1,0:T(8,128)(2,1)}, u32[]{:S(2)}, u32[]{:S(2)}) collective-permute-start(bf16[256,1536]{1,0:T(8,128)(2,1)} %get-tuple-element.171), channel_id=1, source_target_pairs={{0,1},{1,65},{2,3},{3,67},{64,0},{65,64},{66,2},{67,66},{4,5},{5,6... | collective-permute-start | bytes 2359304 | tf_op jit(solution)/shard_map/ppermute | solution.py:829
  223.8 32.8 %collective-permute-start.24 = (bf16[256,1536]{1,0:T(8,128)(2,1)}, bf16[256,1536]{1,0:T(8,128)(2,1)}, u32[]{:S(2)}, u32[]{:S(2)}) collective-permute-start(bf16[256,1536]{1,0:T(8,128)(2,1)} %get-tuple-element.172), channel_id=1, source_target_pairs={{0,3},{1,67},{2,1},{3,65},{64,2},{65,66},{66,0},{67,64},{4,7},{5,7... | collective-permute-start | bytes 2359304 | tf_op jit(solution)/shard_map/ppermute | solution.py:829
  227.6 23.6 %collective-permute-start.21 = (f32[2,48,768]{2,1,0:T(8,128)S(1)}, f32[2,48,768]{2,1,0:T(8,128)S(1)}, u32[]{:S(2)}, u32[]{:S(2)}) collective-permute-start(f32[2,48,768]{2,1,0:T(8,128)S(1)} %convert_reduce_fusion), channel_id=1, source_target_pairs={{0,0},{1,64},{2,2},{3,66},{64,1},{65,65},{66,3},{67,67},{4,4},{5,6... | collective-permute-start | bytes 884744 | tf_op jit(solution)/shard_map/ppermute | solution.py:829
  251.6 12.4 %collective-permute-start.28 = (f32[62,256]{1,0:T(8,128)S(1)}, f32[62,256]{1,0:T(8,128)S(1)}, u32[]{:S(2)}, u32[]{:S(2)}) collective-permute-start(f32[62,256]{1,0:T(8,128)S(1)} %get-tuple-element.178), channel_id=1, source_target_pairs={{0,3},{1,67},{2,1},{3,65},{64,2},{65,66},{66,0},{67,64},{4,7},{5,7... | collective-permute-start | bytes 190472 | tf_op jit(solution)/shard_map/ppermute | solution.py:829
  251.8 12.2 %collective-permute-start.27 = (f32[62,256]{1,0:T(8,128)S(1)}, f32[62,256]{1,0:T(8,128)S(1)}, u32[]{:S(2)}, u32[]{:S(2)}) collective-permute-start(f32[62,256]{1,0:T(8,128)S(1)} %get-tuple-element.178), channel_id=1, source_target_pairs={{0,1},{1,65},{2,3},{3,67},{64,0},{65,64},{66,2},{67,66},{4,5},{5,6... | collective-permute-start | bytes 190472 | tf_op jit(solution)/shard_map/ppermute | solution.py:829
  255.4 8.6 %collective-permute-start.26 = (f32[62,256]{1,0:T(8,128)S(1)}, f32[62,256]{1,0:T(8,128)S(1)}, u32[]{:S(2)}, u32[]{:S(2)}) collective-permute-start(f32[62,256]{1,0:T(8,128)S(1)} %get-tuple-element.178), channel_id=1, source_target_pairs={{0,2},{1,66},{2,0},{3,64},{64,3},{65,67},{66,1},{67,65},{4,6},{5,7... | collective-permute-start | bytes 190472 | tf_op jit(solution)/shard_map/ppermute | solution.py:829
  256.5 9.5 %collective-permute-start.25 = (f32[62,1152]{1,0:T(8,128)S(1)}, f32[62,1152]{1,0:T(8,128)S(1)}, u32[]{:S(2)}, u32[]{:S(2)}) collective-permute-start(f32[62,1152]{1,0:T(8,128)S(1)} %get-tuple-element.177), channel_id=1, source_target_pairs={{0,0},{1,64},{2,2},{3,66},{64,1},{65,65},{66,3},{67,67},{4,4},{5,6... | collective-permute-start | bytes 857096 | tf_op jit(solution)/shard_map/ppermute | solution.py:829

commit v5 on v4

--- a/solution.py
+++ b/solution.py
@@ -66,7 +66,8 @@
 def by_head(value, spread):
     width = spread.shape[0] // 2
     high, low = halves(value)
-    return nt(high, spread[:width]) + nt(low, spread[:width])
+    one = spread[:width]
+    return nt(jnp.concatenate([high, low], axis=1), jnp.concatenate([one, one], axis=1))
 
 
 def logistic(value):

time: 268 us -> 268 us (level)
  transfers between devices with their start and end apart: 32 -> 32, of which waited for: 12 -> 12; matrix products, arithmetic and copies ran while one was open for 2% -> 2% of each run, Pallas kernels for 33% -> 32%
where the time goes in v5:
time: 268 us; the launch traced here: 266 us
  Pallas kernels  109 us (41%)
  starting transfers between devices  73.3 us (27%)
  waiting for transfers between devices  68.8 us (26%)
  other arithmetic  7.36 us (3%)
  local copies, waits for them, and re-layouts  6.76 us (3%)
    ppermute x25, waiting for transfers between devices, permute(): return lax.ppermute(value, GROUP, moves(rule))  61.7 us
    ppermute x25, starting transfers between devices, permute(): return lax.ppermute(value, GROUP, moves(rule))  48.1 us
    pallas_call x1, Pallas kernels, mixer_backward(): pl.pallas_call(backward_kernel, grid=(steps,), in_specs=[pl.BlockSpec((SP...  23.4 us
    all_to_all x2, starting transfers between devices, exchange(): return lax.all_to_all(blocks, PLANE, 0, 0, tiled=True)  14 us
    pallas_call x1, Pallas kernels, project_back(): pl.pallas_call(project_back_kernel, grid=(2 * per,), in_specs=[pl.BlockSp...  11.8 us
    pallas_call x1, Pallas kernels, mixer_forward(): pl.pallas_call(forward_kernel, grid=(steps,), in_specs=[pl.BlockSpec((SPA...  10.9 us
    pallas_call x1, Pallas kernels, project(): pl.pallas_call(project_kernel, grid=(length // rows,), in_specs=[pl.Block...  10.7 us
    pallas_call x1, Pallas kernels, gate_back(): pl.pallas_call(functools.partial(gate_back_kernel, width_all), grid=(inne...  10 us
  transfers between devices with their start and end apart: 32, of which 12 were waited for; matrix products, arithmetic and copies ran while one was open for 2% of the time, Pallas kernels for 32%

profile of v5, /device:TPU:1, one launch (start us, length us, event | category | flops | bytes accessed | tf_op | source)
XLA Modules:
  0.0 266.1 jit_solution(3996399282102889017)
XLA Ops:
  0.7 1.1 pack_weights.1
  1.8 6.0 %collective-permute-start = (bf16[48,2688]{1,0:T(8,128)(2,1)S(1)}, bf16[48,2688]{1,0:T(8,128)(2,1)S(1)}, u32[]{:S(2)}, u32[]{:S(2)}) collective-permute-start(bf16[48,2688]{1,0:T(8,128)(2,1)S(1)} %pack_weights.1), channel_id=1, source_target_pairs={{0,0},{1,64},{2,2},{3,66},{64,1},{65,65},{66,3},{67,67},{4,4},{5,6... | collective-permute-start | bytes 774152 | tf_op jit(solution)/shard_map/ppermute | solution.py:830
  7.9 3.9 %collective-permute-done = bf16[48,2688]{1,0:T(8,128)(2,1)S(1)} collective-permute-done((bf16[48,2688]{1,0:T(8,128)(2,1)S(1)}, bf16[48,2688]{1,0:T(8,128)(2,1)S(1)}, u32[]{:S(2)}, u32[]{:S(2)}) %collective-permute-start) | collective-permute-done | bytes 258080 | tf_op jit(solution)/shard_map/ppermute | solution.py:830
  11.8 2.2 broadcast_in_dim.24
  14.1 7.9 %all-to-all-start = ((bf16[16,48,2688]{2,1,0:T(8,128)(2,1)}), bf16[16,48,2688]{2,1,0:T(8,128)(2,1)}, u32[]{:S(2)}, u32[]{:S(2)}) async-start(bf16[16,48,2688]{2,1,0:T(8,128)(2,1)} %broadcast_in_dim.24), calls=%async_computation | async-start | bytes 8257536 | tf_op jit(solution)/shard_map/all_to_all | solution.py:865
  22.1 3.3 %collective-permute-start.2 = (bf16[256,1536]{1,0:T(8,128)(2,1)S(1)}, bf16[256,1536]{1,0:T(8,128)(2,1)S(1)}, u32[]{:S(2)}, u32[]{:S(2)}) collective-permute-start(bf16[256,1536]{1,0:T(8,128)(2,1)S(1)} %copy-done.17), channel_id=1, source_target_pairs={{0,2},{1,66},{2,0},{3,64},{64,3},{65,67},{66,1},{67,65},{4,6},{5,7... | collective-permute-start | bytes 2359304 | tf_op jit(solution)/shard_map/ppermute | solution.py:830
  25.4 2.2 collective-permute-start.1
  27.9 0.6 stack.32.meta_ref
  28.5 0.7 collective-permute-start.5
  29.2 2.0 collective-permute-start.4
  31.4 0.7 broadcast_in_dim_reshape.3.skip_ref
  32.0 0.6 select_maximum_fusion.1.taps_ref
  32.7 24.6 %collective-permute-done.2.refs_1_ = bf16[256,1536]{1,0:T(8,128)(2,1)S(1)} collective-permute-done((bf16[256,1536]{1,0:T(8,128)(2,1)S(1)}, bf16[256,1536]{1,0:T(8,128)(2,1)S(1)}, u32[]{:S(2)}, u32[]{:S(2)}) %collective-permute-start.2) | collective-permute-done | bytes 786464 | tf_op jit(solution)/shard_map/ppermute | solution.py:830
  57.3 3.4 %collective-permute-start.6 = (bf16[256,1536]{1,0:T(8,128)(2,1)}, bf16[256,1536]{1,0:T(8,128)(2,1)}, u32[]{:S(2)}, u32[]{:S(2)}) collective-permute-start(bf16[256,1536]{1,0:T(8,128)(2,1)} %cot_ref.1), channel_id=1, source_target_pairs={{0,0},{1,64},{2,2},{3,66},{64,1},{65,65},{66,3},{67,67},{4,4},{5,6... | collective-permute-start | bytes 2359304 | tf_op jit(solution)/shard_map/ppermute | solution.py:830
  60.8 0.6 copy-done.6
  61.4 5.4 %place_normed.1 = (bf16[1024,1536]{1,0:T(8,128)(2,1)}, bf16[1536,1024]{1,0:T(8,128)(2,1)S(1)}) custom-call(s32[6]{0:T(128)S(1)} %copy-done.6, f32[1,1536]{1,0:T(1,128)S(1)} %broadcast_in_dim.23.gain_ref, bf16[256,1536]{1,0:T(8,128)(2,1)} %copy-done.23, bf16[256,1536]{1,0:T(8,128)(2,1)} %copy-done.22, bf16[256,1536]{1,0:T(8,128)(2,1)} %collective-permute-done.4.refs_2_, ...), custom_call_target="tpu_custom_call" | custom-call | flops 6899999744 | bytes 1024 | tf_op jit(solution)/shard_map/place_normed/pallas_call | solution.py:321
  66.8 5.6 %collective-permute-done.6.refs_0_ = bf16[256,1536]{1,0:T(8,128)(2,1)} collective-permute-done((bf16[256,1536]{1,0:T(8,128)(2,1)}, bf16[256,1536]{1,0:T(8,128)(2,1)}, u32[]{:S(2)}, u32[]{:S(2)}) %collective-permute-start.6) | collective-permute-done | bytes 786464 | tf_op jit(solution)/shard_map/ppermute | solution.py:830
  72.5 1.4 collective-permute-start.10
  73.9 2.8 %collective-permute-start.9 = (bf16[256,1536]{1,0:T(8,128)(2,1)}, bf16[256,1536]{1,0:T(8,128)(2,1)S(1)}, u32[]{:S(2)}, u32[]{:S(2)}) collective-permute-start(bf16[256,1536]{1,0:T(8,128)(2,1)} %cot_ref.1), channel_id=1, source_target_pairs={{0,64},{1,0},{2,66},{3,2},{64,65},{65,1},{66,67},{67,3},{4,68},{5,... | collective-permute-start | bytes 2359304 | tf_op jit(solution)/shard_map/ppermute | solution.py:830
  76.7 3.1 %collective-permute-done.7.xo_ref.zo_ref.oo_ref = bf16[768,2688]{1,0:T(8,128)(2,1)S(1)} collective-permute-done((bf16[768,2688]{1,0:T(8,128)(2,1)}, bf16[768,2688]{1,0:T(8,128)(2,1)S(1)}, u32[]{:S(2)}, u32[]{:S(2)}) %collective-permute-start.7) | collective-permute-done | bytes 4128800 | tf_op jit(solution)/shard_map/ppermute | solution.py:840
  79.7 10.7 %project_in.1 = (f32[1024,1152]{1,0:T(8,128)S(1)}, f32[1024,768]{1,0:T(8,128)S(1)}) custom-call(bf16[1024,1536]{1,0:T(8,128)(2,1)} %get-tuple-element.110.tokens_ref, bf16[768,2688]{1,0:T(8,128)(2,1)} %bitcast.9.xm_ref.zm_ref.om_ref, bf16[768,2688]{1,0:T(8,128)(2,1)S(1)} %collective-permute-done.7.xo_ref.zo_ref.oo_ref, ...), custom_call_target="tpu_custom_call" | custom-call | flops 6899999744 | bytes 1024 | tf_op jit(solution)/shard_map/project_in/pallas_call | solution.py:354
  90.5 10.9 %mixer_forward.1 = (f32[1024,768]{1,0:T(8,128)S(1)}, bf16[1024,768]{1,0:T(8,128)(2,1)}, f32[1024,1024]{1,0:T(8,128)}) custom-call(f32[1024,1152]{1,0:T(8,128)S(1)} %get-tuple-element.112.pre_ref, f32[8,1024]{1,0:T(8,128)S(1)} %copy-done.2, f32[8,128]{1,0:T(8,128)S(1)} %select_maximum_fusion.4.head_ref, f32[1,768]{1,0:T(1,128)S(1)} %copy-done.4, ...), custom_call_target="tpu_custom_call" | custom-call | flops 14949999616 | bytes 1024 | tf_op jit(solution)/shard_map/mixer_forward/pallas_call | solution.py:760
  101.4 1.3 collective-permute-done.8.refs_1_
  102.7 0.9 copy-done.28
  103.6 3.0 %place_cotangent.1 = (bf16[1024,1536]{1,0:T(8,128)(2,1)S(1)}, bf16[1536,1024]{1,0:T(8,128)(2,1)S(1)}) custom-call(s32[6]{0:T(128)S(1)} %copy-done.7, f32[1,1536]{1,0:T(1,128)S(1)} %broadcast_in_dim.23.gain_ref, bf16[256,1536]{1,0:T(8,128)(2,1)} %collective-permute-done.6.refs_0_, bf16[256,1536]{1,0:T(8,128)(2,1)} %copy-done.28, ...), custom_call_target="tpu_custom_call" | custom-call | flops 6899999744 | bytes 1024 | tf_op jit(solution)/shard_map/place_cotangent/pallas_call | solution.py:321
  106.6 7.4 %gate_sums.1 = (f32[1024,768]{1,0:T(8,128)S(1)}, f32[8,1024]{1,0:T(8,128)S(1)}) custom-call(bf16[1024,1536]{1,0:T(8,128)(2,1)S(1)} %get-tuple-element.124.cot_ref, bf16[768,2688]{1,0:T(8,128)(2,1)} %bitcast.9.xm_ref.zm_ref.om_ref, bf16[768,2688]{1,0:T(8,128)(2,1)} %copy-done, f32[1024,768]{1,0:T(8,128)S(1)} %get-tuple-element.125.y_ref, ...), custom_call_target="tpu_custom_call" | custom-call | flops 6899999744 | bytes 1024 | tf_op jit(solution)/shard_map/gate_sums/pallas_call | solution.py:401
  114.0 2.7 %collective-permute-start.13 = (f32[8,1024]{1,0:T(8,128)S(1)}, f32[8,1024]{1,0:T(8,128)S(1)}, u32[]{:S(2)}, u32[]{:S(2)}) collective-permute-start(f32[8,1024]{1,0:T(8,128)S(1)} %get-tuple-element.128.s0), channel_id=1, source_target_pairs={{0,66},{1,67},{2,64},{3,65},{64,2},{65,3},{66,0},{67,1},{4,70},{5,... | collective-permute-start | bytes 98312 | tf_op jit(solution)/shard_map/ppermute | solution.py:830
  116.7 0.7 collective-permute-start.11
  117.4 0.7 collective-permute-done.13.s3
  118.1 2.9 %collective-permute-done.12.s2 = f32[8,1024]{1,0:T(8,128)S(1)} collective-permute-done((f32[8,1024]{1,0:T(8,128)S(1)}, f32[8,1024]{1,0:T(8,128)S(1)}, u32[]{:S(2)}, u32[]{:S(2)}) %collective-permute-start.12) | collective-permute-done | bytes 32800 | tf_op jit(solution)/shard_map/ppermute | solution.py:830
  121.0 10.0 %gate_back.1 = (bf16[1024,768]{1,0:T(8,128)(2,1)}, bf16[1024,768]{1,0:T(8,128)(2,1)}, f32[1024,768]{1,0:T(8,128)}, f32[8,768]{1,0:T(8,128)S(1)}, bf16[16,2,48,76...) custom-call(f32[8,1024]{1,0:T(8,128)S(1)} %get-tuple-element.128.s0, f32[8,1024]{1,0:T(8,128)S(1)} %collective-permute-done.11.s1, ...), custom_call_target="tpu_custom_call" | custom-call | flops 13799999488 | bytes 1024 | tf_op jit(solution)/shard_map/gate_back/pallas_call | solution.py:457
  131.0 3.1 %collective-permute-start.14 = (bf16[16,2,48,768]{3,2,1,0:T(8,128)(2,1)}, bf16[16,2,48,768]{3,2,1,0:T(8,128)(2,1)S(1)}, u32[]{:S(2)}, u32[]{:S(2)}) collective-permute-start(bf16[16,2,48,768]{3,2,1,0:T(8,128)(2,1)} %get-tuple-element.133), channel_id=1, source_target_pairs={{0,1},{1,0},{2,3},{3,2},{4,5},{5,4},{6,7},{7,6},{8,9},{9,8},{10,11... | collective-permute-start | bytes 7077896 | tf_op jit(solution)/shard_map/ppermute | solution.py:840
  134.1 7.7 %project_out.1 = (bf16[256,1536]{1,0:T(8,128)(2,1)}, bf16[256,1536]{1,0:T(8,128)(2,1)}, bf16[256,1536]{1,0:T(8,128)(2,1)}, bf16[256,1536]{1,0:T(8,128)(2,1)}) custom-call(s32[6]{0:T(128)S(1)} %copy-done.7, bf16[1024,768]{1,0:T(8,128)(2,1)} %get-tuple-element.134.normed_ref, bf16[768,2688]{1,0:T(8,128)(2,1)} %bitcast.9.xm_ref.zm_ref.om_ref, ...), custom_call_target="tpu_custom_call" | custom-call | flops 6899999744 | bytes 1024 | tf_op jit(solution)/shard_map/project_out/pallas_call | solution.py:515
  141.8 2.2 add_convert_fusion
  144.0 7.1 %all-to-all-start.1 = ((bf16[16,2,48,768]{3,2,1,0:T(8,128)(2,1)}), bf16[16,2,48,768]{3,2,1,0:T(8,128)(2,1)}, u32[]{:S(2)}, u32[]{:S(2)}) async-start(bf16[16,2,48,768]{3,2,1,0:T(8,128)(2,1)} %add_convert_fusion), calls=%async_computation.1 | async-start | bytes 4718592 | tf_op jit(solution)/shard_map/all_to_all | solution.py:870
  151.1 3.9 %collective-permute-start.15 = (bf16[256,1536]{1,0:T(8,128)(2,1)}, bf16[256,1536]{1,0:T(8,128)(2,1)S(1)}, u32[]{:S(2)}, u32[]{:S(2)}) collective-permute-start(bf16[256,1536]{1,0:T(8,128)(2,1)} %get-tuple-element.147), channel_id=1, source_target_pairs={{0,0},{1,64},{2,2},{3,66},{64,1},{65,65},{66,3},{67,67},{4,4},{5,6... | collective-permute-start | bytes 2359304 | tf_op jit(solution)/shard_map/ppermute | solution.py:830
  154.9 0.3 collective-permute-start.16
  155.3 3.0 %collective-permute-start.18 = (bf16[256,1536]{1,0:T(8,128)(2,1)S(1)}, bf16[256,1536]{1,0:T(8,128)(2,1)S(1)}, u32[]{:S(2)}, u32[]{:S(2)}) collective-permute-start(bf16[256,1536]{1,0:T(8,128)(2,1)S(1)} %copy-done.24), channel_id=1, source_target_pairs={{0,3},{1,67},{2,1},{3,65},{64,2},{65,66},{66,0},{67,64},{4,7},{5,7... | collective-permute-start | bytes 2359304 | tf_op jit(solution)/shard_map/ppermute | solution.py:830
  158.3 23.4 %mixer_backward.1 = (bf16[1024,1152]{1,0:T(8,128)(2,1)S(1)}, f32[8,1024]{1,0:T(8,128)S(1)}, f32[8,128]{1,0:T(8,128)S(1)}) custom-call(f32[1024,1152]{1,0:T(8,128)} %copy-done.10, f32[1024,1024]{1,0:T(8,128)} %get-tuple-element.117.conv_ref, f32[1024,768]{1,0:T(8,128)} %get-tuple-element.139.dy_ref, bf16[1024,768]{1,0:T(8,128)(2,1)} %get-tuple-element.140.kept_ref, ...), custom_call_target="tpu_custom_call" | custom-call | flops 34500001792 | bytes 1024 | tf_op jit(solution)/shard_map/mixer_backward/pallas_call | solution.py:790
  181.7 11.8 %project_back.1 = (bf16[256,1536]{1,0:T(8,128)(2,1)}, bf16[256,1536]{1,0:T(8,128)(2,1)}, bf16[256,1536]{1,0:T(8,128)(2,1)}, bf16[256,1536]{1,0:T(8,128)(2,1)}, f32[8,1536]{1,0:T(8,128)S(1)}) custom-call(s32[6]{0:T(128)S(1)} %copy-done.8, bf16[1024,1152]{1,0:T(8,128)(2,1)S(1)} %get-tuple-element.151.late_ref, bf16[1024,768]{1,0:T(8,128)(2,1)} %get-tuple-element.142.gate_ref, ...), custom_call_target="tpu_custom_call" | custom-call | flops 575000000 | bytes 1024 | tf_op jit(solution)/shard_map/project_back/pallas_call | solution.py:558
  193.5 2.3 collective-permute-start.19
  195.8 0.7 slice.60
  196.6 8.4 %weight_grad.1 = (f32[768,1152]{1,0:T(8,128)}, bf16[784,1152]{1,0:T(8,128)(2,1)}) custom-call(bf16[1536,1024]{1,0:T(8,128)(2,1)} %copy-done.1, bf16[1024,1152]{1,0:T(8,128)(2,1)S(1)} %get-tuple-element.151.late_ref, f32[16,1152]{1,0:T(8,128)S(1)} %pad.29.vector_ref), custom_call_target="tpu_custom_call" | custom-call | flops 575000000 | bytes 1024 | tf_op jit(solution)/shard_map/weight_grad/pallas_call | solution.py:589
  205.0 3.6 %collective-permute-done.19.b0 = bf16[256,1536]{1,0:T(8,128)(2,1)S(1)} collective-permute-done((bf16[256,1536]{1,0:T(8,128)(2,1)}, bf16[256,1536]{1,0:T(8,128)(2,1)S(1)}, u32[]{:S(2)}, u32[]{:S(2)}) %collective-permute-start.19) | collective-permute-done | bytes 786464 | tf_op jit(solution)/shard_map/ppermute | solution.py:830
  208.6 4.0 %collective-permute-done.20 = bf16[784,1152]{1,0:T(8,128)(2,1)S(1)} collective-permute-done((bf16[784,1152]{1,0:T(8,128)(2,1)}, bf16[784,1152]{1,0:T(8,128)(2,1)S(1)}, u32[]{:S(2)}, u32[]{:S(2)}) %collective-permute-start.20) | collective-permute-done | bytes 1806368 | tf_op jit(solution)/shard_map/ppermute | solution.py:840
  212.5 0.2 convert_element_type.40
  212.8 0.6 fusion
  213.4 1.5 pad_maximum_fusion
  214.9 6.9 %all-to-all-start.2 = ((bf16[16,56,1152]{2,1,0:T(8,128)(2,1)}), bf16[16,56,1152]{2,1,0:T(8,128)(2,1)S(1)}, u32[]{:S(2)}, u32[]{:S(2)}) async-start(bf16[16,56,1152]{2,1,0:T(8,128)(2,1)} %pad_maximum_fusion), calls=%async_computation.2 | async-start | bytes 4128768 | tf_op jit(solution)/shard_map/all_to_all | solution.py:870
  221.8 0.7 collective-permute-start.22
  222.5 0.6 collective-permute-start.23
  223.1 1.8 collective-permute-start.24
  224.9 2.0 convert_reduce_fusion
  226.9 3.0 %collective-permute-start.21 = (f32[2,48,768]{2,1,0:T(8,128)S(1)}, f32[2,48,768]{2,1,0:T(8,128)S(1)}, u32[]{:S(2)}, u32[]{:S(2)}) collective-permute-start(f32[2,48,768]{2,1,0:T(8,128)S(1)} %convert_reduce_fusion), channel_id=1, source_target_pairs={{0,0},{1,64},{2,2},{3,66},{64,1},{65,65},{66,3},{67,67},{4,4},{5,6... | collective-permute-start | bytes 884744 | tf_op jit(solution)/shard_map/ppermute | solution.py:830
  229.9 3.5 %finish_output.1 = bf16[256,1536]{1,0:T(8,128)(2,1)} custom-call(s32[6]{0:T(128)S(1)} %copy-done.8, bf16[256,1536]{1,0:T(8,128)(2,1)} %copy-done.18, bf16[256,1536]{1,0:T(8,128)(2,1)} %copy-done.19, bf16[256,1536]{1,0:T(8,128)(2,1)} %copy-done.20, bf16[256,1536]{1,0:T(8,128)(2,1)} %copy-done.21, bf16[256,1536]{1,0:T(8,128)(2,1)} %hidden_ref.3), custom_call_target="tpu_custom_call" | custom-call | flops 3449999872 | bytes 1024 | tf_op jit(solution)/shard_map/finish_output/pallas_call | solution.py:711
  233.4 17.1 %collective-permute-done.21 = f32[2,48,768]{2,1,0:T(8,128)S(1)} collective-permute-done((f32[2,48,768]{2,1,0:T(8,128)S(1)}, f32[2,48,768]{2,1,0:T(8,128)S(1)}, u32[]{:S(2)}, u32[]{:S(2)}) %collective-permute-start.21) | collective-permute-done | bytes 294944 | tf_op jit(solution)/shard_map/ppermute | solution.py:830
  250.6 0.4 late_total.1
  251.2 3.6 %collective-permute-start.27 = (f32[62,256]{1,0:T(8,128)S(1)}, f32[62,256]{1,0:T(8,128)S(1)}, u32[]{:S(2)}, u32[]{:S(2)}) collective-permute-start(f32[62,256]{1,0:T(8,128)S(1)} %get-tuple-element.178), channel_id=1, source_target_pairs={{0,1},{1,65},{2,3},{3,67},{64,0},{65,64},{66,2},{67,66},{4,5},{5,6... | collective-permute-start | bytes 190472 | tf_op jit(solution)/shard_map/ppermute | solution.py:830
  254.8 1.1 collective-permute-start.26
  255.9 2.3 collective-permute-start.25
  258.2 4.4 %finish_input.1 = f32[256,1536]{1,0:T(8,128)} custom-call(s32[6]{0:T(128)S(1)} %copy-done.8, bf16[256,1536]{1,0:T(8,128)(2,1)S(1)} %collective-permute-done.19.b0, bf16[256,1536]{1,0:T(8,128)(2,1)} %collective-permute-done.22.b1, bf16[256,1536]{1,0:T(8,128)(2,1)} %collective-permute-done.23.b2, bf16[256,1536]{1,0:T(8,128)(2,1)} %collective-permute-done.24.b3, ...), custom_call_target="tpu_custom_call" | custom-call | flops 3449999872 | bytes 1024 | tf_op jit(solution)/shard_map/finish_input/pallas_call | solution.py:732
  262.6 0.7 slice_bitcast_fusion
  263.4 2.1 collective-permute-done.25.joint_ref
  265.4 0.7 deliver_late.1
  (106 shorter events, 1.2 us)
Async XLA Ops:
  0.6 7.2 %copy-start.16 = (f32[3,12]{1,0:T(4,128)S(1)}, f32[3,12]{1,0:T(4,128)}, u32[]{:S(2)}) copy-start(f32[3,12]{1,0:T(4,128)} %param.21) | copy-start | bytes 436
  0.7 7.2 %copy-start.15 = (f32[768]{0:T(1024)S(1)}, f32[768]{0:T(1024)}, u32[]{:S(2)}) copy-start(f32[768]{0:T(1024)} %param.22) | copy-start | bytes 9220
  0.7 7.2 %copy-start.12 = (f32[5,768]{1,0:T(8,128)S(1)}, f32[5,768]{1,0:T(8,128)}, u32[]{:S(2)}) copy-start(f32[5,768]{1,0:T(8,128)} %param.19) | copy-start | bytes 46084
  1.8 10.0 %collective-permute-start = (bf16[48,2688]{1,0:T(8,128)(2,1)S(1)}, bf16[48,2688]{1,0:T(8,128)(2,1)S(1)}, u32[]{:S(2)}, u32[]{:S(2)}) collective-permute-start(bf16[48,2688]{1,0:T(8,128)(2,1)S(1)} %pack_weights.1), channel_id=1, source_target_pairs={{0,0},{1,64},{2,2},{3,66},{64,1},{65,65},{66,3},{67,67},{4,4},{5,6... | collective-permute-start | bytes 774152 | tf_op jit(solution)/shard_map/ppermute | solution.py:830
  14.1 8.0 %copy-start.17 = (bf16[256,1536]{1,0:T(8,128)(2,1)S(1)}, bf16[256,1536]{1,0:T(8,128)(2,1)}, u32[]{:S(2)}) copy-start(bf16[256,1536]{1,0:T(8,128)(2,1)} %hidden_ref.3) | copy-start | bytes 2359300
  14.1 13.8 %copy-start.13 = (f32[1536]{0:T(1024)S(1)}, f32[1536]{0:T(1024)}, u32[]{:S(2)}) copy-start(f32[1536]{0:T(1024)} %param.14) | copy-start | bytes 18436
  14.1 18.0 %copy-start.14 = (f32[5,256]{1,0:T(8,128)S(1)}, f32[5,256]{1,0:T(8,128)}, u32[]{:S(2)}) copy-start(f32[5,256]{1,0:T(8,128)} %param.20) | copy-start | bytes 15364
  14.1 58.3 %all-to-all-start = ((bf16[16,48,2688]{2,1,0:T(8,128)(2,1)}), bf16[16,48,2688]{2,1,0:T(8,128)(2,1)}, u32[]{:S(2)}, u32[]{:S(2)}) async-start(bf16[16,48,2688]{2,1,0:T(8,128)(2,1)} %broadcast_in_dim.24), calls=%async_computation | async-start | bytes 8257536 | tf_op jit(solution)/shard_map/all_to_all | solution.py:865
  22.1 35.2 %collective-permute-start.2 = (bf16[256,1536]{1,0:T(8,128)(2,1)S(1)}, bf16[256,1536]{1,0:T(8,128)(2,1)S(1)}, u32[]{:S(2)}, u32[]{:S(2)}) collective-permute-start(bf16[256,1536]{1,0:T(8,128)(2,1)S(1)} %copy-done.17), channel_id=1, source_target_pairs={{0,2},{1,66},{2,0},{3,64},{64,3},{65,67},{66,1},{67,65},{4,6},{5,7... | collective-permute-start | bytes 2359304 | tf_op jit(solution)/shard_map/ppermute | solution.py:830
  25.4 31.8 %collective-permute-start.1 = (bf16[256,1536]{1,0:T(8,128)(2,1)S(1)}, bf16[256,1536]{1,0:T(8,128)(2,1)S(1)}, u32[]{:S(2)}, u32[]{:S(2)}) collective-permute-start(bf16[256,1536]{1,0:T(8,128)(2,1)S(1)} %copy-done.17), channel_id=1, source_target_pairs={{0,0},{1,64},{2,2},{3,66},{64,1},{65,65},{66,3},{67,67},{4,4},{5,6... | collective-permute-start | bytes 2359304 | tf_op jit(solution)/shard_map/ppermute | solution.py:830
  27.6 3.6 %collective-permute-start.3 = (f32[16,768]{1,0:T(8,128)S(1)}, f32[16,768]{1,0:T(8,128)S(1)}, u32[]{:S(2)}, u32[]{:S(2)}) collective-permute-start(f32[16,768]{1,0:T(8,128)S(1)} %select_maximum_fusion), channel_id=1, source_target_pairs={{0,1},{1,0},{2,3},{3,2},{4,5},{5,4},{6,7},{7,6},{8,9},{9,8},{10,11... | collective-permute-start | bytes 147464 | tf_op jit(solution)/shard_map/ppermute | solution.py:840
  28.5 32.2 %collective-permute-start.5 = (bf16[256,1536]{1,0:T(8,128)(2,1)S(1)}, bf16[256,1536]{1,0:T(8,128)(2,1)}, u32[]{:S(2)}, u32[]{:S(2)}) collective-permute-start(bf16[256,1536]{1,0:T(8,128)(2,1)S(1)} %copy-done.17), channel_id=1, source_target_pairs={{0,66},{1,2},{2,64},{3,0},{64,67},{65,3},{66,65},{67,1},{4,70},{5,... | collective-permute-start | bytes 2359304 | tf_op jit(solution)/shard_map/ppermute | solution.py:830
  29.2 31.5 %collective-permute-start.4 = (bf16[256,1536]{1,0:T(8,128)(2,1)S(1)}, bf16[256,1536]{1,0:T(8,128)(2,1)}, u32[]{:S(2)}, u32[]{:S(2)}) collective-permute-start(bf16[256,1536]{1,0:T(8,128)(2,1)S(1)} %copy-done.17), channel_id=1, source_target_pairs={{0,64},{1,0},{2,66},{3,2},{64,65},{65,1},{66,67},{67,3},{4,68},{5,... | collective-permute-start | bytes 2359304 | tf_op jit(solution)/shard_map/ppermute | solution.py:830
  57.2 3.5 %copy-start.22 = (bf16[256,1536]{1,0:T(8,128)(2,1)}, bf16[256,1536]{1,0:T(8,128)(2,1)S(1)}, u32[]{:S(2)}) copy-start(bf16[256,1536]{1,0:T(8,128)(2,1)S(1)} %collective-permute-done.2.refs_1_) | copy-start | bytes 2359300
  57.3 3.5 %copy-start.23 = (bf16[256,1536]{1,0:T(8,128)(2,1)}, bf16[256,1536]{1,0:T(8,128)(2,1)S(1)}, u32[]{:S(2)}) copy-start(bf16[256,1536]{1,0:T(8,128)(2,1)S(1)} %collective-permute-done.1.refs_0_) | copy-start | bytes 2359300
  57.3 15.1 %collective-permute-start.6 = (bf16[256,1536]{1,0:T(8,128)(2,1)}, bf16[256,1536]{1,0:T(8,128)(2,1)}, u32[]{:S(2)}, u32[]{:S(2)}) collective-permute-start(bf16[256,1536]{1,0:T(8,128)(2,1)} %cot_ref.1), channel_id=1, source_target_pairs={{0,0},{1,64},{2,2},{3,66},{64,1},{65,65},{66,3},{67,67},{4,4},{5,6... | collective-permute-start | bytes 2359304 | tf_op jit(solution)/shard_map/ppermute | solution.py:830
  60.7 0.7 copy-start.6
  66.8 54.1 %copy-start.1 = (bf16[1536,1024]{1,0:T(8,128)(2,1)}, bf16[1536,1024]{1,0:T(8,128)(2,1)S(1)}, u32[]{:S(2)}) copy-start(bf16[1536,1024]{1,0:T(8,128)(2,1)S(1)} %get-tuple-element.107.tokens_t_ref) | copy-start | bytes 9437188
  72.4 18.0 %copy-start.2 = (f32[8,1024]{1,0:T(8,128)S(1)}, f32[8,1024]{1,0:T(8,128)}, u32[]{:S(2)}) copy-start(f32[8,1024]{1,0:T(8,128)} %select_maximum_fusion.1.taps_ref) | copy-start | bytes 98308
  72.4 18.0 %copy-start.4 = (f32[1,768]{1,0:T(1,128)S(1)}, f32[1,768]{1,0:T(1,128)}, u32[]{:S(2)}) copy-start(f32[1,768]{1,0:T(1,128)} %broadcast_in_dim_reshape.3.skip_ref) | copy-start | bytes 9220
  72.4 7.4 %collective-permute-start.7 = (bf16[768,2688]{1,0:T(8,128)(2,1)}, bf16[768,2688]{1,0:T(8,128)(2,1)S(1)}, u32[]{:S(2)}, u32[]{:S(2)}) collective-permute-start(bf16[768,2688]{1,0:T(8,128)(2,1)} %bitcast.9.xm_ref.zm_ref.om_ref), channel_id=1, source_target_pairs={{0,1},{1,0},{2,3},{3,2},{4,5},{5,4},{6,7},{7,6},{8,9},{9,8},{10,11... | collective-permute-start | bytes 12386312 | tf_op jit(solution)/shard_map/ppermute | solution.py:840
  72.5 28.9 %collective-permute-start.10 = (bf16[256,1536]{1,0:T(8,128)(2,1)}, bf16[256,1536]{1,0:T(8,128)(2,1)S(1)}, u32[]{:S(2)}, u32[]{:S(2)}) collective-permute-start(bf16[256,1536]{1,0:T(8,128)(2,1)} %cot_ref.1), channel_id=1, source_target_pairs={{0,66},{1,2},{2,64},{3,0},{64,67},{65,3},{66,65},{67,1},{4,70},{5,... | collective-permute-start | bytes 2359304 | tf_op jit(solution)/shard_map/ppermute | solution.py:830
  73.9 27.5 %collective-permute-start.9 = (bf16[256,1536]{1,0:T(8,128)(2,1)}, bf16[256,1536]{1,0:T(8,128)(2,1)S(1)}, u32[]{:S(2)}, u32[]{:S(2)}) collective-permute-start(bf16[256,1536]{1,0:T(8,128)(2,1)} %cot_ref.1), channel_id=1, source_target_pairs={{0,64},{1,0},{2,66},{3,2},{64,65},{65,1},{66,67},{67,3},{4,68},{5,... | collective-permute-start | bytes 2359304 | tf_op jit(solution)/shard_map/ppermute | solution.py:830
  76.6 26.1 %collective-permute-start.8 = (bf16[256,1536]{1,0:T(8,128)(2,1)}, bf16[256,1536]{1,0:T(8,128)(2,1)S(1)}, u32[]{:S(2)}, u32[]{:S(2)}) collective-permute-start(bf16[256,1536]{1,0:T(8,128)(2,1)} %cot_ref.1), channel_id=1, source_target_pairs={{0,2},{1,66},{2,0},{3,64},{64,3},{65,67},{66,1},{67,65},{4,6},{5,7... | collective-permute-start | bytes 2359304 | tf_op jit(solution)/shard_map/ppermute | solution.py:830
  79.7 10.7 %copy-start = (bf16[768,2688]{1,0:T(8,128)(2,1)}, bf16[768,2688]{1,0:T(8,128)(2,1)S(1)}, u32[]{:S(2)}) copy-start(bf16[768,2688]{1,0:T(8,128)(2,1)S(1)} %collective-permute-done.7.xo_ref.zo_ref.oo_ref) | copy-start | bytes 12386308
  90.4 10.9 %copy-start.10 = (f32[1024,1152]{1,0:T(8,128)}, f32[1024,1152]{1,0:T(8,128)S(1)}, u32[]{:S(2)}) copy-start(f32[1024,1152]{1,0:T(8,128)S(1)} %get-tuple-element.112.pre_ref) | copy-start | bytes 14155780
  90.4 13.2 %copy-start.7 = (s32[6]{0:T(128)S(1)}, s32[6]{0:T(128)}, u32[]{:S(2)}) copy-start(s32[6]{0:T(128)} %stack.32.meta_ref) | copy-start | bytes 76
  101.4 1.4 copy-start.26
  101.4 1.4 copy-start.27
  102.7 0.9 copy-start.28
  114.0 4.1 %collective-permute-start.13 = (f32[8,1024]{1,0:T(8,128)S(1)}, f32[8,1024]{1,0:T(8,128)S(1)}, u32[]{:S(2)}, u32[]{:S(2)}) collective-permute-start(f32[8,1024]{1,0:T(8,128)S(1)} %get-tuple-element.128.s0), channel_id=1, source_target_pairs={{0,66},{1,67},{2,64},{3,65},{64,2},{65,3},{66,0},{67,1},{4,70},{5,... | collective-permute-start | bytes 98312 | tf_op jit(solution)/shard_map/ppermute | solution.py:830
  116.7 4.3 %collective-permute-start.12 = (f32[8,1024]{1,0:T(8,128)S(1)}, f32[8,1024]{1,0:T(8,128)S(1)}, u32[]{:S(2)}, u32[]{:S(2)}) collective-permute-start(f32[8,1024]{1,0:T(8,128)S(1)} %get-tuple-element.128.s0), channel_id=1, source_target_pairs={{0,64},{1,65},{2,66},{3,67},{64,0},{65,1},{66,2},{67,3},{4,68},{5,... | collective-permute-start | bytes 98312 | tf_op jit(solution)/shard_map/ppermute | solution.py:830
  116.7 4.3 %collective-permute-start.11 = (f32[8,1024]{1,0:T(8,128)S(1)}, f32[8,1024]{1,0:T(8,128)S(1)}, u32[]{:S(2)}, u32[]{:S(2)}) collective-permute-start(f32[8,1024]{1,0:T(8,128)S(1)} %get-tuple-element.128.s0), channel_id=1, source_target_pairs={{0,2},{1,3},{2,0},{3,1},{64,66},{65,67},{66,64},{67,65},{4,6},{5,7... | collective-permute-start | bytes 98312 | tf_op jit(solution)/shard_map/ppermute | solution.py:830
  131.0 10.8 %copy-start.9 = (f32[8,768]{1,0:T(8,128)}, f32[8,768]{1,0:T(8,128)S(1)}, u32[]{:S(2)}) copy-start(f32[8,768]{1,0:T(8,128)S(1)} %get-tuple-element.154) | copy-start | bytes 73732
  131.0 10.8 %collective-permute-start.14 = (bf16[16,2,48,768]{3,2,1,0:T(8,128)(2,1)}, bf16[16,2,48,768]{3,2,1,0:T(8,128)(2,1)S(1)}, u32[]{:S(2)}, u32[]{:S(2)}) collective-permute-start(bf16[16,2,48,768]{3,2,1,0:T(8,128)(2,1)} %get-tuple-element.133), channel_id=1, source_target_pairs={{0,1},{1,0},{2,3},{3,2},{4,5},{5,4},{6,7},{7,6},{8,9},{9,8},{10,11... | collective-permute-start | bytes 7077896 | tf_op jit(solution)/shard_map/ppermute | solution.py:840
  144.0 11.3 %copy-start.25 = (bf16[256,1536]{1,0:T(8,128)(2,1)S(1)}, bf16[256,1536]{1,0:T(8,128)(2,1)}, u32[]{:S(2)}) copy-start(bf16[256,1536]{1,0:T(8,128)(2,1)} %get-tuple-element.149) | copy-start | bytes 2359300
  144.0 11.4 %copy-start.24 = (bf16[256,1536]{1,0:T(8,128)(2,1)S(1)}, bf16[256,1536]{1,0:T(8,128)(2,1)}, u32[]{:S(2)}) copy-start(bf16[256,1536]{1,0:T(8,128)(2,1)} %get-tuple-element.150) | copy-start | bytes 2359300
  144.0 14.3 %copy-start.3 = (f32[8,1024]{1,0:T(8,128)S(1)}, f32[8,1024]{1,0:T(8,128)}, u32[]{:S(2)}) copy-start(f32[8,1024]{1,0:T(8,128)} %select_maximum_fusion.1.taps_ref) | copy-start | bytes 98308
  144.0 14.3 %copy-start.5 = (f32[1,768]{1,0:T(1,128)S(1)}, f32[1,768]{1,0:T(1,128)}, u32[]{:S(2)}) copy-start(f32[1,768]{1,0:T(1,128)} %broadcast_in_dim_reshape.3.skip_ref) | copy-start | bytes 9220
  144.0 64.6 %all-to-all-start.1 = ((bf16[16,2,48,768]{3,2,1,0:T(8,128)(2,1)}), bf16[16,2,48,768]{3,2,1,0:T(8,128)(2,1)}, u32[]{:S(2)}, u32[]{:S(2)}) async-start(bf16[16,2,48,768]{3,2,1,0:T(8,128)(2,1)} %add_convert_fusion), calls=%async_computation.1 | async-start | bytes 4718592 | tf_op jit(solution)/shard_map/all_to_all | solution.py:870
  151.1 42.4 %collective-permute-start.15 = (bf16[256,1536]{1,0:T(8,128)(2,1)}, bf16[256,1536]{1,0:T(8,128)(2,1)S(1)}, u32[]{:S(2)}, u32[]{:S(2)}) collective-permute-start(bf16[256,1536]{1,0:T(8,128)(2,1)} %get-tuple-element.147), channel_id=1, source_target_pairs={{0,0},{1,64},{2,2},{3,66},{64,1},{65,65},{66,3},{67,67},{4,4},{5,6... | collective-permute-start | bytes 2359304 | tf_op jit(solution)/shard_map/ppermute | solution.py:830
  154.9 38.6 %collective-permute-start.16 = (bf16[256,1536]{1,0:T(8,128)(2,1)}, bf16[256,1536]{1,0:T(8,128)(2,1)S(1)}, u32[]{:S(2)}, u32[]{:S(2)}) collective-permute-start(bf16[256,1536]{1,0:T(8,128)(2,1)} %get-tuple-element.148), channel_id=1, source_target_pairs={{0,2},{1,66},{2,0},{3,64},{64,3},{65,67},{66,1},{67,65},{4,6},{5,7... | collective-permute-start | bytes 2359304 | tf_op jit(solution)/shard_map/ppermute | solution.py:830
  155.2 38.3 %collective-permute-start.17 = (bf16[256,1536]{1,0:T(8,128)(2,1)S(1)}, bf16[256,1536]{1,0:T(8,128)(2,1)S(1)}, u32[]{:S(2)}, u32[]{:S(2)}) collective-permute-start(bf16[256,1536]{1,0:T(8,128)(2,1)S(1)} %copy-done.25), channel_id=1, source_target_pairs={{0,1},{1,65},{2,3},{3,67},{64,0},{65,64},{66,2},{67,66},{4,5},{5,6... | collective-permute-start | bytes 2359304 | tf_op jit(solution)/shard_map/ppermute | solution.py:830
  155.3 38.2 %collective-permute-start.18 = (bf16[256,1536]{1,0:T(8,128)(2,1)S(1)}, bf16[256,1536]{1,0:T(8,128)(2,1)S(1)}, u32[]{:S(2)}, u32[]{:S(2)}) collective-permute-start(bf16[256,1536]{1,0:T(8,128)(2,1)S(1)} %copy-done.24), channel_id=1, source_target_pairs={{0,3},{1,67},{2,1},{3,65},{64,2},{65,66},{66,0},{67,64},{4,7},{5,7... | collective-permute-start | bytes 2359304 | tf_op jit(solution)/shard_map/ppermute | solution.py:830
  158.3 23.4 %copy-start.8 = (s32[6]{0:T(128)S(1)}, s32[6]{0:T(128)}, u32[]{:S(2)}) copy-start(s32[6]{0:T(128)} %stack.32.meta_ref) | copy-start | bytes 76
  193.5 11.5 %copy-start.18 = (bf16[256,1536]{1,0:T(8,128)(2,1)}, bf16[256,1536]{1,0:T(8,128)(2,1)S(1)}, u32[]{:S(2)}) copy-start(bf16[256,1536]{1,0:T(8,128)(2,1)S(1)} %collective-permute-done.15.b0) | copy-start | bytes 2359300
  193.5 11.5 %copy-start.19 = (bf16[256,1536]{1,0:T(8,128)(2,1)}, bf16[256,1536]{1,0:T(8,128)(2,1)S(1)}, u32[]{:S(2)}) copy-start(bf16[256,1536]{1,0:T(8,128)(2,1)S(1)} %collective-permute-done.16.b1) | copy-start | bytes 2359300
  193.5 11.5 %copy-start.20 = (bf16[256,1536]{1,0:T(8,128)(2,1)}, bf16[256,1536]{1,0:T(8,128)(2,1)S(1)}, u32[]{:S(2)}) copy-start(bf16[256,1536]{1,0:T(8,128)(2,1)S(1)} %collective-permute-done.17.b2) | copy-start | bytes 2359300
  193.5 11.5 %copy-start.21 = (bf16[256,1536]{1,0:T(8,128)(2,1)}, bf16[256,1536]{1,0:T(8,128)(2,1)S(1)}, u32[]{:S(2)}) copy-start(bf16[256,1536]{1,0:T(8,128)(2,1)S(1)} %collective-permute-done.18.b3) | copy-start | bytes 2359300
  193.5 15.0 %collective-permute-start.19 = (bf16[256,1536]{1,0:T(8,128)(2,1)}, bf16[256,1536]{1,0:T(8,128)(2,1)S(1)}, u32[]{:S(2)}, u32[]{:S(2)}) collective-permute-start(bf16[256,1536]{1,0:T(8,128)(2,1)} %get-tuple-element.159), channel_id=1, source_target_pairs={{0,0},{1,64},{2,2},{3,66},{64,1},{65,65},{66,3},{67,67},{4,4},{5,6... | collective-permute-start | bytes 2359304 | tf_op jit(solution)/shard_map/ppermute | solution.py:830
  208.6 4.2 %copy-start.11 = (f32[768,1152]{1,0:T(8,128)S(1)}, f32[768,1152]{1,0:T(8,128)}, u32[]{:S(2)}) copy-start(f32[768,1152]{1,0:T(8,128)} %get-tuple-element.156) | copy-start | bytes 10616836
  208.6 4.0 %collective-permute-start.20 = (bf16[784,1152]{1,0:T(8,128)(2,1)}, bf16[784,1152]{1,0:T(8,128)(2,1)S(1)}, u32[]{:S(2)}, u32[]{:S(2)}) collective-permute-start(bf16[784,1152]{1,0:T(8,128)(2,1)} %get-tuple-element.160), channel_id=1, source_target_pairs={{0,1},{1,0},{2,3},{3,2},{4,5},{5,4},{6,7},{7,6},{8,9},{9,8},{10,11... | collective-permute-start | bytes 5419016 | tf_op jit(solution)/shard_map/ppermute | solution.py:840
  214.9 35.7 %all-to-all-start.2 = ((bf16[16,56,1152]{2,1,0:T(8,128)(2,1)}), bf16[16,56,1152]{2,1,0:T(8,128)(2,1)S(1)}, u32[]{:S(2)}, u32[]{:S(2)}) async-start(bf16[16,56,1152]{2,1,0:T(8,128)(2,1)} %pad_maximum_fusion), calls=%async_computation.2 | async-start | bytes 4128768 | tf_op jit(solution)/shard_map/all_to_all | solution.py:870
  221.8 33.0 %collective-permute-start.22 = (bf16[256,1536]{1,0:T(8,128)(2,1)}, bf16[256,1536]{1,0:T(8,128)(2,1)}, u32[]{:S(2)}, u32[]{:S(2)}) collective-permute-start(bf16[256,1536]{1,0:T(8,128)(2,1)} %get-tuple-element.170), channel_id=1, source_target_pairs={{0,2},{1,66},{2,0},{3,64},{64,3},{65,67},{66,1},{67,65},{4,6},{5,7... | collective-permute-start | bytes 2359304 | tf_op jit(solution)/shard_map/ppermute | solution.py:830
  222.5 33.4 %collective-permute-start.23 = (bf16[256,1536]{1,0:T(8,128)(2,1)}, bf16[256,1536]{1,0:T(8,128)(2,1)}, u32[]{:S(2)}, u32[]{:S(2)}) collective-permute-start(bf16[256,1536]{1,0:T(8,128)(2,1)} %get-tuple-element.171), channel_id=1, source_target_pairs={{0,1},{1,65},{2,3},{3,67},{64,0},{65,64},{66,2},{67,66},{4,5},{5,6... | collective-permute-start | bytes 2359304 | tf_op jit(solution)/shard_map/ppermute | solution.py:830
  223.1 32.8 %collective-permute-start.24 = (bf16[256,1536]{1,0:T(8,128)(2,1)}, bf16[256,1536]{1,0:T(8,128)(2,1)}, u32[]{:S(2)}, u32[]{:S(2)}) collective-permute-start(bf16[256,1536]{1,0:T(8,128)(2,1)} %get-tuple-element.172), channel_id=1, source_target_pairs={{0,3},{1,67},{2,1},{3,65},{64,2},{65,66},{66,0},{67,64},{4,7},{5,7... | collective-permute-start | bytes 2359304 | tf_op jit(solution)/shard_map/ppermute | solution.py:830
  226.9 23.6 %collective-permute-start.21 = (f32[2,48,768]{2,1,0:T(8,128)S(1)}, f32[2,48,768]{2,1,0:T(8,128)S(1)}, u32[]{:S(2)}, u32[]{:S(2)}) collective-permute-start(f32[2,48,768]{2,1,0:T(8,128)S(1)} %convert_reduce_fusion), channel_id=1, source_target_pairs={{0,0},{1,64},{2,2},{3,66},{64,1},{65,65},{66,3},{67,67},{4,4},{5,6... | collective-permute-start | bytes 884744 | tf_op jit(solution)/shard_map/ppermute | solution.py:830
  250.9 12.4 %collective-permute-start.28 = (f32[62,256]{1,0:T(8,128)S(1)}, f32[62,256]{1,0:T(8,128)S(1)}, u32[]{:S(2)}, u32[]{:S(2)}) collective-permute-start(f32[62,256]{1,0:T(8,128)S(1)} %get-tuple-element.178), channel_id=1, source_target_pairs={{0,3},{1,67},{2,1},{3,65},{64,2},{65,66},{66,0},{67,64},{4,7},{5,7... | collective-permute-start | bytes 190472 | tf_op jit(solution)/shard_map/ppermute | solution.py:830
  251.2 12.2 %collective-permute-start.27 = (f32[62,256]{1,0:T(8,128)S(1)}, f32[62,256]{1,0:T(8,128)S(1)}, u32[]{:S(2)}, u32[]{:S(2)}) collective-permute-start(f32[62,256]{1,0:T(8,128)S(1)} %get-tuple-element.178), channel_id=1, source_target_pairs={{0,1},{1,65},{2,3},{3,67},{64,0},{65,64},{66,2},{67,66},{4,5},{5,6... | collective-permute-start | bytes 190472 | tf_op jit(solution)/shard_map/ppermute | solution.py:830
  254.8 8.6 %collective-permute-start.26 = (f32[62,256]{1,0:T(8,128)S(1)}, f32[62,256]{1,0:T(8,128)S(1)}, u32[]{:S(2)}, u32[]{:S(2)}) collective-permute-start(f32[62,256]{1,0:T(8,128)S(1)} %get-tuple-element.178), channel_id=1, source_target_pairs={{0,2},{1,66},{2,0},{3,64},{64,3},{65,67},{66,1},{67,65},{4,6},{5,7... | collective-permute-start | bytes 190472 | tf_op jit(solution)/shard_map/ppermute | solution.py:830
  255.9 9.5 %collective-permute-start.25 = (f32[62,1152]{1,0:T(8,128)S(1)}, f32[62,1152]{1,0:T(8,128)S(1)}, u32[]{:S(2)}, u32[]{:S(2)}) collective-permute-start(f32[62,1152]{1,0:T(8,128)S(1)} %get-tuple-element.177), channel_id=1, source_target_pairs={{0,0},{1,64},{2,2},{3,66},{64,1},{65,65},{66,3},{67,67},{4,4},{5,6... | collective-permute-start | bytes 857096 | tf_op jit(solution)/shard_map/ppermute | solution.py:830
